TPU v7x, 32 devices: a whole 2x2x4 slice. The times are simulated.
32 devices in a mesh: group: 4 (over x, core), sub: 8 (over z, y).
Axes of the slice: x: 2, y: 2, z: 4, core: 2. Of those that a mesh axis runs over, the one named last changes fastest.
Arguments:
- schur: bfloat16 [4, 8, 1024, 1024], P('group', 'sub'), as said below
- local_inverse: bfloat16 [4, 8, 1024, 1024], P('group', 'sub'), as said below
- rhs_parts: bfloat16 [4, 8, 1024, 128], P('group', 'sub'), may hold values from -6 to 6
- basis: bfloat16 [4, 8, 32, 1024], P('group', 'sub'), may hold values from -0.1875 to 0.1875
- coarse_map: int32 [4, 8, 32], P('group', 'sub'), may hold values from 0 to 1023
- coarse_inverse: bfloat16 [4, 1024, 1024], P('group', 'sub'), as said below
- shared_rows: int32 [4, 8, 2, 4, 256], P('group', 'sub'), may hold values from 0 to 1023, as said below
- shared_counts: int32 [4, 8, 4], P('group', 'sub'), may hold values from 0 to 256, as said below
Outputs:
- solution: float32 [4, 8, 1024, 128], P('group', 'sub')
- residual: float32 [4, 8, 1024, 128], P('group', 'sub')
Inputs may be any that keep to these rules, and one draw needn't show every extreme that they name: `schur`: each subdomain matrix is symmetric positive definite. `local_inverse`: each subdomain matrix is symmetric positive definite. `coarse_inverse`: each group's matrix is symmetric positive definite. `shared_rows`: own rows of direction d lie in rows d * 256 to (d + 1) * 256 - 1 and are distinct within a list; the own rows of direction 0 of (g, s) are the partner rows of direction 1 of (g, s + 1) and the reverse, likewise directions 2 and 3 between (g, s) and (g + 1, s); entries past the count are rows of the same block. `shared_counts`: the count of direction 0 of (g, s) equals the count of direction 1 of (g, s + 1), that of direction 2 of (g, s) the count of direction 3 of (g + 1, s); counts are 0 where no neighbour exists; some count equals 256.
All inputs are finite; a program needn't handle non-finite values.
Results may differ from a plain program's by a relative error of at most 0.014.
Values may be sent and summed in bfloat16 or wider, within the bound.
No kernel may reach another device: no remote copies, remote signals or barrier semaphores. Data moves between devices by JAX's collectives and lax.ppermute only.
A program may use at most 64 MiB of HBM per device.

v0:
```python
import functools

import jax
import jax.numpy as jnp
from jax import lax
from jax.experimental import pallas as pl
from jax.experimental.pallas import tpu as pltpu
from jax.sharding import PartitionSpec as P

ITERS = 3
TAIL = 16
HIGHEST = lax.Precision.HIGHEST


def swap(x, axis, bit):
    return lax.ppermute(x, axis, [(i, i ^ bit) for i in range(lax.axis_size(axis))])


def bits_of(axis):
    count = lax.axis_size(axis)
    if count & (count - 1):
        raise ValueError("axis size")
    return [1 << b for b in range(count.bit_length() - 1)]


def total(kept, sent):
    half = kept + swap(sent, "group", 1)
    rest = [("group", bit) for bit in bits_of("group")[1:]]
    subs = [("sub", bit) for bit in bits_of("sub")]
    for axis, bit in subs[:1] + rest + subs[1:]:
        half = half + swap(half, axis, bit)
    return half, swap(half, "group", 1)


def gather_sub(x):
    for bit in bits_of("sub"):
        x = jnp.concatenate([x, swap(x, "sub", bit)], axis=0)
    return x


def eliminate(matrix, block, tile=8):
    n, width = matrix.shape[0], block.shape[1]
    sublane = lax.broadcasted_iota(jnp.int32, (tile, 1), 0)
    left = [matrix[i : i + tile] for i in range(0, n, tile)]
    right = [block[i : i + tile] for i in range(0, n, tile)]
    for k in range(n // tile):
        pivot_left, pivot_right = left[k], right[k]
        at = k * tile
        spread = [
            jnp.broadcast_to(pivot_left[:, at + j : at + j + 1], (tile, n)) for j in range(tile)
        ]
        for j in range(tile):
            inverse = 1.0 / spread[j][j : j + 1]
            here = sublane == j
            column = spread[j]

            def cleared(rows, column=column, inverse=inverse, here=here, j=j):
                pivot = rows[j : j + 1] * inverse
                return jnp.where(here, pivot, rows - column * pivot)

            for i in range(j + 1, tile):
                spread[i] = cleared(spread[i])
            pivot_left, pivot_right = cleared(pivot_left), cleared(pivot_right)
        for i in range(n // tile):
            if i == k:
                continue
            old = left[i]
            new_left, new_right = old, right[i]
            for j in range(tile):
                scale = jnp.broadcast_to(old[:, at + j : at + j + 1], (tile, n))
                new_left = new_left - scale * pivot_left[j : j + 1]
                new_right = new_right - scale * pivot_right[j : j + 1]
            left[i], right[i] = new_left, new_right
        left[k], right[k] = pivot_left, pivot_right
    return jnp.concatenate(right, axis=0)


def exact(a, b):
    return jnp.dot(a, b, precision=HIGHEST, preferred_element_type=jnp.float32)


def symmetric(a):
    return (a + a.T) * 0.5


def halves(x):
    high = x.astype(jnp.bfloat16)
    low = (x - high.astype(jnp.float32)).astype(jnp.bfloat16)
    return jnp.concatenate([high, low], axis=1)


def folded(both):
    n = both.shape[1] // 2
    return both[:, :n] + both[:, n:]


def times(matrix, x, contracting=1):
    dims = (((contracting,), (0,)), ((), ()))
    if x.dtype == jnp.bfloat16:
        return lax.dot_general(matrix, x, dims, preferred_element_type=jnp.float32)
    return folded(lax.dot_general(matrix, halves(x), dims, preferred_element_type=jnp.float32))


def mixer(mixing):
    both = halves(mixing)
    return jnp.concatenate([both, both], axis=0)


def mix(block, mixer_value):
    return folded(jnp.dot(halves(block), mixer_value, preferred_element_type=jnp.float32))


def local_gram(weighted, right):
    n = weighted.shape[1]
    both = lax.dot_general(
        halves(weighted),
        halves(right),
        (((0,), (0,)), ((), ())),
        preferred_element_type=jnp.float32,
    )
    both = both[:n] + both[n:]
    return both[:, :n] + both[:, n:]


def packed(inner, cross):
    n = inner.shape[0]
    rows = lax.broadcasted_iota(jnp.int32, (n, n), 0)
    columns = lax.broadcasted_iota(jnp.int32, (n, n), 1)
    body = jnp.where(rows > columns, inner, jnp.where(rows < columns, cross, 0.0))
    tail_rows = lax.broadcasted_iota(jnp.int32, (TAIL, n), 0)
    first = jnp.sum(jnp.where(rows == columns, inner, 0.0), axis=0, keepdims=True)
    second = jnp.sum(jnp.where(rows == columns, cross, 0.0), axis=0, keepdims=True)
    tail = jnp.where(tail_rows == 0, first, jnp.where(tail_rows == 1, second, 0.0))
    return jnp.concatenate([body, tail], axis=0)


def unpacked(grams):
    n = grams.shape[1]
    rows = lax.broadcasted_iota(jnp.int32, (n, n), 0)
    columns = lax.broadcasted_iota(jnp.int32, (n, n), 1)
    body = grams[:n]
    lower = jnp.where(rows > columns, body, 0.0)
    upper = jnp.where(rows < columns, body, 0.0)
    inner = lower + lower.T + jnp.where(rows == columns, grams[n : n + 1], 0.0)
    cross = upper + upper.T + jnp.where(rows == columns, grams[n + 1 : n + 2], 0.0)
    return inner, cross


def zone_of(parity, slot):
    flip = parity[slot // 2]
    return 2 * (slot // 2) + (flip if slot % 2 == 0 else 1 - flip)


def assemble_into(parity, tables, slots, received, out):
    zone = slots[0].shape[0]
    for slot in range(4):
        start = pl.multiple_of(zone_of(parity, slot) * zone, zone)
        value = slots[slot][:zone].astype(jnp.float32) + times(tables[slot], received[slot][:zone])
        out[pl.ds(start, zone)] = value


def slots_from(parity, block, slots):
    zone = slots[0].shape[0]
    for slot in range(4):
        pair = 2 * (slot // 2)
        swapped = parity[slot // 2] == (1 if slot % 2 == 0 else 0)
        low, high = block[pair * zone : (pair + 1) * zone], block[(pair + 1) * zone : (pair + 2) * zone]
        slots[slot][:zone] = jnp.where(swapped, high, low)


def choice_kernel(first, maps, inverse_rows, out):
    count, modes, total_modes = out.shape
    rows_here, coarse_total = inverse_rows.shape
    unknown = lax.broadcasted_iota(jnp.int32, (coarse_total, total_modes), 0)
    columns = (unknown == maps[...]).astype(jnp.float32).astype(jnp.bfloat16)
    picked = jnp.dot(inverse_rows[...], columns, preferred_element_type=jnp.float32)
    here = lax.broadcasted_iota(jnp.int32, (rows_here, total_modes), 0) + first[0]
    rows = (here == maps[...]).astype(jnp.float32).astype(jnp.bfloat16)
    table = lax.dot_general(
        rows,
        picked.astype(jnp.bfloat16),
        (((0,), (0,)), ((), ())),
        preferred_element_type=jnp.float32,
    ).astype(jnp.bfloat16)
    source = lax.broadcasted_iota(jnp.int32, (total_modes, total_modes), 0)
    target = lax.broadcasted_iota(jnp.int32, (total_modes, total_modes), 1)
    for j in range(count):
        order = (source == (target ^ (j * modes))).astype(jnp.float32).astype(jnp.bfloat16)
        block = table[j * modes : (j + 1) * modes]
        out[j] = jnp.dot(block, order, preferred_element_type=jnp.float32).astype(jnp.bfloat16)


def fold_kernel(grams, own, received, out):
    count = own.shape[0] - grams
    if grams:
        out[:grams] = own[:grams] + received[:grams]
    out[grams : grams + count] = own[grams:]
    out[grams + count :] = received[grams:]


def tables_kernel(parity, rows, counts, tables, weight):
    capacity = rows.shape[2]
    place = lax.broadcasted_iota(jnp.int32, (capacity, capacity), 0)
    entry = lax.broadcasted_iota(jnp.int32, (1, capacity), 1)
    for slot in range(4):
        d = zone_of(parity, slot)
        partner_zone = zone_of(parity, slot ^ 1)
        own = rows[0, pl.ds(d, 1)] - d * capacity
        partner = rows[1, pl.ds(d, 1)] - partner_zone * capacity
        own = jnp.where(entry < counts[d], own, -1)
        to = (place == own).astype(jnp.float32).astype(jnp.bfloat16)
        source = (place == partner).astype(jnp.float32).astype(jnp.bfloat16)
        table = lax.dot_general(
            to, source, (((1,), (1,)), ((), ())), preferred_element_type=jnp.float32
        )
        tables[slot] = table.astype(jnp.bfloat16)
        ones = jnp.ones((capacity, weight.shape[1]), jnp.bfloat16)
        shared = jnp.dot(table.astype(jnp.bfloat16), ones, preferred_element_type=jnp.float32)
        weight[pl.ds(pl.multiple_of(d * capacity, capacity), capacity)] = 1.0 / (1.0 + shared)


def start_kernel(parity, tables, weight, basis, *refs):
    slots, received, (block, piece) = refs[:4], refs[4:8], refs[8:]
    assemble_into(parity, tables, slots, received, block)
    piece[...] = times(basis[...], weight[...] * block[...])


def gram_start_kernel(parity, tables, weight, basis, z, r, *refs):
    slots, received, (block, carried) = refs[:4], refs[4:8], refs[8:]
    n = z.shape[1]
    assemble_into(parity, tables, slots, received, block)
    carried[n + TAIL :] = times(basis[...], weight[...] * block[...])
    weighted = weight[...] * z[...]
    carried[: n + TAIL] = packed(local_gram(weighted, r[...]), local_gram(weighted, block[...]))


def local_kernel(weight, matrix, block, out):
    out[...] = times(matrix[...], weight[...] * block[...])


def finish_kernel(grams, parity, weight, basis, chosen, local, own, received, *slots):
    pieces = jnp.concatenate([own[grams:], received[grams:]], axis=0)
    picked = times(chosen[...], pieces)
    smoothed = weight[...] * (local[...] + times(basis[...], picked, contracting=0))
    slots_from(parity, smoothed, slots)
    if grams:
        slots[2][slots[0].shape[0] :] = own[:grams] + received[:grams]


def operator_kernel(parity, tables, matrix, *refs):
    slots, received, block, out = refs[:4], refs[4:8], refs[8], refs[9:13]
    zone = out[0].shape[0]
    assemble_into(parity, tables, slots, received, block)
    slots_from(parity, times(matrix[...], block[...]), out)
    for grams in refs[13:]:
        grams[...] = slots[2][zone:] + received[2][zone:]


def first_update_kernel(parity, tables, weight, basis, grams, z, w, r, m, *refs):
    slots, received = refs[:4], refs[4:8]
    x, r_out, z_out, w_out, image, curvature_out, carried = refs[8:]
    n = z.shape[1]
    assemble_into(parity, tables, slots, received, image)
    inner, cross = unpacked(grams[...])
    curvature_out[...] = cross
    alpha = mixer(eliminate(cross, inner))
    w_new = w[...] - mix(image[...], alpha)
    w_out[...] = w_new
    carried[n + TAIL :] = times(basis[...], weight[...] * w_new)
    x[...] = mix(z[...], alpha)
    r_new = r[...] - mix(w[...], alpha)
    r_out[...] = r_new
    z_new = z[...] - mix(m[...], alpha)
    z_out[...] = z_new
    weighted = weight[...] * z_new
    carried[: n + TAIL] = packed(local_gram(weighted, r_new), local_gram(weighted, w_new))


def step_sizes(grams, inner_inverse, curvature):
    inner, cross = unpacked(grams)
    beta = exact(inner_inverse[...], inner)
    bent = symmetric(cross - exact(beta.T, exact(curvature[...], beta)))
    return beta, bent, eliminate(bent, inner)


def next_update_kernel(
    parity, tables, weight, basis, grams, inner_inverse, curvature,
    z, w, r, m, p, s, q, t, x, *refs
):
    slots, received = refs[:4], refs[4:8]
    (
        x_out, r_out, z_out, w_out, p_out, s_out, q_out, t_out, curvature_out, *carried
    ) = refs[8:]
    assemble_into(parity, tables, slots, received, t_out)
    beta, bent, alpha = step_sizes(grams[...], inner_inverse, curvature)
    curvature_out[...] = bent
    beta, alpha = mixer(beta), mixer(alpha)
    t_out[...] = t_out[...] + mix(t[...], beta)
    w_new = w[...] - mix(t_out[...], alpha)
    w_out[...] = w_new
    p_out[...] = z[...] + mix(p[...], beta)
    s_out[...] = w[...] + mix(s[...], beta)
    q_out[...] = m[...] + mix(q[...], beta)
    x_out[...] = x[...] + mix(p_out[...], alpha)
    r_new = r[...] - mix(s_out[...], alpha)
    r_out[...] = r_new
    z_new = z[...] - mix(q_out[...], alpha)
    z_out[...] = z_new
    weighted = weight[...] * z_new
    sums = packed(local_gram(weighted, r_new), local_gram(weighted, w_new))
    if len(carried) == 1:
        rows = sums.shape[0]
        carried[0][:rows] = sums
        carried[0][rows:] = times(basis[...], weight[...] * w_new)
    else:
        kept, sent = carried
        low, high = sums[: kept.shape[0]], sums[kept.shape[0] :]
        kept[...] = jnp.where(parity[1] == 0, low, high)
        sent[...] = jnp.where(parity[1] == 0, high, low)


def last_update_kernel(parity, half, other, inner_inverse, curvature, z, w, r, p, s, x, x_out, r_out):
    low = jnp.where(parity[1] == 0, half[...], other[...])
    high = jnp.where(parity[1] == 0, other[...], half[...])
    sums = jnp.concatenate([low, high], axis=0)
    beta, _, alpha = step_sizes(sums, inner_inverse, curvature)
    beta, alpha = mixer(beta), mixer(alpha)
    x_out[...] = x[...] + mix(z[...] + mix(p[...], beta), alpha)
    r_out[...] = r[...] - mix(w[...] + mix(s[...], beta), alpha)


def inverse_kernel(grams, out):
    n = out.shape[0]
    rows = lax.broadcasted_iota(jnp.int32, (n, n), 0)
    columns = lax.broadcasted_iota(jnp.int32, (n, n), 1)
    inner, _ = unpacked(grams[...])
    out[...] = eliminate(inner, (rows == columns).astype(jnp.float32))


VMEM = pl.BlockSpec(memory_space=pltpu.VMEM)
SMEM = pl.BlockSpec(memory_space=pltpu.SMEM)


def call(kernel, name, flops, outs, *args):
    shapes = [jax.ShapeDtypeStruct(shape, dtype) for shape, dtype in outs]
    moved = sum(a.size * a.dtype.itemsize for a in (*args, *shapes))
    return pl.pallas_call(
        kernel,
        out_shape=shapes,
        in_specs=[SMEM if a.ndim == 1 else VMEM for a in args],
        out_specs=[VMEM] * len(shapes),
        name=name,
        compiler_params=pltpu.CompilerParams(vmem_limit_bytes=24 * 1024 * 1024),
        cost_estimate=pl.CostEstimate(flops=flops, bytes_accessed=moved, transcendentals=0),
    )(*args)


def pairs(axis, first):
    count = lax.axis_size(axis)
    low = range(first, count - 1, 2)
    return [(i, i + 1) for i in low] + [(i + 1, i) for i in low]


def exchange(slots):
    return [
        lax.ppermute(slot, axis, pairs(axis, first))
        for slot, (axis, first) in zip(
            slots, (("sub", 0), ("sub", 1), ("group", 0), ("group", 1))
        )
    ]


def shards(
    schur, local_inverse, rhs_parts, basis, coarse_map, coarse_inverse, shared_rows, shared_counts
):
    schur, local_inverse, basis = schur[0, 0], local_inverse[0, 0], basis[0, 0]
    rhs = rhs_parts[0, 0]
    rows, columns = rhs.shape
    zone = shared_rows.shape[-1]
    modes = basis.shape[0]
    parity = jnp.stack([lax.axis_index("sub") % 2, lax.axis_index("group") % 2]).astype(jnp.int32)
    block = ((rows, columns), jnp.float32)
    part = ((zone, columns), jnp.float32)
    square = ((columns, columns), jnp.float32)
    sums = columns + TAIL
    share = ((modes, columns), jnp.float32)
    carry = ((sums + modes, columns), jnp.float32)
    halves_out = [((sums // 2, columns), jnp.float32)] * 2
    solve_flops = 400_000_000
    product_flops = 4 * rows * rows * columns

    def rhs_zone(slot):
        return lax.dynamic_slice_in_dim(rhs, zone_of(parity, slot) * zone, zone, axis=0)

    rhs_slots = [rhs_zone(slot) for slot in range(4)]
    received = exchange(rhs_slots)
    tables, weight = call(
        tables_kernel,
        "shared_row_tables",
        16 * zone**3,
        [((4, zone, zone), jnp.bfloat16), block],
        parity,
        shared_rows[0, 0],
        shared_counts[0, 0],
    )
    subs = lax.axis_size("sub")
    inverse_rows = coarse_inverse[0]
    (chosen,) = call(
        choice_kernel,
        "selected_inverse",
        product_flops // 4,
        [((subs, modes, subs * modes), jnp.bfloat16)],
        (lax.axis_index("sub") * inverse_rows.shape[0]).astype(jnp.int32)[None],
        gather_sub(coarse_map[0, 0])[None],
        inverse_rows,
    )
    for bit in reversed(bits_of("sub")):
        chosen = chosen[:bit] + swap(chosen[bit:], "sub", bit)
    chosen = chosen[0]

    def precondition(vector, carried):
        grams = carried.shape[0] - modes
        (local,) = call(
            local_kernel, "local_inverse", product_flops, [block], weight, local_inverse, vector
        )
        bits = bits_of("sub")
        for bit in bits[:-1]:
            rows_out = 2 * carried.shape[0] - grams
            (carried,) = call(
                functools.partial(fold_kernel, grams),
                "fold",
                columns * rows_out,
                [((rows_out, columns), jnp.float32)],
                carried,
                swap(carried, "sub", bit),
            )
        slots = call(
            functools.partial(finish_kernel, grams),
            "coarse_part",
            product_flops // 8,
            [part, part, ((zone + grams, columns), jnp.float32), part],
            parity,
            weight,
            basis,
            chosen,
            local,
            carried,
            swap(carried, "sub", bits[-1]),
        )
        return slots, exchange(slots)

    def operator(slots, received):
        grams = slots[2].shape[0] - zone
        outs = [((grams, columns), jnp.float32)] if grams else []
        vector, *image = call(
            operator_kernel,
            "operator",
            product_flops,
            [block] + [part] * 4 + outs,
            parity,
            tables,
            schur,
            *slots,
            *received,
        )
        whole = image[4:]
        for bit in bits_of("group")[1:] if grams else ():
            whole = [whole[0] + swap(whole[0], "group", bit)]
        return vector, image[:4], exchange(image[:4]), *whole

    r, pieces = call(
        start_kernel,
        "start",
        product_flops // 8,
        [block, share],
        parity,
        tables,
        weight,
        basis,
        *rhs_slots,
        *received,
    )
    z, image, received = operator(*precondition(r, pieces))
    w, carried = call(
        gram_start_kernel,
        "start_grams",
        product_flops // 4,
        [block, carry],
        parity,
        tables,
        weight,
        basis,
        z,
        r,
        *image,
        *received,
    )
    for iteration in range(ITERS - 1):
        final = iteration + 2 == ITERS
        m, image, received, grams = operator(*precondition(w, carried))
        common = (parity, tables, weight, basis, grams)
        if iteration == 0:
            p, s, q = z, w, m
            x, r, z, w, t, curvature, carried = call(
                first_update_kernel,
                "first_update",
                2 * solve_flops,
                [block] * 5 + [square, carry],
                *common,
                z,
                w,
                r,
                m,
                *image,
                *received,
            )
        else:
            x, r, z, w, p, s, q, t, curvature, *carried = call(
                next_update_kernel,
                "next_update",
                2 * solve_flops,
                [block] * 8 + [square] + (halves_out if final else [carry]),
                *common,
                inner_inverse,
                curvature,
                z,
                w,
                r,
                m,
                p,
                s,
                q,
                t,
                x,
                *image,
                *received,
            )
            if not final:
                (carried,) = carried
        grams, curvature = lax.optimization_barrier((grams, curvature))
        (inner_inverse,) = call(inverse_kernel, "inner_inverse", solve_flops, [square], grams)
    grams = total(*carried)
    x, r = call(
        last_update_kernel,
        "last_update",
        2 * solve_flops,
        [block, block],
        parity,
        *grams,
        inner_inverse,
        curvature,
        z,
        w,
        r,
        p,
        s,
        x,
    )
    return x[None, None], r[None, None]


def solution(mesh):
    placed = (
        P("group", "sub", None, None),
        P("group", "sub", None, None),
        P("group", "sub", None, None),
        P("group", "sub", None, None),
        P("group", "sub", None),
        P("group", "sub", None),
        P("group", "sub", None, None, None),
        P("group", "sub", None),
    )
    return jax.shard_map(
        shards,
        mesh=mesh,
        in_specs=placed,
        out_specs=(P("group", "sub", None, None), P("group", "sub", None, None)),
        check_vma=False,
    )
```

profile of v0, /device:TPU:0, one launch (start us, length us, event | category | flops | bytes accessed | tf_op | source)
XLA Modules:
  0.0 197.7 jit_solution(6872853266931598987)
XLA Ops:
  0.6 3.0 %collective-permute-start = (s32[32]{0:T(128)}, s32[32]{0:T(128)S(1)}, u32[]{:S(2)}, u32[]{:S(2)}) collective-permute-start(s32[32]{0:T(128)} %bitcast.40), channel_id=1, source_target_pairs={{0,1},{1,0},{2,3},{3,2},{4,5},{5,4},{6,7},{7,6},{8,9},{9,8},{10,11... | collective-permute-start | bytes 392 | tf_op jit(solution)/shard_map/ppermute | solution.py:16
  3.7 1.7 collective-permute-done
  6.1 2.1 %collective-permute-start.1 = (s32[64]{0:T(128)S(1)}, s32[64]{0:T(128)S(1)}, u32[]{:S(2)}, u32[]{:S(2)}) collective-permute-start(s32[64]{0:T(128)S(1)} %pad_add_fusion.2), channel_id=1, source_target_pairs={{0,2},{1,3},{2,0},{3,1},{4,6},{5,7},{6,4},{7,5},{8,10},{9,11},{10,... | collective-permute-start | bytes 776 | tf_op jit(solution)/shard_map/ppermute | solution.py:16
  8.1 1.0 dynamic-slice_bitcast_fusion
  10.4 3.0 %collective-permute-start.2 = (s32[128]{0:T(128)S(1)}, s32[128]{0:T(128)S(1)}, u32[]{:S(2)}, u32[]{:S(2)}) collective-permute-start(s32[128]{0:T(128)S(1)} %pad_add_fusion.3), channel_id=1, source_target_pairs={{0,4},{1,5},{2,6},{3,7},{4,0},{5,1},{6,2},{7,3},{8,12},{9,13},{10,... | collective-permute-start | bytes 1544 | tf_op jit(solution)/shard_map/ppermute | solution.py:16
  14.8 4.3 %collective-permute-start.6 = (bf16[256,128]{1,0:T(8,128)(2,1)S(1)}, bf16[256,128]{1,0:T(8,128)(2,1)S(1)}, u32[]{:S(2)}, u32[]{:S(2)}) collective-permute-start(bf16[256,128]{1,0:T(8,128)(2,1)S(1)} %get-tuple-element.118.refs_0_), channel_id=1, source_target_pairs={{0,1},{2,3},{4,5},{6,7},{1,0},{3,2},{5,4},{7,6},{8,9},{10,11},{12,... | collective-permute-start | bytes 196616 | tf_op jit(solution)/shard_map/ppermute | solution.py:366
  19.1 2.3 %collective-permute-start.8 = (bf16[256,128]{1,0:T(8,128)(2,1)S(1)}, bf16[256,128]{1,0:T(8,128)(2,1)S(1)}, u32[]{:S(2)}, u32[]{:S(2)}) collective-permute-start(bf16[256,128]{1,0:T(8,128)(2,1)S(1)} %get-tuple-element.119.refs_2_), channel_id=1, source_target_pairs={{0,8},{16,24},{8,0},{24,16},{1,9},{17,25},{9,1},{25,17},{2,10},{18... | collective-permute-start | bytes 196616 | tf_op jit(solution)/shard_map/ppermute | solution.py:366
  22.1 0.9 copy-done.3
  23.8 1.4 collective-permute-start.3
  25.2 4.7 %collective-permute-done.3 = bf16[4,32,256]{2,1,0:T(8,128)(2,1)S(1)} collective-permute-done((bf16[4,32,256]{2,1,0:T(8,128)(2,1)S(1)}, bf16[4,32,256]{2,1,0:T(8,128)(2,1)S(1)}, u32[]{:S(2)}, u32[]{:S(2)}) %collective-permute-start.3) | collective-permute-done | bytes 65568 | tf_op jit(solution)/shard_map/ppermute | solution.py:16
  31.4 1.2 shared_row_tables.1
  32.7 1.1 start.1
  33.8 1.1 collective-permute-start.10
  34.9 2.7 %collective-permute-done.10.received = f32[32,128]{1,0:T(8,128)S(1)} collective-permute-done((f32[32,128]{1,0:T(8,128)S(1)}, f32[32,128]{1,0:T(8,128)S(1)}, u32[]{:S(2)}, u32[]{:S(2)}) %collective-permute-start.10) | collective-permute-done | bytes 16416 | tf_op jit(solution)/shard_map/ppermute | solution.py:16
  37.6 2.0 %collective-permute-start.11 = (f32[64,128]{1,0:T(8,128)S(1)}, f32[64,128]{1,0:T(8,128)S(1)}, u32[]{:S(2)}, u32[]{:S(2)}) collective-permute-start(f32[64,128]{1,0:T(8,128)S(1)} %fold.6.own), channel_id=1, source_target_pairs={{0,2},{1,3},{2,0},{3,1},{4,6},{5,7},{6,4},{7,5},{8,10},{9,11},{10,... | collective-permute-start | bytes 98312 | tf_op jit(solution)/shard_map/ppermute | solution.py:16
  39.6 0.9 collective-permute-start.5
  41.5 1.1 collective-permute-start.12
  42.6 0.9 collective-permute-done.5
  43.4 3.2 %collective-permute-done.12.received = f32[128,128]{1,0:T(8,128)S(1)} collective-permute-done((f32[128,128]{1,0:T(8,128)S(1)}, f32[128,128]{1,0:T(8,128)S(1)}, u32[]{:S(2)}, u32[]{:S(2)}) %collective-permute-start.12) | collective-permute-done | bytes 65568 | tf_op jit(solution)/shard_map/ppermute | solution.py:16
  46.7 1.0 coarse_part.3
  47.7 1.1 collective-permute-start.13
  50.2 2.5 %collective-permute-done.13.refs_4_ = f32[256,128]{1,0:T(8,128)S(1)} collective-permute-done((f32[256,128]{1,0:T(8,128)S(1)}, f32[256,128]{1,0:T(8,128)S(1)}, u32[]{:S(2)}, u32[]{:S(2)}) %collective-permute-start.13) | collective-permute-done | bytes 131104 | tf_op jit(solution)/shard_map/ppermute | solution.py:366
  52.7 1.6 operator.3
  54.3 4.9 %collective-permute-start.17 = (f32[256,128]{1,0:T(8,128)S(1)}, f32[256,128]{1,0:T(8,128)S(1)}, u32[]{:S(2)}, u32[]{:S(2)}) collective-permute-start(f32[256,128]{1,0:T(8,128)S(1)} %get-tuple-element.68.refs_0_), channel_id=1, source_target_pairs={{0,1},{2,3},{4,5},{6,7},{1,0},{3,2},{5,4},{7,6},{8,9},{10,11},{12,... | collective-permute-start | bytes 393224 | tf_op jit(solution)/shard_map/ppermute | solution.py:366
  59.8 3.1 %collective-permute-start.19 = (f32[256,128]{1,0:T(8,128)S(1)}, f32[256,128]{1,0:T(8,128)S(1)}, u32[]{:S(2)}, u32[]{:S(2)}) collective-permute-start(f32[256,128]{1,0:T(8,128)S(1)} %get-tuple-element.70.refs_2_), channel_id=1, source_target_pairs={{0,8},{16,24},{8,0},{24,16},{1,9},{17,25},{9,1},{25,17},{2,10},{18... | collective-permute-start | bytes 393224 | tf_op jit(solution)/shard_map/ppermute | solution.py:366
  63.9 1.5 start_grams.1
  65.4 4.4 %collective-permute-start.21 = (f32[176,128]{1,0:T(8,128)S(1)}, f32[176,128]{1,0:T(8,128)S(1)}, u32[]{:S(2)}, u32[]{:S(2)}) collective-permute-start(f32[176,128]{1,0:T(8,128)S(1)} %get-tuple-element.73.own), channel_id=1, source_target_pairs={{0,1},{1,0},{2,3},{3,2},{4,5},{5,4},{6,7},{7,6},{8,9},{9,8},{10,11... | collective-permute-start | bytes 270344 | tf_op jit(solution)/shard_map/ppermute | solution.py:16
  69.8 2.5 %collective-permute-done.21.received = f32[176,128]{1,0:T(8,128)S(1)} collective-permute-done((f32[176,128]{1,0:T(8,128)S(1)}, f32[176,128]{1,0:T(8,128)S(1)}, u32[]{:S(2)}, u32[]{:S(2)}) %collective-permute-start.21) | collective-permute-done | bytes 90144 | tf_op jit(solution)/shard_map/ppermute | solution.py:16
  72.3 4.0 %collective-permute-start.22 = (f32[208,128]{1,0:T(8,128)S(1)}, f32[208,128]{1,0:T(8,128)S(1)}, u32[]{:S(2)}, u32[]{:S(2)}) collective-permute-start(f32[208,128]{1,0:T(8,128)S(1)} %fold.8.own), channel_id=1, source_target_pairs={{0,2},{1,3},{2,0},{3,1},{4,6},{5,7},{6,4},{7,5},{8,10},{9,11},{10,... | collective-permute-start | bytes 319496 | tf_op jit(solution)/shard_map/ppermute | solution.py:16
  76.4 3.7 %collective-permute-done.22.received = f32[208,128]{1,0:T(8,128)S(1)} collective-permute-done((f32[208,128]{1,0:T(8,128)S(1)}, f32[208,128]{1,0:T(8,128)S(1)}, u32[]{:S(2)}, u32[]{:S(2)}) %collective-permute-start.22) | collective-permute-done | bytes 106528 | tf_op jit(solution)/shard_map/ppermute | solution.py:16
  80.9 8.8 %collective-permute-done.23.received = f32[272,128]{1,0:T(8,128)S(1)} collective-permute-done((f32[272,128]{1,0:T(8,128)S(1)}, f32[272,128]{1,0:T(8,128)S(1)}, u32[]{:S(2)}, u32[]{:S(2)}) %collective-permute-start.23) | collective-permute-done | bytes 139296 | tf_op jit(solution)/shard_map/ppermute | solution.py:16
  89.8 1.0 coarse_part.4
  92.8 4.0 %collective-permute-done.24.refs_4_ = f32[256,128]{1,0:T(8,128)S(1)} collective-permute-done((f32[256,128]{1,0:T(8,128)S(1)}, f32[256,128]{1,0:T(8,128)S(1)}, u32[]{:S(2)}, u32[]{:S(2)}) %collective-permute-start.24) | collective-permute-done | bytes 131104 | tf_op jit(solution)/shard_map/ppermute | solution.py:366
  96.8 1.6 operator.4
  98.4 4.6 %collective-permute-start.29 = (f32[256,128]{1,0:T(8,128)S(1)}, f32[256,128]{1,0:T(8,128)S(1)}, u32[]{:S(2)}, u32[]{:S(2)}) collective-permute-start(f32[256,128]{1,0:T(8,128)S(1)} %get-tuple-element.80.refs_0_), channel_id=1, source_target_pairs={{0,1},{2,3},{4,5},{6,7},{1,0},{3,2},{5,4},{7,6},{8,9},{10,11},{12,... | collective-permute-start | bytes 393224 | tf_op jit(solution)/shard_map/ppermute | solution.py:366
  104.5 3.4 %collective-permute-start.28 = (f32[144,128]{1,0:T(8,128)S(1)}, f32[144,128]{1,0:T(8,128)S(1)}, u32[]{:S(2)}, u32[]{:S(2)}) collective-permute-start(f32[144,128]{1,0:T(8,128)S(1)} %get-tuple-element.78), channel_id=1, source_target_pairs={{0,16},{8,24},{16,0},{24,8},{1,17},{9,25},{17,1},{25,9},{2,18},{10... | collective-permute-start | bytes 221192 | tf_op jit(solution)/shard_map/ppermute | solution.py:16
  108.0 4.3 %collective-permute-done.28 = f32[144,128]{1,0:T(8,128)S(1)} collective-permute-done((f32[144,128]{1,0:T(8,128)S(1)}, f32[144,128]{1,0:T(8,128)S(1)}, u32[]{:S(2)}, u32[]{:S(2)}) %collective-permute-start.28) | collective-permute-done | bytes 73760 | tf_op jit(solution)/shard_map/ppermute | solution.py:16
  112.3 6.7 %first_update.1 = (f32[1024,128]{1,0:T(8,128)S(1)}, f32[1024,128]{1,0:T(8,128)S(1)}, f32[1024,128]{1,0:T(8,128)S(1)}, f32[1024,128]{1,0:T(8,128)S(1)}, f32[1024,...) custom-call(s32[2]{0:T(128)S(1)} %pad_add_fusion.1.parity, ...), custom_call_target="tpu_custom_call" | custom-call | flops 800000000 | bytes 7110664 | tf_op jit(solution)/shard_map/first_update/pallas_call | solution.py:347
  119.0 3.2 %collective-permute-start.33 = (f32[176,128]{1,0:T(8,128)S(1)}, f32[176,128]{1,0:T(8,128)S(1)}, u32[]{:S(2)}, u32[]{:S(2)}) collective-permute-start(f32[176,128]{1,0:T(8,128)S(1)} %get-tuple-element.85.own), channel_id=1, source_target_pairs={{0,1},{1,0},{2,3},{3,2},{4,5},{5,4},{6,7},{7,6},{8,9},{9,8},{10,11... | collective-permute-start | bytes 270344 | tf_op jit(solution)/shard_map/ppermute | solution.py:16
  122.2 2.5 %collective-permute-done.33.received = f32[176,128]{1,0:T(8,128)S(1)} collective-permute-done((f32[176,128]{1,0:T(8,128)S(1)}, f32[176,128]{1,0:T(8,128)S(1)}, u32[]{:S(2)}, u32[]{:S(2)}) %collective-permute-start.33) | collective-permute-done | bytes 90144 | tf_op jit(solution)/shard_map/ppermute | solution.py:16
  124.7 1.7 collective-permute-start.34
  126.4 3.0 %collective-permute-done.34.received = f32[208,128]{1,0:T(8,128)S(1)} collective-permute-done((f32[208,128]{1,0:T(8,128)S(1)}, f32[208,128]{1,0:T(8,128)S(1)}, u32[]{:S(2)}, u32[]{:S(2)}) %collective-permute-start.34) | collective-permute-done | bytes 106528 | tf_op jit(solution)/shard_map/ppermute | solution.py:16
  129.5 3.3 %collective-permute-start.35 = (f32[272,128]{1,0:T(8,128)S(1)}, f32[272,128]{1,0:T(8,128)S(1)}, u32[]{:S(2)}, u32[]{:S(2)}) collective-permute-start(f32[272,128]{1,0:T(8,128)S(1)} %fold.11.own), channel_id=1, source_target_pairs={{0,4},{1,5},{2,6},{3,7},{4,0},{5,1},{6,2},{7,3},{8,12},{9,13},{10,... | collective-permute-start | bytes 417800 | tf_op jit(solution)/shard_map/ppermute | solution.py:16
  133.5 3.8 %collective-permute-done.35.received = f32[272,128]{1,0:T(8,128)S(1)} collective-permute-done((f32[272,128]{1,0:T(8,128)S(1)}, f32[272,128]{1,0:T(8,128)S(1)}, u32[]{:S(2)}, u32[]{:S(2)}) %collective-permute-start.35) | collective-permute-done | bytes 139296 | tf_op jit(solution)/shard_map/ppermute | solution.py:16
  137.3 1.0 coarse_part.5
  140.0 4.2 %collective-permute-done.36.refs_4_ = f32[256,128]{1,0:T(8,128)S(1)} collective-permute-done((f32[256,128]{1,0:T(8,128)S(1)}, f32[256,128]{1,0:T(8,128)S(1)}, u32[]{:S(2)}, u32[]{:S(2)}) %collective-permute-start.36) | collective-permute-done | bytes 131104 | tf_op jit(solution)/shard_map/ppermute | solution.py:366
  144.3 1.6 operator.5
  145.9 4.6 %collective-permute-start.41 = (f32[256,128]{1,0:T(8,128)S(1)}, f32[256,128]{1,0:T(8,128)S(1)}, u32[]{:S(2)}, u32[]{:S(2)}) collective-permute-start(f32[256,128]{1,0:T(8,128)S(1)} %get-tuple-element.99.refs_0_), channel_id=1, source_target_pairs={{0,1},{2,3},{4,5},{6,7},{1,0},{3,2},{5,4},{7,6},{8,9},{10,11},{12,... | collective-permute-start | bytes 393224 | tf_op jit(solution)/shard_map/ppermute | solution.py:366
  151.1 1.3 collective-permute-start.43
  152.4 0.9 collective-permute-start.44
  153.2 3.0 %collective-permute-start.40 = (f32[144,128]{1,0:T(8,128)S(1)}, f32[144,128]{1,0:T(8,128)S(1)}, u32[]{:S(2)}, u32[]{:S(2)}) collective-permute-start(f32[144,128]{1,0:T(8,128)S(1)} %get-tuple-element.90), channel_id=1, source_target_pairs={{0,16},{8,24},{16,0},{24,8},{1,17},{9,25},{17,1},{25,9},{2,18},{10... | collective-permute-start | bytes 221192 | tf_op jit(solution)/shard_map/ppermute | solution.py:16
  156.2 3.9 %inner_inverse.2 = f32[128,128]{1,0:T(8,128)S(1)} custom-call(f32[144,128]{1,0:T(8,128)S(1)} %add.67.grams), custom_call_target="tpu_custom_call" | custom-call | flops 400000000 | bytes 139264 | tf_op jit(solution)/shard_map/inner_inverse/pallas_call | solution.py:347
  160.5 6.7 %next_update.1 = (f32[1024,128]{1,0:T(8,128)S(1)}, f32[1024,128]{1,0:T(8,128)S(1)}, f32[1024,128]{1,0:T(8,128)S(1)}, f32[1024,128]{1,0:T(8,128)S(1)}, f32[1024,1...) custom-call(s32[2]{0:T(128)S(1)} %pad_add_fusion.1.parity, ...), custom_call_target="tpu_custom_call" | custom-call | flops 800000000 | bytes 11419656 | tf_op jit(solution)/shard_map/next_update/pallas_call | solution.py:347
  167.3 1.2 collective-permute-done.45
  168.4 3.2 %collective-permute-start.46 = (f32[72,128]{1,0:T(8,128)S(1)}, f32[72,128]{1,0:T(8,128)S(1)}, u32[]{:S(2)}, u32[]{:S(2)}) collective-permute-start(f32[72,128]{1,0:T(8,128)S(1)} %add.69), channel_id=1, source_target_pairs={{0,1},{1,0},{2,3},{3,2},{4,5},{5,4},{6,7},{7,6},{8,9},{9,8},{10,11... | collective-permute-start | bytes 110600 | tf_op jit(solution)/shard_map/ppermute | solution.py:16
  171.7 1.9 collective-permute-done.46
  173.6 1.4 collective-permute-start.47
  175.0 2.5 %collective-permute-done.47 = f32[72,128]{1,0:T(8,128)S(1)} collective-permute-done((f32[72,128]{1,0:T(8,128)S(1)}, f32[72,128]{1,0:T(8,128)S(1)}, u32[]{:S(2)}, u32[]{:S(2)}) %collective-permute-start.47) | collective-permute-done | bytes 36896 | tf_op jit(solution)/shard_map/ppermute | solution.py:16
  177.6 1.5 collective-permute-start.48
  179.1 2.4 %collective-permute-done.48 = f32[72,128]{1,0:T(8,128)S(1)} collective-permute-done((f32[72,128]{1,0:T(8,128)S(1)}, f32[72,128]{1,0:T(8,128)S(1)}, u32[]{:S(2)}, u32[]{:S(2)}) %collective-permute-start.48) | collective-permute-done | bytes 36896 | tf_op jit(solution)/shard_map/ppermute | solution.py:16
  181.5 3.5 %collective-permute-start.49 = (f32[72,128]{1,0:T(8,128)S(1)}, f32[72,128]{1,0:T(8,128)S(1)}, u32[]{:S(2)}, u32[]{:S(2)}) collective-permute-start(f32[72,128]{1,0:T(8,128)S(1)} %add.72), channel_id=1, source_target_pairs={{0,4},{1,5},{2,6},{3,7},{4,0},{5,1},{6,2},{7,3},{8,12},{9,13},{10,... | collective-permute-start | bytes 110600 | tf_op jit(solution)/shard_map/ppermute | solution.py:16
  185.0 1.9 collective-permute-done.49
  186.9 4.2 %inner_inverse.3 = f32[128,128]{1,0:T(8,128)S(1)} custom-call(f32[144,128]{1,0:T(8,128)S(1)} %add.68.grams), custom_call_target="tpu_custom_call" | custom-call | flops 400000000 | bytes 139264 | tf_op jit(solution)/shard_map/inner_inverse/pallas_call | solution.py:347
  191.2 6.5 %last_update.1 = (f32[1024,128]{1,0:T(8,128)}, f32[1024,128]{1,0:T(8,128)}) custom-call(s32[2]{0:T(128)S(1)} %pad_add_fusion.1.parity, f32[72,128]{1,0:T(8,128)S(1)} %add.73.half, f32[72,128]{1,0:T(8,128)S(1)} %collective-permute-done.50.other, f32[128,128]{1,0:T(8,128)S(1)} %inner_inverse.3, f32[128,128]{1,0:T(8,128)S(1)} %get-tuple-element.107.curvature, ...), custom_call_target="tpu_custom_call" | custom-call | flops 800000000 | bytes 4399112 | tf_op jit(solution)/shard_map/last_update/pallas_call | solution.py:347
  (92 shorter events, 18.3 us)
Async XLA Ops:
  0.6 32.0 %copy-start.2 = (bf16[1,1,32,1024]{3,2,1,0:T(8,128)(2,1)S(1)}, bf16[1,1,32,1024]{3,2,1,0:T(8,128)(2,1)}, u32[]{:S(2)}) copy-start(bf16[1,1,32,1024]{3,2,1,0:T(8,128)(2,1)} %param.11) | copy-start | bytes 196612
  0.6 4.7 %collective-permute-start = (s32[32]{0:T(128)}, s32[32]{0:T(128)S(1)}, u32[]{:S(2)}, u32[]{:S(2)}) collective-permute-start(s32[32]{0:T(128)} %bitcast.40), channel_id=1, source_target_pairs={{0,1},{1,0},{2,3},{3,2},{4,5},{5,4},{6,7},{7,6},{8,9},{9,8},{10,11... | collective-permute-start | bytes 392 | tf_op jit(solution)/shard_map/ppermute | solution.py:16
  6.1 34.5 %copy-start = (bf16[1,1,1024,1024]{3,2,1,0:T(8,128)(2,1)S(1)}, bf16[1,1,1024,1024]{3,2,1,0:T(8,128)(2,1)}, u32[]{:S(2)}) copy-start(bf16[1,1,1024,1024]{3,2,1,0:T(8,128)(2,1)} %param.9) | copy-start | bytes 6291460
  6.1 3.6 %collective-permute-start.1 = (s32[64]{0:T(128)S(1)}, s32[64]{0:T(128)S(1)}, u32[]{:S(2)}, u32[]{:S(2)}) collective-permute-start(s32[64]{0:T(128)S(1)} %pad_add_fusion.2), channel_id=1, source_target_pairs={{0,2},{1,3},{2,0},{3,1},{4,6},{5,7},{6,4},{7,5},{8,10},{9,11},{10,... | collective-permute-start | bytes 776 | tf_op jit(solution)/shard_map/ppermute | solution.py:16
  10.4 11.0 %collective-permute-start.2 = (s32[128]{0:T(128)S(1)}, s32[128]{0:T(128)S(1)}, u32[]{:S(2)}, u32[]{:S(2)}) collective-permute-start(s32[128]{0:T(128)S(1)} %pad_add_fusion.3), channel_id=1, source_target_pairs={{0,4},{1,5},{2,6},{3,7},{4,0},{5,1},{6,2},{7,3},{8,12},{9,13},{10,... | collective-permute-start | bytes 1544 | tf_op jit(solution)/shard_map/ppermute | solution.py:16
  13.4 19.2 %collective-permute-start.9 = (bf16[256,128]{1,0:T(8,128)(2,1)S(1)}, bf16[256,128]{1,0:T(8,128)(2,1)S(1)}, u32[]{:S(2)}, u32[]{:S(2)}) collective-permute-start(bf16[256,128]{1,0:T(8,128)(2,1)S(1)} %get-tuple-element.116.refs_3_), channel_id=1, source_target_pairs={{8,16},{16,8},{9,17},{17,9},{10,18},{18,10},{11,19},{19,11},{12,20... | collective-permute-start | bytes 196616 | tf_op jit(solution)/shard_map/ppermute | solution.py:366
  14.1 18.6 %collective-permute-start.7 = (bf16[256,128]{1,0:T(8,128)(2,1)S(1)}, bf16[256,128]{1,0:T(8,128)(2,1)S(1)}, u32[]{:S(2)}, u32[]{:S(2)}) collective-permute-start(bf16[256,128]{1,0:T(8,128)(2,1)S(1)} %get-tuple-element.117.refs_1_), channel_id=1, source_target_pairs={{1,2},{3,4},{5,6},{2,1},{4,3},{6,5},{9,10},{11,12},{13,14},{10,9},... | collective-permute-start | bytes 196616 | tf_op jit(solution)/shard_map/ppermute | solution.py:366
  14.8 17.9 %collective-permute-start.6 = (bf16[256,128]{1,0:T(8,128)(2,1)S(1)}, bf16[256,128]{1,0:T(8,128)(2,1)S(1)}, u32[]{:S(2)}, u32[]{:S(2)}) collective-permute-start(bf16[256,128]{1,0:T(8,128)(2,1)S(1)} %get-tuple-element.118.refs_0_), channel_id=1, source_target_pairs={{0,1},{2,3},{4,5},{6,7},{1,0},{3,2},{5,4},{7,6},{8,9},{10,11},{12,... | collective-permute-start | bytes 196616 | tf_op jit(solution)/shard_map/ppermute | solution.py:366
  19.1 13.6 %collective-permute-start.8 = (bf16[256,128]{1,0:T(8,128)(2,1)S(1)}, bf16[256,128]{1,0:T(8,128)(2,1)S(1)}, u32[]{:S(2)}, u32[]{:S(2)}) collective-permute-start(bf16[256,128]{1,0:T(8,128)(2,1)S(1)} %get-tuple-element.119.refs_2_), channel_id=1, source_target_pairs={{0,8},{16,24},{8,0},{24,16},{1,9},{17,25},{9,1},{25,17},{2,10},{18... | collective-permute-start | bytes 196616 | tf_op jit(solution)/shard_map/ppermute | solution.py:366
  22.1 1.0 copy-start.3
  23.8 6.2 %collective-permute-start.3 = (bf16[4,32,256]{2,1,0:T(8,128)(2,1)S(1)}, bf16[4,32,256]{2,1,0:T(8,128)(2,1)S(1)}, u32[]{:S(2)}, u32[]{:S(2)}) collective-permute-start(bf16[4,32,256]{2,1,0:T(8,128)(2,1)S(1)} %slice.25), channel_id=1, source_target_pairs={{0,4},{1,5},{2,6},{3,7},{4,0},{5,1},{6,2},{7,3},{8,12},{9,13},{10,... | collective-permute-start | bytes 196616 | tf_op jit(solution)/shard_map/ppermute | solution.py:16
  29.9 9.6 %collective-permute-start.4 = (bf16[2,32,256]{2,1,0:T(8,128)(2,1)S(1)}, bf16[2,32,256]{2,1,0:T(8,128)(2,1)S(1)}, u32[]{:S(2)}, u32[]{:S(2)}) collective-permute-start(bf16[2,32,256]{2,1,0:T(8,128)(2,1)S(1)} %slice.27), channel_id=1, source_target_pairs={{0,2},{1,3},{2,0},{3,1},{4,6},{5,7},{6,4},{7,5},{8,10},{9,11},{10,... | collective-permute-start | bytes 98312 | tf_op jit(solution)/shard_map/ppermute | solution.py:16
  30.0 0.7 copy-start.4
  30.7 0.7 copy-start.5
  33.8 3.8 %collective-permute-start.10 = (f32[32,128]{1,0:T(8,128)S(1)}, f32[32,128]{1,0:T(8,128)S(1)}, u32[]{:S(2)}, u32[]{:S(2)}) collective-permute-start(f32[32,128]{1,0:T(8,128)S(1)} %get-tuple-element.62.own), channel_id=1, source_target_pairs={{0,1},{1,0},{2,3},{3,2},{4,5},{5,4},{6,7},{7,6},{8,9},{9,8},{10,11... | collective-permute-start | bytes 49160 | tf_op jit(solution)/shard_map/ppermute | solution.py:16
  37.6 3.9 %collective-permute-start.11 = (f32[64,128]{1,0:T(8,128)S(1)}, f32[64,128]{1,0:T(8,128)S(1)}, u32[]{:S(2)}, u32[]{:S(2)}) collective-permute-start(f32[64,128]{1,0:T(8,128)S(1)} %fold.6.own), channel_id=1, source_target_pairs={{0,2},{1,3},{2,0},{3,1},{4,6},{5,7},{6,4},{7,5},{8,10},{9,11},{10,... | collective-permute-start | bytes 98312 | tf_op jit(solution)/shard_map/ppermute | solution.py:16
  39.6 3.8 %collective-permute-start.5 = (bf16[1,32,256]{2,1,0:T(8,128)(2,1)S(1)}, bf16[1,32,256]{2,1,0:T(8,128)(2,1)S(1)}, u32[]{:S(2)}, u32[]{:S(2)}) collective-permute-start(bf16[1,32,256]{2,1,0:T(8,128)(2,1)S(1)} %slice.29), channel_id=1, source_target_pairs={{0,1},{1,0},{2,3},{3,2},{4,5},{5,4},{6,7},{7,6},{8,9},{9,8},{10,11... | collective-permute-start | bytes 49160 | tf_op jit(solution)/shard_map/ppermute | solution.py:16
  40.5 12.2 %copy-start.1 = (bf16[1,1,1024,1024]{3,2,1,0:T(8,128)(2,1)S(1)}, bf16[1,1,1024,1024]{3,2,1,0:T(8,128)(2,1)}, u32[]{:S(2)}) copy-start(bf16[1,1,1024,1024]{3,2,1,0:T(8,128)(2,1)} %param.8) | copy-start | bytes 6291460
  41.5 5.2 %collective-permute-start.12 = (f32[128,128]{1,0:T(8,128)S(1)}, f32[128,128]{1,0:T(8,128)S(1)}, u32[]{:S(2)}, u32[]{:S(2)}) collective-permute-start(f32[128,128]{1,0:T(8,128)S(1)} %fold.7.own), channel_id=1, source_target_pairs={{0,4},{1,5},{2,6},{3,7},{4,0},{5,1},{6,2},{7,3},{8,12},{9,13},{10,... | collective-permute-start | bytes 196616 | tf_op jit(solution)/shard_map/ppermute | solution.py:16
  47.7 5.0 %collective-permute-start.13 = (f32[256,128]{1,0:T(8,128)S(1)}, f32[256,128]{1,0:T(8,128)S(1)}, u32[]{:S(2)}, u32[]{:S(2)}) collective-permute-start(f32[256,128]{1,0:T(8,128)S(1)} %get-tuple-element.63.refs_0_), channel_id=1, source_target_pairs={{0,1},{2,3},{4,5},{6,7},{1,0},{3,2},{5,4},{7,6},{8,9},{10,11},{12,... | collective-permute-start | bytes 393224 | tf_op jit(solution)/shard_map/ppermute | solution.py:366
  48.8 3.9 %collective-permute-start.14 = (f32[256,128]{1,0:T(8,128)S(1)}, f32[256,128]{1,0:T(8,128)S(1)}, u32[]{:S(2)}, u32[]{:S(2)}) collective-permute-start(f32[256,128]{1,0:T(8,128)S(1)} %get-tuple-element.64.refs_1_), channel_id=1, source_target_pairs={{1,2},{3,4},{5,6},{2,1},{4,3},{6,5},{9,10},{11,12},{13,14},{10,9},... | collective-permute-start | bytes 393224 | tf_op jit(solution)/shard_map/ppermute | solution.py:366
  49.5 3.3 %collective-permute-start.15 = (f32[256,128]{1,0:T(8,128)S(1)}, f32[256,128]{1,0:T(8,128)S(1)}, u32[]{:S(2)}, u32[]{:S(2)}) collective-permute-start(f32[256,128]{1,0:T(8,128)S(1)} %get-tuple-element.65.refs_2_), channel_id=1, source_target_pairs={{0,8},{16,24},{8,0},{24,16},{1,9},{17,25},{9,1},{25,17},{2,10},{18... | collective-permute-start | bytes 393224 | tf_op jit(solution)/shard_map/ppermute | solution.py:366
  49.5 3.2 %collective-permute-start.16 = (f32[256,128]{1,0:T(8,128)S(1)}, f32[256,128]{1,0:T(8,128)S(1)}, u32[]{:S(2)}, u32[]{:S(2)}) collective-permute-start(f32[256,128]{1,0:T(8,128)S(1)} %get-tuple-element.66.refs_3_), channel_id=1, source_target_pairs={{8,16},{16,8},{9,17},{17,9},{10,18},{18,10},{11,19},{19,11},{12,20... | collective-permute-start | bytes 393224 | tf_op jit(solution)/shard_map/ppermute | solution.py:366
  54.3 9.3 %collective-permute-start.17 = (f32[256,128]{1,0:T(8,128)S(1)}, f32[256,128]{1,0:T(8,128)S(1)}, u32[]{:S(2)}, u32[]{:S(2)}) collective-permute-start(f32[256,128]{1,0:T(8,128)S(1)} %get-tuple-element.68.refs_0_), channel_id=1, source_target_pairs={{0,1},{2,3},{4,5},{6,7},{1,0},{3,2},{5,4},{7,6},{8,9},{10,11},{12,... | collective-permute-start | bytes 393224 | tf_op jit(solution)/shard_map/ppermute | solution.py:366
  59.2 4.4 %collective-permute-start.18 = (f32[256,128]{1,0:T(8,128)S(1)}, f32[256,128]{1,0:T(8,128)S(1)}, u32[]{:S(2)}, u32[]{:S(2)}) collective-permute-start(f32[256,128]{1,0:T(8,128)S(1)} %get-tuple-element.69.refs_1_), channel_id=1, source_target_pairs={{1,2},{3,4},{5,6},{2,1},{4,3},{6,5},{9,10},{11,12},{13,14},{10,9},... | collective-permute-start | bytes 393224 | tf_op jit(solution)/shard_map/ppermute | solution.py:366
  59.8 4.1 %collective-permute-start.19 = (f32[256,128]{1,0:T(8,128)S(1)}, f32[256,128]{1,0:T(8,128)S(1)}, u32[]{:S(2)}, u32[]{:S(2)}) collective-permute-start(f32[256,128]{1,0:T(8,128)S(1)} %get-tuple-element.70.refs_2_), channel_id=1, source_target_pairs={{0,8},{16,24},{8,0},{24,16},{1,9},{17,25},{9,1},{25,17},{2,10},{18... | collective-permute-start | bytes 393224 | tf_op jit(solution)/shard_map/ppermute | solution.py:366
  62.9 1.0 collective-permute-start.20
  65.4 6.9 %collective-permute-start.21 = (f32[176,128]{1,0:T(8,128)S(1)}, f32[176,128]{1,0:T(8,128)S(1)}, u32[]{:S(2)}, u32[]{:S(2)}) collective-permute-start(f32[176,128]{1,0:T(8,128)S(1)} %get-tuple-element.73.own), channel_id=1, source_target_pairs={{0,1},{1,0},{2,3},{3,2},{4,5},{5,4},{6,7},{7,6},{8,9},{9,8},{10,11... | collective-permute-start | bytes 270344 | tf_op jit(solution)/shard_map/ppermute | solution.py:16
  72.3 7.8 %collective-permute-start.22 = (f32[208,128]{1,0:T(8,128)S(1)}, f32[208,128]{1,0:T(8,128)S(1)}, u32[]{:S(2)}, u32[]{:S(2)}) collective-permute-start(f32[208,128]{1,0:T(8,128)S(1)} %fold.8.own), channel_id=1, source_target_pairs={{0,2},{1,3},{2,0},{3,1},{4,6},{5,7},{6,4},{7,5},{8,10},{9,11},{10,... | collective-permute-start | bytes 319496 | tf_op jit(solution)/shard_map/ppermute | solution.py:16
  80.1 9.6 %collective-permute-start.23 = (f32[272,128]{1,0:T(8,128)S(1)}, f32[272,128]{1,0:T(8,128)S(1)}, u32[]{:S(2)}, u32[]{:S(2)}) collective-permute-start(f32[272,128]{1,0:T(8,128)S(1)} %fold.9.own), channel_id=1, source_target_pairs={{0,4},{1,5},{2,6},{3,7},{4,0},{5,1},{6,2},{7,3},{8,12},{9,13},{10,... | collective-permute-start | bytes 417800 | tf_op jit(solution)/shard_map/ppermute | solution.py:16
  90.8 6.0 %collective-permute-start.26 = (f32[400,128]{1,0:T(8,128)S(1)}, f32[400,128]{1,0:T(8,128)S(1)}, u32[]{:S(2)}, u32[]{:S(2)}) collective-permute-start(f32[400,128]{1,0:T(8,128)S(1)} %get-tuple-element.76.refs_2_), channel_id=1, source_target_pairs={{0,8},{16,24},{8,0},{24,16},{1,9},{17,25},{9,1},{25,17},{2,10},{18... | collective-permute-start | bytes 614408 | tf_op jit(solution)/shard_map/ppermute | solution.py:366
  90.8 5.9 %collective-permute-start.24 = (f32[256,128]{1,0:T(8,128)S(1)}, f32[256,128]{1,0:T(8,128)S(1)}, u32[]{:S(2)}, u32[]{:S(2)}) collective-permute-start(f32[256,128]{1,0:T(8,128)S(1)} %get-tuple-element.74.refs_0_), channel_id=1, source_target_pairs={{0,1},{2,3},{4,5},{6,7},{1,0},{3,2},{5,4},{7,6},{8,9},{10,11},{12,... | collective-permute-start | bytes 393224 | tf_op jit(solution)/shard_map/ppermute | solution.py:366
  91.4 5.3 %collective-permute-start.25 = (f32[256,128]{1,0:T(8,128)S(1)}, f32[256,128]{1,0:T(8,128)S(1)}, u32[]{:S(2)}, u32[]{:S(2)}) collective-permute-start(f32[256,128]{1,0:T(8,128)S(1)} %get-tuple-element.75.refs_1_), channel_id=1, source_target_pairs={{1,2},{3,4},{5,6},{2,1},{4,3},{6,5},{9,10},{11,12},{13,14},{10,9},... | collective-permute-start | bytes 393224 | tf_op jit(solution)/shard_map/ppermute | solution.py:366
  92.1 4.7 %collective-permute-start.27 = (f32[256,128]{1,0:T(8,128)S(1)}, f32[256,128]{1,0:T(8,128)S(1)}, u32[]{:S(2)}, u32[]{:S(2)}) collective-permute-start(f32[256,128]{1,0:T(8,128)S(1)} %get-tuple-element.77.refs_3_), channel_id=1, source_target_pairs={{8,16},{16,8},{9,17},{17,9},{10,18},{18,10},{11,19},{19,11},{12,20... | collective-permute-start | bytes 393224 | tf_op jit(solution)/shard_map/ppermute | solution.py:366
  98.4 13.9 %collective-permute-start.29 = (f32[256,128]{1,0:T(8,128)S(1)}, f32[256,128]{1,0:T(8,128)S(1)}, u32[]{:S(2)}, u32[]{:S(2)}) collective-permute-start(f32[256,128]{1,0:T(8,128)S(1)} %get-tuple-element.80.refs_0_), channel_id=1, source_target_pairs={{0,1},{2,3},{4,5},{6,7},{1,0},{3,2},{5,4},{7,6},{8,9},{10,11},{12,... | collective-permute-start | bytes 393224 | tf_op jit(solution)/shard_map/ppermute | solution.py:366
  102.9 9.3 %collective-permute-start.30 = (f32[256,128]{1,0:T(8,128)S(1)}, f32[256,128]{1,0:T(8,128)S(1)}, u32[]{:S(2)}, u32[]{:S(2)}) collective-permute-start(f32[256,128]{1,0:T(8,128)S(1)} %get-tuple-element.81.refs_1_), channel_id=1, source_target_pairs={{1,2},{3,4},{5,6},{2,1},{4,3},{6,5},{9,10},{11,12},{13,14},{10,9},... | collective-permute-start | bytes 393224 | tf_op jit(solution)/shard_map/ppermute | solution.py:366
  103.6 8.6 %collective-permute-start.31 = (f32[256,128]{1,0:T(8,128)S(1)}, f32[256,128]{1,0:T(8,128)S(1)}, u32[]{:S(2)}, u32[]{:S(2)}) collective-permute-start(f32[256,128]{1,0:T(8,128)S(1)} %get-tuple-element.82.refs_2_), channel_id=1, source_target_pairs={{0,8},{16,24},{8,0},{24,16},{1,9},{17,25},{9,1},{25,17},{2,10},{18... | collective-permute-start | bytes 393224 | tf_op jit(solution)/shard_map/ppermute | solution.py:366
  103.7 8.6 %collective-permute-start.32 = (f32[256,128]{1,0:T(8,128)S(1)}, f32[256,128]{1,0:T(8,128)S(1)}, u32[]{:S(2)}, u32[]{:S(2)}) collective-permute-start(f32[256,128]{1,0:T(8,128)S(1)} %get-tuple-element.83.refs_3_), channel_id=1, source_target_pairs={{8,16},{16,8},{9,17},{17,9},{10,18},{18,10},{11,19},{19,11},{12,20... | collective-permute-start | bytes 393224 | tf_op jit(solution)/shard_map/ppermute | solution.py:366
  104.5 7.7 %collective-permute-start.28 = (f32[144,128]{1,0:T(8,128)S(1)}, f32[144,128]{1,0:T(8,128)S(1)}, u32[]{:S(2)}, u32[]{:S(2)}) collective-permute-start(f32[144,128]{1,0:T(8,128)S(1)} %get-tuple-element.78), channel_id=1, source_target_pairs={{0,16},{8,24},{16,0},{24,8},{1,17},{9,25},{17,1},{25,9},{2,18},{10... | collective-permute-start | bytes 221192 | tf_op jit(solution)/shard_map/ppermute | solution.py:16
  119.0 5.7 %collective-permute-start.33 = (f32[176,128]{1,0:T(8,128)S(1)}, f32[176,128]{1,0:T(8,128)S(1)}, u32[]{:S(2)}, u32[]{:S(2)}) collective-permute-start(f32[176,128]{1,0:T(8,128)S(1)} %get-tuple-element.85.own), channel_id=1, source_target_pairs={{0,1},{1,0},{2,3},{3,2},{4,5},{5,4},{6,7},{7,6},{8,9},{9,8},{10,11... | collective-permute-start | bytes 270344 | tf_op jit(solution)/shard_map/ppermute | solution.py:16
  124.7 4.8 %collective-permute-start.34 = (f32[208,128]{1,0:T(8,128)S(1)}, f32[208,128]{1,0:T(8,128)S(1)}, u32[]{:S(2)}, u32[]{:S(2)}) collective-permute-start(f32[208,128]{1,0:T(8,128)S(1)} %fold.10.own), channel_id=1, source_target_pairs={{0,2},{1,3},{2,0},{3,1},{4,6},{5,7},{6,4},{7,5},{8,10},{9,11},{10,... | collective-permute-start | bytes 319496 | tf_op jit(solution)/shard_map/ppermute | solution.py:16
  129.5 7.8 %collective-permute-start.35 = (f32[272,128]{1,0:T(8,128)S(1)}, f32[272,128]{1,0:T(8,128)S(1)}, u32[]{:S(2)}, u32[]{:S(2)}) collective-permute-start(f32[272,128]{1,0:T(8,128)S(1)} %fold.11.own), channel_id=1, source_target_pairs={{0,4},{1,5},{2,6},{3,7},{4,0},{5,1},{6,2},{7,3},{8,12},{9,13},{10,... | collective-permute-start | bytes 417800 | tf_op jit(solution)/shard_map/ppermute | solution.py:16
  138.3 6.0 %collective-permute-start.38 = (f32[400,128]{1,0:T(8,128)S(1)}, f32[400,128]{1,0:T(8,128)S(1)}, u32[]{:S(2)}, u32[]{:S(2)}) collective-permute-start(f32[400,128]{1,0:T(8,128)S(1)} %get-tuple-element.88.refs_2_), channel_id=1, source_target_pairs={{0,8},{16,24},{8,0},{24,16},{1,9},{17,25},{9,1},{25,17},{2,10},{18... | collective-permute-start | bytes 614408 | tf_op jit(solution)/shard_map/ppermute | solution.py:366
  138.3 5.9 %collective-permute-start.36 = (f32[256,128]{1,0:T(8,128)S(1)}, f32[256,128]{1,0:T(8,128)S(1)}, u32[]{:S(2)}, u32[]{:S(2)}) collective-permute-start(f32[256,128]{1,0:T(8,128)S(1)} %get-tuple-element.86.refs_0_), channel_id=1, source_target_pairs={{0,1},{2,3},{4,5},{6,7},{1,0},{3,2},{5,4},{7,6},{8,9},{10,11},{12,... | collective-permute-start | bytes 393224 | tf_op jit(solution)/shard_map/ppermute | solution.py:366
  138.7 5.6 %collective-permute-start.37 = (f32[256,128]{1,0:T(8,128)S(1)}, f32[256,128]{1,0:T(8,128)S(1)}, u32[]{:S(2)}, u32[]{:S(2)}) collective-permute-start(f32[256,128]{1,0:T(8,128)S(1)} %get-tuple-element.87.refs_1_), channel_id=1, source_target_pairs={{1,2},{3,4},{5,6},{2,1},{4,3},{6,5},{9,10},{11,12},{13,14},{10,9},... | collective-permute-start | bytes 393224 | tf_op jit(solution)/shard_map/ppermute | solution.py:366
  139.3 4.9 %collective-permute-start.39 = (f32[256,128]{1,0:T(8,128)S(1)}, f32[256,128]{1,0:T(8,128)S(1)}, u32[]{:S(2)}, u32[]{:S(2)}) collective-permute-start(f32[256,128]{1,0:T(8,128)S(1)} %get-tuple-element.89.refs_3_), channel_id=1, source_target_pairs={{8,16},{16,8},{9,17},{17,9},{10,18},{18,10},{11,19},{19,11},{12,20... | collective-permute-start | bytes 393224 | tf_op jit(solution)/shard_map/ppermute | solution.py:366
  145.9 14.6 %collective-permute-start.41 = (f32[256,128]{1,0:T(8,128)S(1)}, f32[256,128]{1,0:T(8,128)S(1)}, u32[]{:S(2)}, u32[]{:S(2)}) collective-permute-start(f32[256,128]{1,0:T(8,128)S(1)} %get-tuple-element.99.refs_0_), channel_id=1, source_target_pairs={{0,1},{2,3},{4,5},{6,7},{1,0},{3,2},{5,4},{7,6},{8,9},{10,11},{12,... | collective-permute-start | bytes 393224 | tf_op jit(solution)/shard_map/ppermute | solution.py:366
  150.4 10.0 %collective-permute-start.42 = (f32[256,128]{1,0:T(8,128)S(1)}, f32[256,128]{1,0:T(8,128)S(1)}, u32[]{:S(2)}, u32[]{:S(2)}) collective-permute-start(f32[256,128]{1,0:T(8,128)S(1)} %get-tuple-element.100.refs_1_), channel_id=1, source_target_pairs={{1,2},{3,4},{5,6},{2,1},{4,3},{6,5},{9,10},{11,12},{13,14},{10,9},... | collective-permute-start | bytes 393224 | tf_op jit(solution)/shard_map/ppermute | solution.py:366
  151.1 9.4 %collective-permute-start.43 = (f32[256,128]{1,0:T(8,128)S(1)}, f32[256,128]{1,0:T(8,128)S(1)}, u32[]{:S(2)}, u32[]{:S(2)}) collective-permute-start(f32[256,128]{1,0:T(8,128)S(1)} %get-tuple-element.101.refs_2_), channel_id=1, source_target_pairs={{0,8},{16,24},{8,0},{24,16},{1,9},{17,25},{9,1},{25,17},{2,10},{18... | collective-permute-start | bytes 393224 | tf_op jit(solution)/shard_map/ppermute | solution.py:366
  152.4 8.1 %collective-permute-start.44 = (f32[256,128]{1,0:T(8,128)S(1)}, f32[256,128]{1,0:T(8,128)S(1)}, u32[]{:S(2)}, u32[]{:S(2)}) collective-permute-start(f32[256,128]{1,0:T(8,128)S(1)} %get-tuple-element.102.refs_3_), channel_id=1, source_target_pairs={{8,16},{16,8},{9,17},{17,9},{10,18},{18,10},{11,19},{19,11},{12,20... | collective-permute-start | bytes 393224 | tf_op jit(solution)/shard_map/ppermute | solution.py:366
  153.2 7.2 %collective-permute-start.40 = (f32[144,128]{1,0:T(8,128)S(1)}, f32[144,128]{1,0:T(8,128)S(1)}, u32[]{:S(2)}, u32[]{:S(2)}) collective-permute-start(f32[144,128]{1,0:T(8,128)S(1)} %get-tuple-element.90), channel_id=1, source_target_pairs={{0,16},{8,24},{16,0},{24,8},{1,17},{9,25},{17,1},{25,9},{2,18},{10... | collective-permute-start | bytes 221192 | tf_op jit(solution)/shard_map/ppermute | solution.py:16
  167.1 1.3 collective-permute-start.45
  168.4 5.2 %collective-permute-start.46 = (f32[72,128]{1,0:T(8,128)S(1)}, f32[72,128]{1,0:T(8,128)S(1)}, u32[]{:S(2)}, u32[]{:S(2)}) collective-permute-start(f32[72,128]{1,0:T(8,128)S(1)} %add.69), channel_id=1, source_target_pairs={{0,1},{1,0},{2,3},{3,2},{4,5},{5,4},{6,7},{7,6},{8,9},{9,8},{10,11... | collective-permute-start | bytes 110600 | tf_op jit(solution)/shard_map/ppermute | solution.py:16
  173.6 4.0 %collective-permute-start.47 = (f32[72,128]{1,0:T(8,128)S(1)}, f32[72,128]{1,0:T(8,128)S(1)}, u32[]{:S(2)}, u32[]{:S(2)}) collective-permute-start(f32[72,128]{1,0:T(8,128)S(1)} %add.70), channel_id=1, source_target_pairs={{0,16},{8,24},{16,0},{24,8},{1,17},{9,25},{17,1},{25,9},{2,18},{10... | collective-permute-start | bytes 110600 | tf_op jit(solution)/shard_map/ppermute | solution.py:16
  177.6 4.0 %collective-permute-start.48 = (f32[72,128]{1,0:T(8,128)S(1)}, f32[72,128]{1,0:T(8,128)S(1)}, u32[]{:S(2)}, u32[]{:S(2)}) collective-permute-start(f32[72,128]{1,0:T(8,128)S(1)} %add.71), channel_id=1, source_target_pairs={{0,2},{1,3},{2,0},{3,1},{4,6},{5,7},{6,4},{7,5},{8,10},{9,11},{10,... | collective-permute-start | bytes 110600 | tf_op jit(solution)/shard_map/ppermute | solution.py:16
  181.5 5.4 %collective-permute-start.49 = (f32[72,128]{1,0:T(8,128)S(1)}, f32[72,128]{1,0:T(8,128)S(1)}, u32[]{:S(2)}, u32[]{:S(2)}) collective-permute-start(f32[72,128]{1,0:T(8,128)S(1)} %add.72), channel_id=1, source_target_pairs={{0,4},{1,5},{2,6},{3,7},{4,0},{5,1},{6,2},{7,3},{8,12},{9,13},{10,... | collective-permute-start | bytes 110600 | tf_op jit(solution)/shard_map/ppermute | solution.py:16
  186.9 4.2 %collective-permute-start.50 = (f32[72,128]{1,0:T(8,128)S(1)}, f32[72,128]{1,0:T(8,128)S(1)}, u32[]{:S(2)}, u32[]{:S(2)}) collective-permute-start(f32[72,128]{1,0:T(8,128)S(1)} %add.73.half), channel_id=1, source_target_pairs={{0,8},{8,0},{16,24},{24,16},{1,9},{9,1},{17,25},{25,17},{2,10},{10... | collective-permute-start | bytes 110600 | tf_op jit(solution)/shard_map/ppermute | solution.py:16
where the time goes:
time: 198 us
  starting transfers between devices  84.4 us (43%)
  waiting for transfers between devices  64 us (32%)
  Pallas kernels  42.5 us (21%)
  local copies, waits for them, and re-layouts  3.28 us (2%)
  other arithmetic  2.34 us (1%)
    ppermute x23, waiting for transfers between devices, swap(): lax.ppermute(x, axis, [(i, i ^ bit) for i in range(lax.axis_size(axis))])  52.9 us
    ppermute x23, starting transfers between devices, swap(): lax.ppermute(x, axis, [(i, i ^ bit) for i in range(lax.axis_size(axis))])  47.5 us
    pallas_call x24, Pallas kernels, call(): pl.pallas_call(kernel, out_shape=shapes, in_specs=[SMEM if a.ndim == 1 el...  42.5 us
    ppermute x28, starting transfers between devices, exchange(): lax.ppermute(slot, axis, pairs(axis, first))  36.9 us
    ppermute x28, waiting for transfers between devices, exchange(): lax.ppermute(slot, axis, pairs(axis, first))  11.1 us
  transfers between devices with their start and end apart: 51, of which 24 were waited for; matrix products, arithmetic and copies ran while one was open for 1% of the time, Pallas kernels for 7%

commit v1 on v0

--- a/solution.py
+++ b/solution.py
@@ -23,13 +23,16 @@
     return [1 << b for b in range(count.bit_length() - 1)]
 
 
-def total(kept, sent):
+def total(kept, sent, ride):
     half = kept + swap(sent, "group", 1)
     rest = [("group", bit) for bit in bits_of("group")[1:]]
     subs = [("sub", bit) for bit in bits_of("sub")]
-    for axis, bit in subs[:1] + rest + subs[1:]:
-        half = half + swap(half, axis, bit)
-    return half, swap(half, "group", 1)
+    for number, (axis, bit) in enumerate(subs[:1] + rest + subs[1:]):
+        arrived = swap(half, axis, bit)
+        if number == 1:
+            arrived, ride = lax.optimization_barrier((arrived, ride))
+        half = half + arrived
+    return half, swap(half, "group", 1), ride
 
 
 def gather_sub(x):
@@ -152,7 +155,7 @@
 
 
 def assemble_into(parity, tables, slots, received, out):
-    zone = slots[0].shape[0]
+    zone = tables.shape[1]
     for slot in range(4):
         start = pl.multiple_of(zone_of(parity, slot) * zone, zone)
         value = slots[slot][:zone].astype(jnp.float32) + times(tables[slot], received[slot][:zone])
@@ -160,7 +163,7 @@
 
 
 def slots_from(parity, block, slots):
-    zone = slots[0].shape[0]
+    zone = slots[3].shape[0]
     for slot in range(4):
         pair = 2 * (slot // 2)
         swapped = parity[slot // 2] == (1 if slot % 2 == 0 else 0)
@@ -234,17 +237,62 @@
     carried[: n + TAIL] = packed(local_gram(weighted, r[...]), local_gram(weighted, block[...]))
 
 
-def local_kernel(weight, matrix, block, out):
-    out[...] = times(matrix[...], weight[...] * block[...])
-
-
-def finish_kernel(grams, parity, weight, basis, chosen, local, own, received, *slots):
+def send_kernel(parity, rhs, basis, *slots):
+    zone, columns = slots[3].shape
+    slots_from(parity, rhs[...], slots)
+    modes = basis.shape[0]
+    for slot in range(2):
+        for part in range(zone // columns):
+            at = part * columns
+            low, high = basis[:, at : at + columns], basis[:, zone + at : zone + at + columns]
+            chosen = jnp.where(parity[0] == slot, low, high)
+            slots[slot][zone + part * modes : zone + (part + 1) * modes] = chosen
+
+
+def neighbour_kernel(shift, tables, chosen, first, second, first_zone, second_zone, rows, columns):
+    modes, total_modes = chosen.shape
+    zone, width = tables.shape[1], first_zone.shape[1]
+    source = lax.broadcasted_iota(jnp.int32, (total_modes, total_modes), 0)
+    target = lax.broadcasted_iota(jnp.int32, (total_modes, total_modes), 1)
+    rows[:modes] = chosen[...]
+    for slot, (theirs, below) in enumerate(((first, first_zone), (second, second_zone))):
+        order = (source == (target ^ shift[slot])).astype(jnp.float32).astype(jnp.bfloat16)
+        ordered = jnp.dot(theirs[...], order, preferred_element_type=jnp.float32)
+        rows[(slot + 1) * modes : (slot + 2) * modes] = ordered.astype(jnp.bfloat16)
+        basis = jnp.concatenate(
+            [
+                below[zone + part * modes : zone + (part + 1) * modes]
+                for part in range(zone // width)
+            ],
+            axis=1,
+        )
+        columns[slot] = lax.dot_general(
+            basis, tables[slot], (((1,), (1,)), ((), ())), preferred_element_type=jnp.float32
+        ).astype(jnp.bfloat16)
+
+
+def local_kernel(parity, weight, matrix, block, out, *early):
+    zone = early[0].shape[0]
+    out[...] = weight[...] * times(matrix[...], weight[...] * block[...])
+    low, high = out[:zone], out[zone : 2 * zone]
+    early[0][...] = jnp.where(parity[0] == 0, low, high)
+    early[1][...] = jnp.where(parity[0] == 0, high, low)
+
+
+def finish_kernel(
+    grams, parity, weight, basis, chosen, near, local, own, received, *slots
+):
+    modes, zone = basis.shape[0], slots[0].shape[0]
     pieces = jnp.concatenate([own[grams:], received[grams:]], axis=0)
     picked = times(chosen[...], pieces)
-    smoothed = weight[...] * (local[...] + times(basis[...], picked, contracting=0))
+    smoothed = local[...] + weight[...] * times(basis[...], picked[:modes], contracting=0)
     slots_from(parity, smoothed, slots)
+    for slot in range(2):
+        start = pl.multiple_of(zone_of(parity, slot) * zone, zone)
+        theirs = times(near[slot], picked[(slot + 1) * modes : (slot + 2) * modes], contracting=0)
+        slots[slot][...] = slots[slot][...] + weight[pl.ds(start, zone)] * theirs
     if grams:
-        slots[2][slots[0].shape[0] :] = own[:grams] + received[:grams]
+        slots[2][zone:] = own[:grams] + received[:grams]
 
 
 def operator_kernel(parity, tables, matrix, *refs):
@@ -361,12 +409,11 @@
     return [(i, i + 1) for i in low] + [(i + 1, i) for i in low]
 
 
-def exchange(slots):
+def exchange(slots, first=0):
+    patterns = (("sub", 0), ("sub", 1), ("group", 0), ("group", 1))
     return [
-        lax.ppermute(slot, axis, pairs(axis, first))
-        for slot, (axis, first) in zip(
-            slots, (("sub", 0), ("sub", 1), ("group", 0), ("group", 1))
-        )
+        lax.ppermute(slot, axis, pairs(axis, low))
+        for slot, (axis, low) in zip(slots, patterns[first:])
     ]
 
 
@@ -389,10 +436,17 @@
     solve_flops = 400_000_000
     product_flops = 4 * rows * rows * columns
 
-    def rhs_zone(slot):
-        return lax.dynamic_slice_in_dim(rhs, zone_of(parity, slot) * zone, zone, axis=0)
-
-    rhs_slots = [rhs_zone(slot) for slot in range(4)]
+    low_part = ((zone, columns), jnp.bfloat16)
+    long_part = ((zone + modes * (zone // columns), columns), jnp.bfloat16)
+    rhs_slots = call(
+        send_kernel,
+        "first_zones",
+        rows * columns,
+        [long_part, long_part, low_part, low_part],
+        parity,
+        rhs,
+        basis,
+    )
     received = exchange(rhs_slots)
     tables, weight = call(
         tables_kernel,
@@ -417,22 +471,46 @@
     for bit in reversed(bits_of("sub")):
         chosen = chosen[:bit] + swap(chosen[bit:], "sub", bit)
     chosen = chosen[0]
-
-    def precondition(vector, carried):
+    me = lax.axis_index("sub")
+    across = jnp.stack([me ^ (me ^ 1), me ^ (((me + 1) ^ 1) - 1)]) & (subs - 1)
+    chosen, near = call(
+        neighbour_kernel,
+        "neighbours",
+        product_flops // 16,
+        [((3 * modes, subs * modes), jnp.bfloat16), ((2, modes, zone), jnp.bfloat16)],
+        (across * modes).astype(jnp.int32),
+        tables,
+        chosen,
+        *exchange([chosen, chosen]),
+        *received[:2],
+    )
+
+    def precondition(vector, carried, ride=None):
         grams = carried.shape[0] - modes
-        (local,) = call(
-            local_kernel, "local_inverse", product_flops, [block], weight, local_inverse, vector
+        local, *early = call(
+            local_kernel,
+            "local_inverse",
+            product_flops,
+            [block, part, part],
+            parity,
+            weight,
+            local_inverse,
+            vector,
         )
+        early = exchange(early)
         bits = bits_of("sub")
         for bit in bits[:-1]:
             rows_out = 2 * carried.shape[0] - grams
+            arrived = swap(carried, "sub", bit)
+            if ride is not None and bit == bits[0]:
+                arrived, ride = lax.optimization_barrier((arrived, ride))
             (carried,) = call(
                 functools.partial(fold_kernel, grams),
                 "fold",
                 columns * rows_out,
                 [((rows_out, columns), jnp.float32)],
                 carried,
-                swap(carried, "sub", bit),
+                arrived,
             )
         slots = call(
             functools.partial(finish_kernel, grams),
@@ -443,11 +521,12 @@
             weight,
             basis,
             chosen,
+            near,
             local,
             carried,
             swap(carried, "sub", bits[-1]),
         )
-        return slots, exchange(slots)
+        return slots, early + exchange(slots[2:], 2), ride
 
     def operator(slots, received):
         grams = slots[2].shape[0] - zone
@@ -480,7 +559,8 @@
         *rhs_slots,
         *received,
     )
-    z, image, received = operator(*precondition(r, pieces))
+    slots, received, _ = precondition(r, pieces)
+    z, image, received = operator(slots, received)
     w, carried = call(
         gram_start_kernel,
         "start_grams",
@@ -495,9 +575,11 @@
         *image,
         *received,
     )
+    ride = None
     for iteration in range(ITERS - 1):
         final = iteration + 2 == ITERS
-        m, image, received, grams = operator(*precondition(w, carried))
+        slots, received, inner_inverse = precondition(w, carried, ride)
+        m, image, received, grams = operator(slots, received)
         common = (parity, tables, weight, basis, grams)
         if iteration == 0:
             p, s, q = z, w, m
@@ -538,8 +620,8 @@
             if not final:
                 (carried,) = carried
         grams, curvature = lax.optimization_barrier((grams, curvature))
-        (inner_inverse,) = call(inverse_kernel, "inner_inverse", solve_flops, [square], grams)
-    grams = total(*carried)
+        (ride,) = call(inverse_kernel, "inner_inverse", solve_flops, [square], grams)
+    *grams, inner_inverse = total(*carried, ride)
     x, r = call(
         last_update_kernel,
         "last_update",

time: 198 us -> 205 us (1.035)
  starting transfers between devices: 84.4 us -> 97.2 us
  waiting for transfers between devices: 64 us -> 51.3 us
  Pallas kernels: 42.5 us -> 45.8 us
  local copies, waits for them, and re-layouts: 3.28 us -> 5.99 us
    ppermute x23, waiting for transfers between devices: 52.9 us -> 43 us  [swap(): lax.ppermute(x, axis, [(i, i ^ bit) for i in range(lax.axis_size(axis))])]
    ppermute x28 -> x30, starting transfers between devices: 36.9 us -> 45.6 us  [exchange(): lax.ppermute(slot, axis, pairs(axis, low))]
    ppermute x23, starting transfers between devices: 47.5 us -> 51.6 us  [swap(): lax.ppermute(x, axis, [(i, i ^ bit) for i in range(lax.axis_size(axis))])]
    unnamed x12 -> x22, local copies, waits for them, and re-layouts: 2.31 us -> 5.97 us
    pallas_call x24 -> x26, Pallas kernels: 42.5 us -> 45.8 us  [call(): pl.pallas_call(kernel, out_shape=shapes, in_specs=[SMEM if a.ndim == 1 el...]
    ppermute x28 -> x30, waiting for transfers between devices: 11.1 us -> 8.3 us  [exchange(): lax.ppermute(slot, axis, pairs(axis, low))]
  transfers between devices with their start and end apart: 51 -> 53, of which waited for: 24 -> 22; matrix products, arithmetic and copies ran while one was open for 1% -> 0% of each run, Pallas kernels for 7% -> 8%
where the time goes in v1:
time: 205 us; the launch traced here: 204 us
  starting transfers between devices  97.2 us (47%)
  waiting for transfers between devices  51.3 us (25%)
  Pallas kernels  45.8 us (22%)
  local copies, waits for them, and re-layouts  5.99 us (3%)
  other arithmetic  2.41 us (1%)
    ppermute x23, starting transfers between devices, swap(): lax.ppermute(x, axis, [(i, i ^ bit) for i in range(lax.axis_size(axis))])  51.6 us
    pallas_call x26, Pallas kernels, call(): pl.pallas_call(kernel, out_shape=shapes, in_specs=[SMEM if a.ndim == 1 el...  45.8 us
    ppermute x30, starting transfers between devices, exchange(): lax.ppermute(slot, axis, pairs(axis, low))  45.6 us
    ppermute x23, waiting for transfers between devices, swap(): lax.ppermute(x, axis, [(i, i ^ bit) for i in range(lax.axis_size(axis))])  43 us
    ppermute x30, waiting for transfers between devices, exchange(): lax.ppermute(slot, axis, pairs(axis, low))  8.3 us
    unnamed x22, local copies, waits for them, and re-layouts  5.97 us
  transfers between devices with their start and end apart: 53, of which 22 were waited for; matrix products, arithmetic and copies ran while one was open for 0% of the time, Pallas kernels for 8%

profile of v1, /device:TPU:0, one launch (start us, length us, event | category | flops | bytes accessed | tf_op | source)
XLA Modules:
  0.0 203.8 jit_solution(3102490357939289767)
XLA Ops:
  0.6 3.0 %collective-permute-start = (s32[32]{0:T(128)}, s32[32]{0:T(128)S(1)}, u32[]{:S(2)}, u32[]{:S(2)}) collective-permute-start(s32[32]{0:T(128)} %bitcast.37), channel_id=1, source_target_pairs={{0,1},{1,0},{2,3},{3,2},{4,5},{5,4},{6,7},{7,6},{8,9},{9,8},{10,11... | collective-permute-start | bytes 392 | tf_op jit(solution)/shard_map/ppermute | solution.py:16
  3.7 1.7 collective-permute-done
  6.0 2.1 %collective-permute-start.1 = (s32[64]{0:T(128)S(1)}, s32[64]{0:T(128)S(1)}, u32[]{:S(2)}, u32[]{:S(2)}) collective-permute-start(s32[64]{0:T(128)S(1)} %pad_add_fusion.2), channel_id=1, source_target_pairs={{0,2},{1,3},{2,0},{3,1},{4,6},{5,7},{6,4},{7,5},{8,10},{9,11},{10,... | collective-permute-start | bytes 776 | tf_op jit(solution)/shard_map/ppermute | solution.py:16
  8.1 1.5 collective-permute-done.1
  10.4 3.0 %collective-permute-start.2 = (s32[128]{0:T(128)S(1)}, s32[128]{0:T(128)S(1)}, u32[]{:S(2)}, u32[]{:S(2)}) collective-permute-start(s32[128]{0:T(128)S(1)} %pad_add_fusion.3), channel_id=1, source_target_pairs={{0,4},{1,5},{2,6},{3,7},{4,0},{5,1},{6,2},{7,3},{8,12},{9,13},{10,... | collective-permute-start | bytes 1544 | tf_op jit(solution)/shard_map/ppermute | solution.py:16
  13.4 1.5 collective-permute-done.2
  17.3 3.0 %collective-permute-start.3 = (bf16[4,32,256]{2,1,0:T(8,128)(2,1)S(1)}, bf16[4,32,256]{2,1,0:T(8,128)(2,1)S(1)}, u32[]{:S(2)}, u32[]{:S(2)}) collective-permute-start(bf16[4,32,256]{2,1,0:T(8,128)(2,1)S(1)} %slice.25), channel_id=1, source_target_pairs={{0,4},{1,5},{2,6},{3,7},{4,0},{5,1},{6,2},{7,3},{8,12},{9,13},{10,... | collective-permute-start | bytes 196616 | tf_op jit(solution)/shard_map/ppermute | solution.py:16
  23.5 1.6 collective-permute-start.8
  25.8 3.3 %collective-permute-start.4 = (bf16[2,32,256]{2,1,0:T(8,128)(2,1)S(1)}, bf16[2,32,256]{2,1,0:T(8,128)(2,1)S(1)}, u32[]{:S(2)}, u32[]{:S(2)}) collective-permute-start(bf16[2,32,256]{2,1,0:T(8,128)(2,1)S(1)} %slice.27), channel_id=1, source_target_pairs={{0,2},{1,3},{2,0},{3,1},{4,6},{5,7},{6,4},{7,5},{8,10},{9,11},{10,... | collective-permute-start | bytes 98312 | tf_op jit(solution)/shard_map/ppermute | solution.py:16
  30.4 1.2 shared_row_tables.1
  31.7 1.1 start.1
  33.7 1.1 collective-permute-start.12
  34.8 2.6 %collective-permute-done.12.received = f32[32,128]{1,0:T(8,128)S(1)} collective-permute-done((f32[32,128]{1,0:T(8,128)S(1)}, f32[32,128]{1,0:T(8,128)S(1)}, u32[]{:S(2)}, u32[]{:S(2)}) %collective-permute-start.12) | collective-permute-done | bytes 16416 | tf_op jit(solution)/shard_map/ppermute | solution.py:16
  37.4 2.2 %collective-permute-start.13 = (f32[64,128]{1,0:T(8,128)S(1)}, f32[64,128]{1,0:T(8,128)S(1)}, u32[]{:S(2)}, u32[]{:S(2)}) collective-permute-start(f32[64,128]{1,0:T(8,128)S(1)} %fold.6.own), channel_id=1, source_target_pairs={{0,2},{1,3},{2,0},{3,1},{4,6},{5,7},{6,4},{7,5},{8,10},{9,11},{10,... | collective-permute-start | bytes 98312 | tf_op jit(solution)/shard_map/ppermute | solution.py:16
  44.1 4.0 %collective-permute-start.6 = (bf16[32,256]{1,0:T(8,128)(2,1)S(1)}, bf16[32,256]{1,0:T(8,128)(2,1)S(1)}, u32[]{:S(2)}, u32[]{:S(2)}) collective-permute-start(bf16[32,256]{1,0:T(8,128)(2,1)S(1)} %fusion.chosen), channel_id=1, source_target_pairs={{0,1},{2,3},{4,5},{6,7},{1,0},{3,2},{5,4},{7,6},{8,9},{10,11},{12,... | collective-permute-start | bytes 49160 | tf_op jit(solution)/shard_map/ppermute | solution.py:415
  49.1 1.3 local_inverse.3
  52.0 1.1 coarse_part.3
  54.0 1.5 collective-permute-done.15.refs_4_
  55.4 1.6 operator.3
  57.0 4.9 %collective-permute-start.19 = (f32[256,128]{1,0:T(8,128)S(1)}, f32[256,128]{1,0:T(8,128)S(1)}, u32[]{:S(2)}, u32[]{:S(2)}) collective-permute-start(f32[256,128]{1,0:T(8,128)S(1)} %get-tuple-element.96.refs_0_), channel_id=1, source_target_pairs={{0,1},{2,3},{4,5},{6,7},{1,0},{3,2},{5,4},{7,6},{8,9},{10,11},{12,... | collective-permute-start | bytes 393224 | tf_op jit(solution)/shard_map/ppermute | solution.py:415
  62.6 5.6 %collective-permute-start.21 = (f32[256,128]{1,0:T(8,128)S(1)}, f32[256,128]{1,0:T(8,128)S(1)}, u32[]{:S(2)}, u32[]{:S(2)}) collective-permute-start(f32[256,128]{1,0:T(8,128)S(1)} %get-tuple-element.98.refs_2_), channel_id=1, source_target_pairs={{0,8},{16,24},{8,0},{24,16},{1,9},{17,25},{9,1},{25,17},{2,10},{18... | collective-permute-start | bytes 393224 | tf_op jit(solution)/shard_map/ppermute | solution.py:415
  69.1 1.5 start_grams.1
  70.6 3.5 %collective-permute-start.23 = (f32[176,128]{1,0:T(8,128)S(1)}, f32[176,128]{1,0:T(8,128)S(1)}, u32[]{:S(2)}, u32[]{:S(2)}) collective-permute-start(f32[176,128]{1,0:T(8,128)S(1)} %get-tuple-element.102.own), channel_id=1, source_target_pairs={{0,1},{1,0},{2,3},{3,2},{4,5},{5,4},{6,7},{7,6},{8,9},{9,8},{10,11... | collective-permute-start | bytes 270344 | tf_op jit(solution)/shard_map/ppermute | solution.py:16
  74.2 2.5 %collective-permute-done.23.received = f32[176,128]{1,0:T(8,128)S(1)} collective-permute-done((f32[176,128]{1,0:T(8,128)S(1)}, f32[176,128]{1,0:T(8,128)S(1)}, u32[]{:S(2)}, u32[]{:S(2)}) %collective-permute-start.23) | collective-permute-done | bytes 90144 | tf_op jit(solution)/shard_map/ppermute | solution.py:16
  76.7 1.4 collective-permute-start.24
  78.1 3.4 %collective-permute-done.24.received = f32[208,128]{1,0:T(8,128)S(1)} collective-permute-done((f32[208,128]{1,0:T(8,128)S(1)}, f32[208,128]{1,0:T(8,128)S(1)}, u32[]{:S(2)}, u32[]{:S(2)}) %collective-permute-start.24) | collective-permute-done | bytes 106528 | tf_op jit(solution)/shard_map/ppermute | solution.py:16
  81.5 3.1 %collective-permute-start.25 = (f32[272,128]{1,0:T(8,128)S(1)}, f32[272,128]{1,0:T(8,128)S(1)}, u32[]{:S(2)}, u32[]{:S(2)}) collective-permute-start(f32[272,128]{1,0:T(8,128)S(1)} %fold.9.own), channel_id=1, source_target_pairs={{0,4},{1,5},{2,6},{3,7},{4,0},{5,1},{6,2},{7,3},{8,12},{9,13},{10,... | collective-permute-start | bytes 417800 | tf_op jit(solution)/shard_map/ppermute | solution.py:16
  84.6 1.3 local_inverse.4
  85.9 2.7 %collective-permute-done.25.received = f32[272,128]{1,0:T(8,128)S(1)} collective-permute-done((f32[272,128]{1,0:T(8,128)S(1)}, f32[272,128]{1,0:T(8,128)S(1)}, u32[]{:S(2)}, u32[]{:S(2)}) %collective-permute-start.25) | collective-permute-done | bytes 139296 | tf_op jit(solution)/shard_map/ppermute | solution.py:16
  88.6 1.1 coarse_part.4
  89.7 3.9 %collective-permute-start.28 = (f32[400,128]{1,0:T(8,128)S(1)}, f32[400,128]{1,0:T(8,128)S(1)}, u32[]{:S(2)}, u32[]{:S(2)}) collective-permute-start(f32[400,128]{1,0:T(8,128)S(1)} %get-tuple-element.105.refs_2_), channel_id=1, source_target_pairs={{0,8},{16,24},{8,0},{24,16},{1,9},{17,25},{9,1},{25,17},{2,10},{18... | collective-permute-start | bytes 614408 | tf_op jit(solution)/shard_map/ppermute | solution.py:415
  93.6 1.4 collective-permute-start.26
  96.3 2.8 %collective-permute-done.26.refs_4_ = f32[256,128]{1,0:T(8,128)S(1)} collective-permute-done((f32[256,128]{1,0:T(8,128)S(1)}, f32[256,128]{1,0:T(8,128)S(1)}, u32[]{:S(2)}, u32[]{:S(2)}) %collective-permute-start.26) | collective-permute-done | bytes 131104 | tf_op jit(solution)/shard_map/ppermute | solution.py:415
  99.1 1.6 operator.4
  100.7 4.6 %collective-permute-start.31 = (f32[256,128]{1,0:T(8,128)S(1)}, f32[256,128]{1,0:T(8,128)S(1)}, u32[]{:S(2)}, u32[]{:S(2)}) collective-permute-start(f32[256,128]{1,0:T(8,128)S(1)} %get-tuple-element.111.refs_0_), channel_id=1, source_target_pairs={{0,1},{2,3},{4,5},{6,7},{1,0},{3,2},{5,4},{7,6},{8,9},{10,11},{12,... | collective-permute-start | bytes 393224 | tf_op jit(solution)/shard_map/ppermute | solution.py:415
  105.9 3.4 %collective-permute-start.33 = (f32[256,128]{1,0:T(8,128)S(1)}, f32[256,128]{1,0:T(8,128)S(1)}, u32[]{:S(2)}, u32[]{:S(2)}) collective-permute-start(f32[256,128]{1,0:T(8,128)S(1)} %get-tuple-element.113.refs_2_), channel_id=1, source_target_pairs={{0,8},{16,24},{8,0},{24,16},{1,9},{17,25},{9,1},{25,17},{2,10},{18... | collective-permute-start | bytes 393224 | tf_op jit(solution)/shard_map/ppermute | solution.py:415
  110.2 3.2 %collective-permute-start.30 = (f32[144,128]{1,0:T(8,128)S(1)}, f32[144,128]{1,0:T(8,128)S(1)}, u32[]{:S(2)}, u32[]{:S(2)}) collective-permute-start(f32[144,128]{1,0:T(8,128)S(1)} %get-tuple-element.109), channel_id=1, source_target_pairs={{0,16},{8,24},{16,0},{24,8},{1,17},{9,25},{17,1},{25,9},{2,18},{10... | collective-permute-start | bytes 221192 | tf_op jit(solution)/shard_map/ppermute | solution.py:16
  113.4 4.2 %collective-permute-done.30 = f32[144,128]{1,0:T(8,128)S(1)} collective-permute-done((f32[144,128]{1,0:T(8,128)S(1)}, f32[144,128]{1,0:T(8,128)S(1)}, u32[]{:S(2)}, u32[]{:S(2)}) %collective-permute-start.30) | collective-permute-done | bytes 73760 | tf_op jit(solution)/shard_map/ppermute | solution.py:16
  117.7 6.7 %first_update.1 = (f32[1024,128]{1,0:T(8,128)S(1)}, f32[1024,128]{1,0:T(8,128)S(1)}, f32[1024,128]{1,0:T(8,128)S(1)}, f32[1024,128]{1,0:T(8,128)S(1)}, f32[1024,...) custom-call(s32[2]{0:T(128)S(1)} %pad_add_fusion.1.parity, ...), custom_call_target="tpu_custom_call" | custom-call | flops 800000000 | bytes 7110664 | tf_op jit(solution)/shard_map/first_update/pallas_call | solution.py:395
  124.3 3.8 %collective-permute-start.35 = (f32[176,128]{1,0:T(8,128)S(1)}, f32[176,128]{1,0:T(8,128)S(1)}, u32[]{:S(2)}, u32[]{:S(2)}) collective-permute-start(f32[176,128]{1,0:T(8,128)S(1)} %get-tuple-element.117.own), channel_id=1, source_target_pairs={{0,1},{1,0},{2,3},{3,2},{4,5},{5,4},{6,7},{7,6},{8,9},{9,8},{10,11... | collective-permute-start | bytes 270344 | tf_op jit(solution)/shard_map/ppermute | solution.py:16
  128.2 3.9 %inner_inverse.2 = f32[128,128]{1,0:T(8,128)S(1)} custom-call(f32[144,128]{1,0:T(8,128)S(1)} %add.47.grams), custom_call_target="tpu_custom_call" | custom-call | flops 400000000 | bytes 139264 | tf_op jit(solution)/shard_map/inner_inverse/pallas_call | solution.py:395
  132.2 1.1 collective-permute-start.36
  133.3 3.7 %collective-permute-done.36.received = f32[208,128]{1,0:T(8,128)S(1)} collective-permute-done((f32[208,128]{1,0:T(8,128)S(1)}, f32[208,128]{1,0:T(8,128)S(1)}, u32[]{:S(2)}, u32[]{:S(2)}) %collective-permute-start.36) | collective-permute-done | bytes 106528 | tf_op jit(solution)/shard_map/ppermute | solution.py:16
  136.9 2.1 %collective-permute-start.37 = (f32[272,128]{1,0:T(8,128)S(1)}, f32[272,128]{1,0:T(8,128)S(1)}, u32[]{:S(2)}, u32[]{:S(2)}) collective-permute-start(f32[272,128]{1,0:T(8,128)S(1)} %fold.11.own), channel_id=1, source_target_pairs={{0,4},{1,5},{2,6},{3,7},{4,0},{5,1},{6,2},{7,3},{8,12},{9,13},{10,... | collective-permute-start | bytes 417800 | tf_op jit(solution)/shard_map/ppermute | solution.py:16
  139.1 1.3 local_inverse.5
  140.4 4.8 %collective-permute-done.37.received = f32[272,128]{1,0:T(8,128)S(1)} collective-permute-done((f32[272,128]{1,0:T(8,128)S(1)}, f32[272,128]{1,0:T(8,128)S(1)}, u32[]{:S(2)}, u32[]{:S(2)}) %collective-permute-start.37) | collective-permute-done | bytes 139296 | tf_op jit(solution)/shard_map/ppermute | solution.py:16
  145.2 1.1 coarse_part.5
  148.5 3.7 %collective-permute-done.38.refs_4_ = f32[256,128]{1,0:T(8,128)S(1)} collective-permute-done((f32[256,128]{1,0:T(8,128)S(1)}, f32[256,128]{1,0:T(8,128)S(1)}, u32[]{:S(2)}, u32[]{:S(2)}) %collective-permute-start.38) | collective-permute-done | bytes 131104 | tf_op jit(solution)/shard_map/ppermute | solution.py:415
  152.3 1.6 operator.5
  153.8 4.6 %collective-permute-start.43 = (f32[256,128]{1,0:T(8,128)S(1)}, f32[256,128]{1,0:T(8,128)S(1)}, u32[]{:S(2)}, u32[]{:S(2)}) collective-permute-start(f32[256,128]{1,0:T(8,128)S(1)} %get-tuple-element.135.refs_0_), channel_id=1, source_target_pairs={{0,1},{2,3},{4,5},{6,7},{1,0},{3,2},{5,4},{7,6},{8,9},{10,11},{12,... | collective-permute-start | bytes 393224 | tf_op jit(solution)/shard_map/ppermute | solution.py:415
  160.1 3.4 %collective-permute-start.42 = (f32[144,128]{1,0:T(8,128)S(1)}, f32[144,128]{1,0:T(8,128)S(1)}, u32[]{:S(2)}, u32[]{:S(2)}) collective-permute-start(f32[144,128]{1,0:T(8,128)S(1)} %get-tuple-element.127), channel_id=1, source_target_pairs={{0,16},{8,24},{16,0},{24,8},{1,17},{9,25},{17,1},{25,9},{2,18},{10... | collective-permute-start | bytes 221192 | tf_op jit(solution)/shard_map/ppermute | solution.py:16
  163.5 4.2 %collective-permute-done.42 = f32[144,128]{1,0:T(8,128)S(1)} collective-permute-done((f32[144,128]{1,0:T(8,128)S(1)}, f32[144,128]{1,0:T(8,128)S(1)}, u32[]{:S(2)}, u32[]{:S(2)}) %collective-permute-start.42) | collective-permute-done | bytes 73760 | tf_op jit(solution)/shard_map/ppermute | solution.py:16
  167.8 6.6 %next_update.1 = (f32[1024,128]{1,0:T(8,128)S(1)}, f32[1024,128]{1,0:T(8,128)S(1)}, f32[1024,128]{1,0:T(8,128)S(1)}, f32[1024,128]{1,0:T(8,128)S(1)}, f32[1024,1...) custom-call(s32[2]{0:T(128)S(1)} %pad_add_fusion.1.parity, ...), custom_call_target="tpu_custom_call" | custom-call | flops 800000000 | bytes 11419656 | tf_op jit(solution)/shard_map/next_update/pallas_call | solution.py:395
  174.5 1.2 collective-permute-done.47
  175.7 3.6 %collective-permute-start.48 = (f32[72,128]{1,0:T(8,128)S(1)}, f32[72,128]{1,0:T(8,128)S(1)}, u32[]{:S(2)}, u32[]{:S(2)}) collective-permute-start(f32[72,128]{1,0:T(8,128)S(1)} %add.49), channel_id=1, source_target_pairs={{0,1},{1,0},{2,3},{3,2},{4,5},{5,4},{6,7},{7,6},{8,9},{9,8},{10,11... | collective-permute-start | bytes 110600 | tf_op jit(solution)/shard_map/ppermute | solution.py:16
  179.2 1.9 collective-permute-done.48
  181.2 1.1 collective-permute-start.49
  182.3 3.9 %inner_inverse.3 = f32[128,128]{1,0:T(8,128)S(1)} custom-call(f32[144,128]{1,0:T(8,128)S(1)} %add.48.grams), custom_call_target="tpu_custom_call" | custom-call | flops 400000000 | bytes 139264 | tf_op jit(solution)/shard_map/inner_inverse/pallas_call | solution.py:395
  186.3 2.8 %collective-permute-start.50 = (f32[72,128]{1,0:T(8,128)S(1)}, f32[72,128]{1,0:T(8,128)S(1)}, u32[]{:S(2)}, u32[]{:S(2)}) collective-permute-start(f32[72,128]{1,0:T(8,128)S(1)} %add.51), channel_id=1, source_target_pairs={{0,2},{1,3},{2,0},{3,1},{4,6},{5,7},{6,4},{7,5},{8,10},{9,11},{10,... | collective-permute-start | bytes 110600 | tf_op jit(solution)/shard_map/ppermute | solution.py:16
  189.0 1.9 collective-permute-done.50
  191.0 2.7 %collective-permute-start.51 = (f32[72,128]{1,0:T(8,128)S(1)}, f32[72,128]{1,0:T(8,128)S(1)}, u32[]{:S(2)}, u32[]{:S(2)}) collective-permute-start(f32[72,128]{1,0:T(8,128)S(1)} %add.52), channel_id=1, source_target_pairs={{0,4},{1,5},{2,6},{3,7},{4,0},{5,1},{6,2},{7,3},{8,12},{9,13},{10,... | collective-permute-start | bytes 110600 | tf_op jit(solution)/shard_map/ppermute | solution.py:16
  193.7 2.1 %collective-permute-done.51 = f32[72,128]{1,0:T(8,128)S(1)} collective-permute-done((f32[72,128]{1,0:T(8,128)S(1)}, f32[72,128]{1,0:T(8,128)S(1)}, u32[]{:S(2)}, u32[]{:S(2)}) %collective-permute-start.51) | collective-permute-done | bytes 36896 | tf_op jit(solution)/shard_map/ppermute | solution.py:16
  195.8 1.2 collective-permute-done.52.other
  197.0 6.8 %last_update.1 = (f32[1024,128]{1,0:T(8,128)}, f32[1024,128]{1,0:T(8,128)}) custom-call(s32[2]{0:T(128)S(1)} %pad_add_fusion.1.parity, f32[72,128]{1,0:T(8,128)S(1)} %add.53.half, f32[72,128]{1,0:T(8,128)S(1)} %collective-permute-done.52.other, f32[128,128]{1,0:T(8,128)S(1)} %inner_inverse.3, f32[128,128]{1,0:T(8,128)S(1)} %get-tuple-element.145.curvature, ...), custom_call_target="tpu_custom_call" | custom-call | flops 800000000 | bytes 4399112 | tf_op jit(solution)/shard_map/last_update/pallas_call | solution.py:395
  (108 shorter events, 26.4 us)
Async XLA Ops:
  0.6 4.7 %collective-permute-start = (s32[32]{0:T(128)}, s32[32]{0:T(128)S(1)}, u32[]{:S(2)}, u32[]{:S(2)}) collective-permute-start(s32[32]{0:T(128)} %bitcast.37), channel_id=1, source_target_pairs={{0,1},{1,0},{2,3},{3,2},{4,5},{5,4},{6,7},{7,6},{8,9},{9,8},{10,11... | collective-permute-start | bytes 392 | tf_op jit(solution)/shard_map/ppermute | solution.py:16
  6.0 3.6 %collective-permute-start.1 = (s32[64]{0:T(128)S(1)}, s32[64]{0:T(128)S(1)}, u32[]{:S(2)}, u32[]{:S(2)}) collective-permute-start(s32[64]{0:T(128)S(1)} %pad_add_fusion.2), channel_id=1, source_target_pairs={{0,2},{1,3},{2,0},{3,1},{4,6},{5,7},{6,4},{7,5},{8,10},{9,11},{10,... | collective-permute-start | bytes 776 | tf_op jit(solution)/shard_map/ppermute | solution.py:16
  10.4 4.6 %collective-permute-start.2 = (s32[128]{0:T(128)S(1)}, s32[128]{0:T(128)S(1)}, u32[]{:S(2)}, u32[]{:S(2)}) collective-permute-start(s32[128]{0:T(128)S(1)} %pad_add_fusion.3), channel_id=1, source_target_pairs={{0,4},{1,5},{2,6},{3,7},{4,0},{5,1},{6,2},{7,3},{8,12},{9,13},{10,... | collective-permute-start | bytes 1544 | tf_op jit(solution)/shard_map/ppermute | solution.py:16
  15.7 1.0 copy-start.8
  16.6 31.4 %copy-start = (bf16[1,1,1024,1024]{3,2,1,0:T(8,128)(2,1)S(1)}, bf16[1,1,1024,1024]{3,2,1,0:T(8,128)(2,1)}, u32[]{:S(2)}) copy-start(bf16[1,1,1024,1024]{3,2,1,0:T(8,128)(2,1)} %param.9) | copy-start | bytes 6291460
  17.3 8.5 %collective-permute-start.3 = (bf16[4,32,256]{2,1,0:T(8,128)(2,1)S(1)}, bf16[4,32,256]{2,1,0:T(8,128)(2,1)S(1)}, u32[]{:S(2)}, u32[]{:S(2)}) collective-permute-start(bf16[4,32,256]{2,1,0:T(8,128)(2,1)S(1)} %slice.25), channel_id=1, source_target_pairs={{0,4},{1,5},{2,6},{3,7},{4,0},{5,1},{6,2},{7,3},{8,12},{9,13},{10,... | collective-permute-start | bytes 196616 | tf_op jit(solution)/shard_map/ppermute | solution.py:16
  20.4 0.8 copy-start.5
  21.2 0.9 copy-start.7
  22.8 8.9 %collective-permute-start.10 = (bf16[256,128]{1,0:T(8,128)(2,1)S(1)}, bf16[256,128]{1,0:T(8,128)(2,1)S(1)}, u32[]{:S(2)}, u32[]{:S(2)}) collective-permute-start(bf16[256,128]{1,0:T(8,128)(2,1)S(1)} %get-tuple-element.84.refs_2_), channel_id=1, source_target_pairs={{0,8},{16,24},{8,0},{24,16},{1,9},{17,25},{9,1},{25,17},{2,10},{18... | collective-permute-start | bytes 196616 | tf_op jit(solution)/shard_map/ppermute | solution.py:415
  22.8 8.9 %collective-permute-start.11 = (bf16[256,128]{1,0:T(8,128)(2,1)S(1)}, bf16[256,128]{1,0:T(8,128)(2,1)S(1)}, u32[]{:S(2)}, u32[]{:S(2)}) collective-permute-start(bf16[256,128]{1,0:T(8,128)(2,1)S(1)} %get-tuple-element.85.refs_3_), channel_id=1, source_target_pairs={{8,16},{16,8},{9,17},{17,9},{10,18},{18,10},{11,19},{19,11},{12,20... | collective-permute-start | bytes 196616 | tf_op jit(solution)/shard_map/ppermute | solution.py:415
  23.5 8.2 %collective-permute-start.8 = (bf16[320,128]{1,0:T(8,128)(2,1)S(1)}, bf16[320,128]{1,0:T(8,128)(2,1)S(1)}, u32[]{:S(2)}, u32[]{:S(2)}) collective-permute-start(bf16[320,128]{1,0:T(8,128)(2,1)S(1)} %get-tuple-element.80.refs_0_), channel_id=1, source_target_pairs={{0,1},{2,3},{4,5},{6,7},{1,0},{3,2},{5,4},{7,6},{8,9},{10,11},{12,... | collective-permute-start | bytes 245768 | tf_op jit(solution)/shard_map/ppermute | solution.py:415
  25.1 6.6 %collective-permute-start.9 = (bf16[320,128]{1,0:T(8,128)(2,1)S(1)}, bf16[320,128]{1,0:T(8,128)(2,1)S(1)}, u32[]{:S(2)}, u32[]{:S(2)}) collective-permute-start(bf16[320,128]{1,0:T(8,128)(2,1)S(1)} %get-tuple-element.81.refs_1_), channel_id=1, source_target_pairs={{1,2},{3,4},{5,6},{2,1},{4,3},{6,5},{9,10},{11,12},{13,14},{10,9},... | collective-permute-start | bytes 245768 | tf_op jit(solution)/shard_map/ppermute | solution.py:415
  25.8 13.8 %collective-permute-start.4 = (bf16[2,32,256]{2,1,0:T(8,128)(2,1)S(1)}, bf16[2,32,256]{2,1,0:T(8,128)(2,1)S(1)}, u32[]{:S(2)}, u32[]{:S(2)}) collective-permute-start(bf16[2,32,256]{2,1,0:T(8,128)(2,1)S(1)} %slice.27), channel_id=1, source_target_pairs={{0,2},{1,3},{2,0},{3,1},{4,6},{5,7},{6,4},{7,5},{8,10},{9,11},{10,... | collective-permute-start | bytes 98312 | tf_op jit(solution)/shard_map/ppermute | solution.py:16
  29.1 0.7 copy-start.9
  29.8 0.7 copy-start.10
  32.8 0.8 copy-start.2
  33.7 3.7 %collective-permute-start.12 = (f32[32,128]{1,0:T(8,128)S(1)}, f32[32,128]{1,0:T(8,128)S(1)}, u32[]{:S(2)}, u32[]{:S(2)}) collective-permute-start(f32[32,128]{1,0:T(8,128)S(1)} %get-tuple-element.88.own), channel_id=1, source_target_pairs={{0,1},{1,0},{2,3},{3,2},{4,5},{5,4},{6,7},{7,6},{8,9},{9,8},{10,11... | collective-permute-start | bytes 49160 | tf_op jit(solution)/shard_map/ppermute | solution.py:16
  37.4 14.6 %copy-start.6 = (bf16[1,1,32,1024]{3,2,1,0:T(8,128)(2,1)S(1)}, bf16[1,1,32,1024]{3,2,1,0:T(8,128)(2,1)}, u32[]{:S(2)}) copy-start(bf16[1,1,32,1024]{3,2,1,0:T(8,128)(2,1)} %param.11) | copy-start | bytes 196612
  37.4 4.2 %collective-permute-start.13 = (f32[64,128]{1,0:T(8,128)S(1)}, f32[64,128]{1,0:T(8,128)S(1)}, u32[]{:S(2)}, u32[]{:S(2)}) collective-permute-start(f32[64,128]{1,0:T(8,128)S(1)} %fold.6.own), channel_id=1, source_target_pairs={{0,2},{1,3},{2,0},{3,1},{4,6},{5,7},{6,4},{7,5},{8,10},{9,11},{10,... | collective-permute-start | bytes 98312 | tf_op jit(solution)/shard_map/ppermute | solution.py:16
  39.6 3.8 %collective-permute-start.5 = (bf16[1,32,256]{2,1,0:T(8,128)(2,1)S(1)}, bf16[1,32,256]{2,1,0:T(8,128)(2,1)S(1)}, u32[]{:S(2)}, u32[]{:S(2)}) collective-permute-start(bf16[1,32,256]{2,1,0:T(8,128)(2,1)S(1)} %slice.29), channel_id=1, source_target_pairs={{0,1},{1,0},{2,3},{3,2},{4,5},{5,4},{6,7},{7,6},{8,9},{9,8},{10,11... | collective-permute-start | bytes 49160 | tf_op jit(solution)/shard_map/ppermute | solution.py:16
  41.6 10.4 %collective-permute-start.14 = (f32[128,128]{1,0:T(8,128)S(1)}, f32[128,128]{1,0:T(8,128)S(1)}, u32[]{:S(2)}, u32[]{:S(2)}) collective-permute-start(f32[128,128]{1,0:T(8,128)S(1)} %fold.7.own), channel_id=1, source_target_pairs={{0,4},{1,5},{2,6},{3,7},{4,0},{5,1},{6,2},{7,3},{8,12},{9,13},{10,... | collective-permute-start | bytes 196616 | tf_op jit(solution)/shard_map/ppermute | solution.py:16
  43.4 7.7 %collective-permute-start.7 = (bf16[32,256]{1,0:T(8,128)(2,1)S(1)}, bf16[32,256]{1,0:T(8,128)(2,1)S(1)}, u32[]{:S(2)}, u32[]{:S(2)}) collective-permute-start(bf16[32,256]{1,0:T(8,128)(2,1)S(1)} %fusion.chosen), channel_id=1, source_target_pairs={{1,2},{3,4},{5,6},{2,1},{4,3},{6,5},{9,10},{11,12},{13,14},{10,9},... | collective-permute-start | bytes 49160 | tf_op jit(solution)/shard_map/ppermute | solution.py:415
  44.1 7.1 %collective-permute-start.6 = (bf16[32,256]{1,0:T(8,128)(2,1)S(1)}, bf16[32,256]{1,0:T(8,128)(2,1)S(1)}, u32[]{:S(2)}, u32[]{:S(2)}) collective-permute-start(bf16[32,256]{1,0:T(8,128)(2,1)S(1)} %fusion.chosen), channel_id=1, source_target_pairs={{0,1},{2,3},{4,5},{6,7},{1,0},{3,2},{5,4},{7,6},{8,9},{10,11},{12,... | collective-permute-start | bytes 49160 | tf_op jit(solution)/shard_map/ppermute | solution.py:415
  48.1 1.0 copy-start.3
  49.1 6.3 %copy-start.1 = (bf16[1,1,1024,1024]{3,2,1,0:T(8,128)(2,1)S(1)}, bf16[1,1,1024,1024]{3,2,1,0:T(8,128)(2,1)}, u32[]{:S(2)}) copy-start(bf16[1,1,1024,1024]{3,2,1,0:T(8,128)(2,1)} %param.8) | copy-start | bytes 6291460
  50.4 5.0 %collective-permute-start.15 = (f32[256,128]{1,0:T(8,128)S(1)}, f32[256,128]{1,0:T(8,128)S(1)}, u32[]{:S(2)}, u32[]{:S(2)}) collective-permute-start(f32[256,128]{1,0:T(8,128)S(1)} %get-tuple-element.93), channel_id=1, source_target_pairs={{0,1},{2,3},{4,5},{6,7},{1,0},{3,2},{5,4},{7,6},{8,9},{10,11},{12,... | collective-permute-start | bytes 393224 | tf_op jit(solution)/shard_map/ppermute | solution.py:415
  50.5 4.9 %collective-permute-start.16 = (f32[256,128]{1,0:T(8,128)S(1)}, f32[256,128]{1,0:T(8,128)S(1)}, u32[]{:S(2)}, u32[]{:S(2)}) collective-permute-start(f32[256,128]{1,0:T(8,128)S(1)} %get-tuple-element.94), channel_id=1, source_target_pairs={{1,2},{3,4},{5,6},{2,1},{4,3},{6,5},{9,10},{11,12},{13,14},{10,9},... | collective-permute-start | bytes 393224 | tf_op jit(solution)/shard_map/ppermute | solution.py:415
  53.1 16.1 %copy-start.4 = (f32[1024,128]{1,0:T(8,128)S(1)}, f32[1024,128]{1,0:T(8,128)}, u32[]{:S(2)}) copy-start(f32[1024,128]{1,0:T(8,128)} %copy-done.2) | copy-start | bytes 1572868
  53.1 2.4 %collective-permute-start.17 = (f32[256,128]{1,0:T(8,128)S(1)}, f32[256,128]{1,0:T(8,128)S(1)}, u32[]{:S(2)}, u32[]{:S(2)}) collective-permute-start(f32[256,128]{1,0:T(8,128)S(1)} %get-tuple-element.91.refs_2_), channel_id=1, source_target_pairs={{0,8},{16,24},{8,0},{24,16},{1,9},{17,25},{9,1},{25,17},{2,10},{18... | collective-permute-start | bytes 393224 | tf_op jit(solution)/shard_map/ppermute | solution.py:415
  53.1 2.3 %collective-permute-start.18 = (f32[256,128]{1,0:T(8,128)S(1)}, f32[256,128]{1,0:T(8,128)S(1)}, u32[]{:S(2)}, u32[]{:S(2)}) collective-permute-start(f32[256,128]{1,0:T(8,128)S(1)} %get-tuple-element.92.refs_3_), channel_id=1, source_target_pairs={{8,16},{16,8},{9,17},{17,9},{10,18},{18,10},{11,19},{19,11},{12,20... | collective-permute-start | bytes 393224 | tf_op jit(solution)/shard_map/ppermute | solution.py:415
  57.0 11.8 %collective-permute-start.19 = (f32[256,128]{1,0:T(8,128)S(1)}, f32[256,128]{1,0:T(8,128)S(1)}, u32[]{:S(2)}, u32[]{:S(2)}) collective-permute-start(f32[256,128]{1,0:T(8,128)S(1)} %get-tuple-element.96.refs_0_), channel_id=1, source_target_pairs={{0,1},{2,3},{4,5},{6,7},{1,0},{3,2},{5,4},{7,6},{8,9},{10,11},{12,... | collective-permute-start | bytes 393224 | tf_op jit(solution)/shard_map/ppermute | solution.py:415
  61.9 6.9 %collective-permute-start.20 = (f32[256,128]{1,0:T(8,128)S(1)}, f32[256,128]{1,0:T(8,128)S(1)}, u32[]{:S(2)}, u32[]{:S(2)}) collective-permute-start(f32[256,128]{1,0:T(8,128)S(1)} %get-tuple-element.97.refs_1_), channel_id=1, source_target_pairs={{1,2},{3,4},{5,6},{2,1},{4,3},{6,5},{9,10},{11,12},{13,14},{10,9},... | collective-permute-start | bytes 393224 | tf_op jit(solution)/shard_map/ppermute | solution.py:415
  62.6 6.5 %collective-permute-start.21 = (f32[256,128]{1,0:T(8,128)S(1)}, f32[256,128]{1,0:T(8,128)S(1)}, u32[]{:S(2)}, u32[]{:S(2)}) collective-permute-start(f32[256,128]{1,0:T(8,128)S(1)} %get-tuple-element.98.refs_2_), channel_id=1, source_target_pairs={{0,8},{16,24},{8,0},{24,16},{1,9},{17,25},{9,1},{25,17},{2,10},{18... | collective-permute-start | bytes 393224 | tf_op jit(solution)/shard_map/ppermute | solution.py:415
  68.1 1.0 collective-permute-start.22
  70.6 6.0 %collective-permute-start.23 = (f32[176,128]{1,0:T(8,128)S(1)}, f32[176,128]{1,0:T(8,128)S(1)}, u32[]{:S(2)}, u32[]{:S(2)}) collective-permute-start(f32[176,128]{1,0:T(8,128)S(1)} %get-tuple-element.102.own), channel_id=1, source_target_pairs={{0,1},{1,0},{2,3},{3,2},{4,5},{5,4},{6,7},{7,6},{8,9},{9,8},{10,11... | collective-permute-start | bytes 270344 | tf_op jit(solution)/shard_map/ppermute | solution.py:16
  76.7 4.8 %collective-permute-start.24 = (f32[208,128]{1,0:T(8,128)S(1)}, f32[208,128]{1,0:T(8,128)S(1)}, u32[]{:S(2)}, u32[]{:S(2)}) collective-permute-start(f32[208,128]{1,0:T(8,128)S(1)} %fold.8.own), channel_id=1, source_target_pairs={{0,2},{1,3},{2,0},{3,1},{4,6},{5,7},{6,4},{7,5},{8,10},{9,11},{10,... | collective-permute-start | bytes 319496 | tf_op jit(solution)/shard_map/ppermute | solution.py:16
  81.5 7.1 %collective-permute-start.25 = (f32[272,128]{1,0:T(8,128)S(1)}, f32[272,128]{1,0:T(8,128)S(1)}, u32[]{:S(2)}, u32[]{:S(2)}) collective-permute-start(f32[272,128]{1,0:T(8,128)S(1)} %fold.9.own), channel_id=1, source_target_pairs={{0,4},{1,5},{2,6},{3,7},{4,0},{5,1},{6,2},{7,3},{8,12},{9,13},{10,... | collective-permute-start | bytes 417800 | tf_op jit(solution)/shard_map/ppermute | solution.py:16
  89.7 9.4 %collective-permute-start.28 = (f32[400,128]{1,0:T(8,128)S(1)}, f32[400,128]{1,0:T(8,128)S(1)}, u32[]{:S(2)}, u32[]{:S(2)}) collective-permute-start(f32[400,128]{1,0:T(8,128)S(1)} %get-tuple-element.105.refs_2_), channel_id=1, source_target_pairs={{0,8},{16,24},{8,0},{24,16},{1,9},{17,25},{9,1},{25,17},{2,10},{18... | collective-permute-start | bytes 614408 | tf_op jit(solution)/shard_map/ppermute | solution.py:415
  93.6 5.5 %collective-permute-start.26 = (f32[256,128]{1,0:T(8,128)S(1)}, f32[256,128]{1,0:T(8,128)S(1)}, u32[]{:S(2)}, u32[]{:S(2)}) collective-permute-start(f32[256,128]{1,0:T(8,128)S(1)} %get-tuple-element.107), channel_id=1, source_target_pairs={{0,1},{2,3},{4,5},{6,7},{1,0},{3,2},{5,4},{7,6},{8,9},{10,11},{12,... | collective-permute-start | bytes 393224 | tf_op jit(solution)/shard_map/ppermute | solution.py:415
  95.0 4.1 %collective-permute-start.27 = (f32[256,128]{1,0:T(8,128)S(1)}, f32[256,128]{1,0:T(8,128)S(1)}, u32[]{:S(2)}, u32[]{:S(2)}) collective-permute-start(f32[256,128]{1,0:T(8,128)S(1)} %get-tuple-element.108), channel_id=1, source_target_pairs={{1,2},{3,4},{5,6},{2,1},{4,3},{6,5},{9,10},{11,12},{13,14},{10,9},... | collective-permute-start | bytes 393224 | tf_op jit(solution)/shard_map/ppermute | solution.py:415
  95.7 3.4 %collective-permute-start.29 = (f32[256,128]{1,0:T(8,128)S(1)}, f32[256,128]{1,0:T(8,128)S(1)}, u32[]{:S(2)}, u32[]{:S(2)}) collective-permute-start(f32[256,128]{1,0:T(8,128)S(1)} %get-tuple-element.106.refs_3_), channel_id=1, source_target_pairs={{8,16},{16,8},{9,17},{17,9},{10,18},{18,10},{11,19},{19,11},{12,20... | collective-permute-start | bytes 393224 | tf_op jit(solution)/shard_map/ppermute | solution.py:415
  100.7 16.9 %collective-permute-start.31 = (f32[256,128]{1,0:T(8,128)S(1)}, f32[256,128]{1,0:T(8,128)S(1)}, u32[]{:S(2)}, u32[]{:S(2)}) collective-permute-start(f32[256,128]{1,0:T(8,128)S(1)} %get-tuple-element.111.refs_0_), channel_id=1, source_target_pairs={{0,1},{2,3},{4,5},{6,7},{1,0},{3,2},{5,4},{7,6},{8,9},{10,11},{12,... | collective-permute-start | bytes 393224 | tf_op jit(solution)/shard_map/ppermute | solution.py:415
  105.3 12.4 %collective-permute-start.32 = (f32[256,128]{1,0:T(8,128)S(1)}, f32[256,128]{1,0:T(8,128)S(1)}, u32[]{:S(2)}, u32[]{:S(2)}) collective-permute-start(f32[256,128]{1,0:T(8,128)S(1)} %get-tuple-element.112.refs_1_), channel_id=1, source_target_pairs={{1,2},{3,4},{5,6},{2,1},{4,3},{6,5},{9,10},{11,12},{13,14},{10,9},... | collective-permute-start | bytes 393224 | tf_op jit(solution)/shard_map/ppermute | solution.py:415
  105.9 11.7 %collective-permute-start.33 = (f32[256,128]{1,0:T(8,128)S(1)}, f32[256,128]{1,0:T(8,128)S(1)}, u32[]{:S(2)}, u32[]{:S(2)}) collective-permute-start(f32[256,128]{1,0:T(8,128)S(1)} %get-tuple-element.113.refs_2_), channel_id=1, source_target_pairs={{0,8},{16,24},{8,0},{24,16},{1,9},{17,25},{9,1},{25,17},{2,10},{18... | collective-permute-start | bytes 393224 | tf_op jit(solution)/shard_map/ppermute | solution.py:415
  109.3 8.3 %collective-permute-start.34 = (f32[256,128]{1,0:T(8,128)S(1)}, f32[256,128]{1,0:T(8,128)S(1)}, u32[]{:S(2)}, u32[]{:S(2)}) collective-permute-start(f32[256,128]{1,0:T(8,128)S(1)} %get-tuple-element.114.refs_3_), channel_id=1, source_target_pairs={{8,16},{16,8},{9,17},{17,9},{10,18},{18,10},{11,19},{19,11},{12,20... | collective-permute-start | bytes 393224 | tf_op jit(solution)/shard_map/ppermute | solution.py:415
  110.2 7.4 %collective-permute-start.30 = (f32[144,128]{1,0:T(8,128)S(1)}, f32[144,128]{1,0:T(8,128)S(1)}, u32[]{:S(2)}, u32[]{:S(2)}) collective-permute-start(f32[144,128]{1,0:T(8,128)S(1)} %get-tuple-element.109), channel_id=1, source_target_pairs={{0,16},{8,24},{16,0},{24,8},{1,17},{9,25},{17,1},{25,9},{2,18},{10... | collective-permute-start | bytes 221192 | tf_op jit(solution)/shard_map/ppermute | solution.py:16
  124.3 7.8 %collective-permute-start.35 = (f32[176,128]{1,0:T(8,128)S(1)}, f32[176,128]{1,0:T(8,128)S(1)}, u32[]{:S(2)}, u32[]{:S(2)}) collective-permute-start(f32[176,128]{1,0:T(8,128)S(1)} %get-tuple-element.117.own), channel_id=1, source_target_pairs={{0,1},{1,0},{2,3},{3,2},{4,5},{5,4},{6,7},{7,6},{8,9},{9,8},{10,11... | collective-permute-start | bytes 270344 | tf_op jit(solution)/shard_map/ppermute | solution.py:16
  132.2 4.8 %collective-permute-start.36 = (f32[208,128]{1,0:T(8,128)S(1)}, f32[208,128]{1,0:T(8,128)S(1)}, u32[]{:S(2)}, u32[]{:S(2)}) collective-permute-start(f32[208,128]{1,0:T(8,128)S(1)} %fold.10.own), channel_id=1, source_target_pairs={{0,2},{1,3},{2,0},{3,1},{4,6},{5,7},{6,4},{7,5},{8,10},{9,11},{10,... | collective-permute-start | bytes 319496 | tf_op jit(solution)/shard_map/ppermute | solution.py:16
  136.9 8.2 %collective-permute-start.37 = (f32[272,128]{1,0:T(8,128)S(1)}, f32[272,128]{1,0:T(8,128)S(1)}, u32[]{:S(2)}, u32[]{:S(2)}) collective-permute-start(f32[272,128]{1,0:T(8,128)S(1)} %fold.11.own), channel_id=1, source_target_pairs={{0,4},{1,5},{2,6},{3,7},{4,0},{5,1},{6,2},{7,3},{8,12},{9,13},{10,... | collective-permute-start | bytes 417800 | tf_op jit(solution)/shard_map/ppermute | solution.py:16
  146.2 6.0 %collective-permute-start.40 = (f32[400,128]{1,0:T(8,128)S(1)}, f32[400,128]{1,0:T(8,128)S(1)}, u32[]{:S(2)}, u32[]{:S(2)}) collective-permute-start(f32[400,128]{1,0:T(8,128)S(1)} %get-tuple-element.123.refs_2_), channel_id=1, source_target_pairs={{0,8},{16,24},{8,0},{24,16},{1,9},{17,25},{9,1},{25,17},{2,10},{18... | collective-permute-start | bytes 614408 | tf_op jit(solution)/shard_map/ppermute | solution.py:415
  146.3 5.9 %collective-permute-start.38 = (f32[256,128]{1,0:T(8,128)S(1)}, f32[256,128]{1,0:T(8,128)S(1)}, u32[]{:S(2)}, u32[]{:S(2)}) collective-permute-start(f32[256,128]{1,0:T(8,128)S(1)} %get-tuple-element.125), channel_id=1, source_target_pairs={{0,1},{2,3},{4,5},{6,7},{1,0},{3,2},{5,4},{7,6},{8,9},{10,11},{12,... | collective-permute-start | bytes 393224 | tf_op jit(solution)/shard_map/ppermute | solution.py:415
  147.2 5.1 %collective-permute-start.39 = (f32[256,128]{1,0:T(8,128)S(1)}, f32[256,128]{1,0:T(8,128)S(1)}, u32[]{:S(2)}, u32[]{:S(2)}) collective-permute-start(f32[256,128]{1,0:T(8,128)S(1)} %get-tuple-element.126), channel_id=1, source_target_pairs={{1,2},{3,4},{5,6},{2,1},{4,3},{6,5},{9,10},{11,12},{13,14},{10,9},... | collective-permute-start | bytes 393224 | tf_op jit(solution)/shard_map/ppermute | solution.py:415
  147.9 4.4 %collective-permute-start.41 = (f32[256,128]{1,0:T(8,128)S(1)}, f32[256,128]{1,0:T(8,128)S(1)}, u32[]{:S(2)}, u32[]{:S(2)}) collective-permute-start(f32[256,128]{1,0:T(8,128)S(1)} %get-tuple-element.124.refs_3_), channel_id=1, source_target_pairs={{8,16},{16,8},{9,17},{17,9},{10,18},{18,10},{11,19},{19,11},{12,20... | collective-permute-start | bytes 393224 | tf_op jit(solution)/shard_map/ppermute | solution.py:415
  153.8 13.9 %collective-permute-start.43 = (f32[256,128]{1,0:T(8,128)S(1)}, f32[256,128]{1,0:T(8,128)S(1)}, u32[]{:S(2)}, u32[]{:S(2)}) collective-permute-start(f32[256,128]{1,0:T(8,128)S(1)} %get-tuple-element.135.refs_0_), channel_id=1, source_target_pairs={{0,1},{2,3},{4,5},{6,7},{1,0},{3,2},{5,4},{7,6},{8,9},{10,11},{12,... | collective-permute-start | bytes 393224 | tf_op jit(solution)/shard_map/ppermute | solution.py:415
  158.4 9.3 %collective-permute-start.44 = (f32[256,128]{1,0:T(8,128)S(1)}, f32[256,128]{1,0:T(8,128)S(1)}, u32[]{:S(2)}, u32[]{:S(2)}) collective-permute-start(f32[256,128]{1,0:T(8,128)S(1)} %get-tuple-element.136.refs_1_), channel_id=1, source_target_pairs={{1,2},{3,4},{5,6},{2,1},{4,3},{6,5},{9,10},{11,12},{13,14},{10,9},... | collective-permute-start | bytes 393224 | tf_op jit(solution)/shard_map/ppermute | solution.py:415
  159.1 8.6 %collective-permute-start.45 = (f32[256,128]{1,0:T(8,128)S(1)}, f32[256,128]{1,0:T(8,128)S(1)}, u32[]{:S(2)}, u32[]{:S(2)}) collective-permute-start(f32[256,128]{1,0:T(8,128)S(1)} %get-tuple-element.137.refs_2_), channel_id=1, source_target_pairs={{0,8},{16,24},{8,0},{24,16},{1,9},{17,25},{9,1},{25,17},{2,10},{18... | collective-permute-start | bytes 393224 | tf_op jit(solution)/shard_map/ppermute | solution.py:415
  159.2 8.6 %collective-permute-start.46 = (f32[256,128]{1,0:T(8,128)S(1)}, f32[256,128]{1,0:T(8,128)S(1)}, u32[]{:S(2)}, u32[]{:S(2)}) collective-permute-start(f32[256,128]{1,0:T(8,128)S(1)} %get-tuple-element.138.refs_3_), channel_id=1, source_target_pairs={{8,16},{16,8},{9,17},{17,9},{10,18},{18,10},{11,19},{19,11},{12,20... | collective-permute-start | bytes 393224 | tf_op jit(solution)/shard_map/ppermute | solution.py:415
  160.1 7.6 %collective-permute-start.42 = (f32[144,128]{1,0:T(8,128)S(1)}, f32[144,128]{1,0:T(8,128)S(1)}, u32[]{:S(2)}, u32[]{:S(2)}) collective-permute-start(f32[144,128]{1,0:T(8,128)S(1)} %get-tuple-element.127), channel_id=1, source_target_pairs={{0,16},{8,24},{16,0},{24,8},{1,17},{9,25},{17,1},{25,9},{2,18},{10... | collective-permute-start | bytes 221192 | tf_op jit(solution)/shard_map/ppermute | solution.py:16
  174.4 1.3 collective-permute-start.47
  175.7 5.5 %collective-permute-start.48 = (f32[72,128]{1,0:T(8,128)S(1)}, f32[72,128]{1,0:T(8,128)S(1)}, u32[]{:S(2)}, u32[]{:S(2)}) collective-permute-start(f32[72,128]{1,0:T(8,128)S(1)} %add.49), channel_id=1, source_target_pairs={{0,1},{1,0},{2,3},{3,2},{4,5},{5,4},{6,7},{7,6},{8,9},{9,8},{10,11... | collective-permute-start | bytes 110600 | tf_op jit(solution)/shard_map/ppermute | solution.py:16
  181.2 5.1 %collective-permute-start.49 = (f32[72,128]{1,0:T(8,128)S(1)}, f32[72,128]{1,0:T(8,128)S(1)}, u32[]{:S(2)}, u32[]{:S(2)}) collective-permute-start(f32[72,128]{1,0:T(8,128)S(1)} %add.50), channel_id=1, source_target_pairs={{0,16},{8,24},{16,0},{24,8},{1,17},{9,25},{17,1},{25,9},{2,18},{10... | collective-permute-start | bytes 110600 | tf_op jit(solution)/shard_map/ppermute | solution.py:16
  186.3 4.7 %collective-permute-start.50 = (f32[72,128]{1,0:T(8,128)S(1)}, f32[72,128]{1,0:T(8,128)S(1)}, u32[]{:S(2)}, u32[]{:S(2)}) collective-permute-start(f32[72,128]{1,0:T(8,128)S(1)} %add.51), channel_id=1, source_target_pairs={{0,2},{1,3},{2,0},{3,1},{4,6},{5,7},{6,4},{7,5},{8,10},{9,11},{10,... | collective-permute-start | bytes 110600 | tf_op jit(solution)/shard_map/ppermute | solution.py:16
  191.0 4.9 %collective-permute-start.51 = (f32[72,128]{1,0:T(8,128)S(1)}, f32[72,128]{1,0:T(8,128)S(1)}, u32[]{:S(2)}, u32[]{:S(2)}) collective-permute-start(f32[72,128]{1,0:T(8,128)S(1)} %add.52), channel_id=1, source_target_pairs={{0,4},{1,5},{2,6},{3,7},{4,0},{5,1},{6,2},{7,3},{8,12},{9,13},{10,... | collective-permute-start | bytes 110600 | tf_op jit(solution)/shard_map/ppermute | solution.py:16
  195.8 1.2 collective-permute-start.52

commit v2 on v1

--- a/solution.py
+++ b/solution.py
@@ -35,10 +35,14 @@
     return half, swap(half, "group", 1), ride
 
 
-def gather_sub(x):
-    for bit in bits_of("sub"):
-        x = jnp.concatenate([x, swap(x, "sub", bit)], axis=0)
-    return x
+def gather_sub(x, *rides):
+    rides = list(rides)
+    for number, bit in enumerate(bits_of("sub")):
+        arrived = swap(x, "sub", bit)
+        if number < len(rides):
+            arrived, rides[number] = lax.optimization_barrier((arrived, rides[number]))
+        x = jnp.concatenate([x, arrived], axis=0)
+    return x, rides
 
 
 def eliminate(matrix, block, tile=8):
@@ -459,13 +463,19 @@
     )
     subs = lax.axis_size("sub")
     inverse_rows = coarse_inverse[0]
+    maps, (rhs_slots, (received[0], received[2]), (received[1], received[3], weight)) = gather_sub(
+        coarse_map[0, 0],
+        rhs_slots,
+        (received[0], received[2]),
+        (received[1], received[3], weight),
+    )
     (chosen,) = call(
         choice_kernel,
         "selected_inverse",
         product_flops // 4,
         [((subs, modes, subs * modes), jnp.bfloat16)],
         (lax.axis_index("sub") * inverse_rows.shape[0]).astype(jnp.int32)[None],
-        gather_sub(coarse_map[0, 0])[None],
+        maps[None],
         inverse_rows,
     )
     for bit in reversed(bits_of("sub")):
@@ -499,11 +509,13 @@
         )
         early = exchange(early)
         bits = bits_of("sub")
-        for bit in bits[:-1]:
+        for number, bit in enumerate(bits[:-1]):
             rows_out = 2 * carried.shape[0] - grams
             arrived = swap(carried, "sub", bit)
-            if ride is not None and bit == bits[0]:
+            if ride is not None and number == 0:
                 arrived, ride = lax.optimization_barrier((arrived, ride))
+            if number == 1:
+                arrived, early[0] = lax.optimization_barrier((arrived, early[0]))
             (carried,) = call(
                 functools.partial(fold_kernel, grams),
                 "fold",
@@ -512,6 +524,7 @@
                 carried,
                 arrived,
             )
+        arrived, early = lax.optimization_barrier((swap(carried, "sub", bits[-1]), early))
         slots = call(
             functools.partial(finish_kernel, grams),
             "coarse_part",
@@ -524,7 +537,7 @@
             near,
             local,
             carried,
-            swap(carried, "sub", bits[-1]),
+            arrived,
         )
         return slots, early + exchange(slots[2:], 2), ride
 

time: 205 us -> 201 us (0.980)
  waiting for transfers between devices: 51.3 us -> 45.5 us
  local copies, waits for them, and re-layouts: 5.99 us -> 8.27 us
    ppermute x30, waiting for transfers between devices: 8.3 us -> 5.06 us  [exchange(): lax.ppermute(slot, axis, pairs(axis, low))]
    ppermute x30, starting transfers between devices: 45.6 us -> 42.6 us  [exchange(): lax.ppermute(slot, axis, pairs(axis, low))]
    ppermute x23, waiting for transfers between devices: 43 us -> 40.4 us  [swap(): lax.ppermute(x, axis, [(i, i ^ bit) for i in range(lax.axis_size(axis))])]
    unnamed x22 -> x26, local copies, waits for them, and re-layouts: 5.97 us -> 7.65 us
  transfers between devices with their start and end apart: 53 -> 53, of which waited for: 22 -> 19; matrix products, arithmetic and copies ran while one was open for 0% -> 1% of each run, Pallas kernels for 8% -> 8%
where the time goes in v2:
time: 201 us
  starting transfers between devices  95.3 us (47%)
  Pallas kernels  46.6 us (23%)
  waiting for transfers between devices  45.5 us (23%)
  local copies, waits for them, and re-layouts  8.27 us (4%)
  other arithmetic  3.7 us (2%)
    ppermute x23, starting transfers between devices, swap(): lax.ppermute(x, axis, [(i, i ^ bit) for i in range(lax.axis_size(axis))])  52.8 us
    pallas_call x26, Pallas kernels, call(): pl.pallas_call(kernel, out_shape=shapes, in_specs=[SMEM if a.ndim == 1 el...  46.6 us
    ppermute x30, starting transfers between devices, exchange(): lax.ppermute(slot, axis, pairs(axis, low))  42.6 us
    ppermute x23, waiting for transfers between devices, swap(): lax.ppermute(x, axis, [(i, i ^ bit) for i in range(lax.axis_size(axis))])  40.4 us
    unnamed x26, local copies, waits for them, and re-layouts  7.65 us
    ppermute x30, waiting for transfers between devices, exchange(): lax.ppermute(slot, axis, pairs(axis, low))  5.06 us
  transfers between devices with their start and end apart: 53, of which 19 were waited for; matrix products, arithmetic and copies ran while one was open for 1% of the time, Pallas kernels for 8%

profile of v2, /device:TPU:0, one launch (start us, length us, event | category | flops | bytes accessed | tf_op | source)
XLA Modules:
  0.0 200.5 jit_solution(18339679991157570538)
XLA Ops:
  0.6 3.0 %collective-permute-start = (s32[32]{0:T(128)}, s32[32]{0:T(128)S(1)}, u32[]{:S(2)}, u32[]{:S(2)}) collective-permute-start(s32[32]{0:T(128)} %bitcast.37), channel_id=1, source_target_pairs={{0,1},{1,0},{2,3},{3,2},{4,5},{5,4},{6,7},{7,6},{8,9},{9,8},{10,11... | collective-permute-start | bytes 392 | tf_op jit(solution)/shard_map/ppermute | solution.py:16
  4.6 0.9 copy-done.4
  5.5 1.2 first_zones.1
  8.3 1.9 collective-permute-start.1
  10.2 1.3 collective-permute-start.6
  12.8 1.2 pad_add_fusion.3
  14.0 4.1 %collective-permute-start.4 = (s32[128]{0:T(128)}, s32[128]{0:T(128)S(1)}, u32[]{:S(2)}, u32[]{:S(2)}) collective-permute-start(s32[128]{0:T(128)} %pad_add_fusion.3), channel_id=1, source_target_pairs={{0,4},{1,5},{2,6},{3,7},{4,0},{5,1},{6,2},{7,3},{8,12},{9,13},{10,... | collective-permute-start | bytes 1544 | tf_op jit(solution)/shard_map/ppermute | solution.py:16
  19.5 1.2 shared_row_tables.1
  21.5 0.9 copy-done.9
  23.2 2.1 %collective-permute-start.7 = (bf16[4,32,256]{2,1,0:T(8,128)(2,1)S(1)}, bf16[4,32,256]{2,1,0:T(8,128)(2,1)S(1)}, u32[]{:S(2)}, u32[]{:S(2)}) collective-permute-start(bf16[4,32,256]{2,1,0:T(8,128)(2,1)S(1)} %slice.25), channel_id=1, source_target_pairs={{0,4},{1,5},{2,6},{3,7},{4,0},{5,1},{6,2},{7,3},{8,12},{9,13},{10,... | collective-permute-start | bytes 196616 | tf_op jit(solution)/shard_map/ppermute | solution.py:16
  25.2 3.2 %collective-permute-done.7 = bf16[4,32,256]{2,1,0:T(8,128)(2,1)S(1)} collective-permute-done((bf16[4,32,256]{2,1,0:T(8,128)(2,1)S(1)}, bf16[4,32,256]{2,1,0:T(8,128)(2,1)S(1)}, u32[]{:S(2)}, u32[]{:S(2)}) %collective-permute-start.7) | collective-permute-done | bytes 65568 | tf_op jit(solution)/shard_map/ppermute | solution.py:16
  29.6 2.7 %collective-permute-start.8 = (bf16[2,32,256]{2,1,0:T(8,128)(2,1)}, bf16[2,32,256]{2,1,0:T(8,128)(2,1)}, u32[]{:S(2)}, u32[]{:S(2)}) collective-permute-start(bf16[2,32,256]{2,1,0:T(8,128)(2,1)} %slice.27), channel_id=1, source_target_pairs={{0,2},{1,3},{2,0},{3,1},{4,6},{5,7},{6,4},{7,5},{8,10},{9,11},{10,... | collective-permute-start | bytes 98312 | tf_op jit(solution)/shard_map/ppermute | solution.py:16
  34.0 1.4 start.1
  35.4 1.6 collective-permute-start.12
  38.4 1.3 local_inverse.3
  39.7 1.6 collective-permute-start.14
  42.0 3.2 %collective-permute-start.13 = (f32[64,128]{1,0:T(8,128)S(1)}, f32[64,128]{1,0:T(8,128)S(1)}, u32[]{:S(2)}, u32[]{:S(2)}) collective-permute-start(f32[64,128]{1,0:T(8,128)S(1)} %fold.6.own), channel_id=1, source_target_pairs={{0,2},{1,3},{2,0},{3,1},{4,6},{5,7},{6,4},{7,5},{8,10},{9,11},{10,... | collective-permute-start | bytes 98312 | tf_op jit(solution)/shard_map/ppermute | solution.py:16
  45.9 3.7 %collective-permute-start.10 = (bf16[32,256]{1,0:T(8,128)(2,1)S(1)}, bf16[32,256]{1,0:T(8,128)(2,1)S(1)}, u32[]{:S(2)}, u32[]{:S(2)}) collective-permute-start(bf16[32,256]{1,0:T(8,128)(2,1)S(1)} %fusion.chosen), channel_id=1, source_target_pairs={{0,1},{2,3},{4,5},{6,7},{1,0},{3,2},{5,4},{7,6},{8,9},{10,11},{12,... | collective-permute-start | bytes 49160 | tf_op jit(solution)/shard_map/ppermute | solution.py:419
  49.6 1.7 collective-permute-start.15
  52.2 2.6 %collective-permute-done.15.received = f32[128,128]{1,0:T(8,128)S(1)} collective-permute-done((f32[128,128]{1,0:T(8,128)S(1)}, f32[128,128]{1,0:T(8,128)S(1)}, u32[]{:S(2)}, u32[]{:S(2)}) %collective-permute-start.15) | collective-permute-done | bytes 65568 | tf_op jit(solution)/shard_map/ppermute | solution.py:16
  54.8 1.1 coarse_part.3
  57.3 1.6 operator.3
  60.2 5.5 %collective-permute-start.21 = (f32[256,128]{1,0:T(8,128)S(1)}, f32[256,128]{1,0:T(8,128)S(1)}, u32[]{:S(2)}, u32[]{:S(2)}) collective-permute-start(f32[256,128]{1,0:T(8,128)S(1)} %get-tuple-element.142.refs_2_), channel_id=1, source_target_pairs={{0,8},{16,24},{8,0},{24,16},{1,9},{17,25},{9,1},{25,17},{2,10},{18... | collective-permute-start | bytes 393224 | tf_op jit(solution)/shard_map/ppermute | solution.py:419
  66.7 1.5 start_grams.1
  68.2 5.4 %collective-permute-start.23 = (f32[176,128]{1,0:T(8,128)S(1)}, f32[176,128]{1,0:T(8,128)S(1)}, u32[]{:S(2)}, u32[]{:S(2)}) collective-permute-start(f32[176,128]{1,0:T(8,128)S(1)} %get-tuple-element.146.own), channel_id=1, source_target_pairs={{0,1},{1,0},{2,3},{3,2},{4,5},{5,4},{6,7},{7,6},{8,9},{9,8},{10,11... | collective-permute-start | bytes 270344 | tf_op jit(solution)/shard_map/ppermute | solution.py:16
  73.6 1.3 local_inverse.4
  75.0 1.2 collective-permute-done.23.received
  77.1 2.9 %collective-permute-done.25.refs_4_ = f32[256,128]{1,0:T(8,128)S(1)} collective-permute-done((f32[256,128]{1,0:T(8,128)S(1)}, f32[256,128]{1,0:T(8,128)S(1)}, u32[]{:S(2)}, u32[]{:S(2)}) %collective-permute-start.25) | collective-permute-done | bytes 131104 | tf_op jit(solution)/shard_map/ppermute | solution.py:419
  79.9 1.0 collective-permute-done.24.received
  80.9 2.3 %collective-permute-start.26 = (f32[272,128]{1,0:T(8,128)S(1)}, f32[272,128]{1,0:T(8,128)S(1)}, u32[]{:S(2)}, u32[]{:S(2)}) collective-permute-start(f32[272,128]{1,0:T(8,128)S(1)} %fold.9.own), channel_id=1, source_target_pairs={{0,4},{1,5},{2,6},{3,7},{4,0},{5,1},{6,2},{7,3},{8,12},{9,13},{10,... | collective-permute-start | bytes 417800 | tf_op jit(solution)/shard_map/ppermute | solution.py:16
  83.9 6.1 %collective-permute-done.26.received = f32[272,128]{1,0:T(8,128)S(1)} collective-permute-done((f32[272,128]{1,0:T(8,128)S(1)}, f32[272,128]{1,0:T(8,128)S(1)}, u32[]{:S(2)}, u32[]{:S(2)}) %collective-permute-start.26) | collective-permute-done | bytes 139296 | tf_op jit(solution)/shard_map/ppermute | solution.py:16
  90.0 1.1 coarse_part.4
  91.1 2.8 %collective-permute-start.28 = (f32[400,128]{1,0:T(8,128)S(1)}, f32[400,128]{1,0:T(8,128)S(1)}, u32[]{:S(2)}, u32[]{:S(2)}) collective-permute-start(f32[400,128]{1,0:T(8,128)S(1)} %get-tuple-element.154.refs_2_), channel_id=1, source_target_pairs={{0,8},{16,24},{8,0},{24,16},{1,9},{17,25},{9,1},{25,17},{2,10},{18... | collective-permute-start | bytes 614408 | tf_op jit(solution)/shard_map/ppermute | solution.py:419
  95.0 1.6 operator.4
  96.6 1.7 collective-permute-start.31
  99.0 7.3 %collective-permute-start.33 = (f32[256,128]{1,0:T(8,128)S(1)}, f32[256,128]{1,0:T(8,128)S(1)}, u32[]{:S(2)}, u32[]{:S(2)}) collective-permute-start(f32[256,128]{1,0:T(8,128)S(1)} %get-tuple-element.162.refs_2_), channel_id=1, source_target_pairs={{0,8},{16,24},{8,0},{24,16},{1,9},{17,25},{9,1},{25,17},{2,10},{18... | collective-permute-start | bytes 393224 | tf_op jit(solution)/shard_map/ppermute | solution.py:419
  107.1 3.2 %collective-permute-start.30 = (f32[144,128]{1,0:T(8,128)S(1)}, f32[144,128]{1,0:T(8,128)S(1)}, u32[]{:S(2)}, u32[]{:S(2)}) collective-permute-start(f32[144,128]{1,0:T(8,128)S(1)} %get-tuple-element.158), channel_id=1, source_target_pairs={{0,16},{8,24},{16,0},{24,8},{1,17},{9,25},{17,1},{25,9},{2,18},{10... | collective-permute-start | bytes 221192 | tf_op jit(solution)/shard_map/ppermute | solution.py:16
  110.4 4.2 %collective-permute-done.30 = f32[144,128]{1,0:T(8,128)S(1)} collective-permute-done((f32[144,128]{1,0:T(8,128)S(1)}, f32[144,128]{1,0:T(8,128)S(1)}, u32[]{:S(2)}, u32[]{:S(2)}) %collective-permute-start.30) | collective-permute-done | bytes 73760 | tf_op jit(solution)/shard_map/ppermute | solution.py:16
  114.6 6.7 %first_update.1 = (f32[1024,128]{1,0:T(8,128)S(1)}, f32[1024,128]{1,0:T(8,128)S(1)}, f32[1024,128]{1,0:T(8,128)S(1)}, f32[1024,128]{1,0:T(8,128)S(1)}, f32[1024,...) custom-call(s32[2]{0:T(128)S(1)} %pad_add_fusion.1.parity, ...), custom_call_target="tpu_custom_call" | custom-call | flops 800000000 | bytes 7110664 | tf_op jit(solution)/shard_map/first_update/pallas_call | solution.py:399
  121.3 3.5 %collective-permute-start.35 = (f32[176,128]{1,0:T(8,128)S(1)}, f32[176,128]{1,0:T(8,128)S(1)}, u32[]{:S(2)}, u32[]{:S(2)}) collective-permute-start(f32[176,128]{1,0:T(8,128)S(1)} %get-tuple-element.166.own), channel_id=1, source_target_pairs={{0,1},{1,0},{2,3},{3,2},{4,5},{5,4},{6,7},{7,6},{8,9},{9,8},{10,11... | collective-permute-start | bytes 270344 | tf_op jit(solution)/shard_map/ppermute | solution.py:16
  124.8 1.3 local_inverse.5
  126.1 3.9 %inner_inverse.2 = f32[128,128]{1,0:T(8,128)S(1)} custom-call(f32[144,128]{1,0:T(8,128)S(1)} %add.47.grams), custom_call_target="tpu_custom_call" | custom-call | flops 400000000 | bytes 139264 | tf_op jit(solution)/shard_map/inner_inverse/pallas_call | solution.py:399
  130.1 1.7 collective-permute-start.36
  131.8 3.1 %collective-permute-done.36.received = f32[208,128]{1,0:T(8,128)S(1)} collective-permute-done((f32[208,128]{1,0:T(8,128)S(1)}, f32[208,128]{1,0:T(8,128)S(1)}, u32[]{:S(2)}, u32[]{:S(2)}) %collective-permute-start.36) | collective-permute-done | bytes 106528 | tf_op jit(solution)/shard_map/ppermute | solution.py:16
  134.9 3.0 %collective-permute-start.38 = (f32[272,128]{1,0:T(8,128)S(1)}, f32[272,128]{1,0:T(8,128)S(1)}, u32[]{:S(2)}, u32[]{:S(2)}) collective-permute-start(f32[272,128]{1,0:T(8,128)S(1)} %fold.11.own), channel_id=1, source_target_pairs={{0,4},{1,5},{2,6},{3,7},{4,0},{5,1},{6,2},{7,3},{8,12},{9,13},{10,... | collective-permute-start | bytes 417800 | tf_op jit(solution)/shard_map/ppermute | solution.py:16
  138.5 5.5 %collective-permute-done.38.received = f32[272,128]{1,0:T(8,128)S(1)} collective-permute-done((f32[272,128]{1,0:T(8,128)S(1)}, f32[272,128]{1,0:T(8,128)S(1)}, u32[]{:S(2)}, u32[]{:S(2)}) %collective-permute-start.38) | collective-permute-done | bytes 139296 | tf_op jit(solution)/shard_map/ppermute | solution.py:16
  144.0 1.1 coarse_part.5
  146.6 1.6 operator.5
  148.2 2.5 %collective-permute-start.43 = (f32[256,128]{1,0:T(8,128)S(1)}, f32[256,128]{1,0:T(8,128)S(1)}, u32[]{:S(2)}, u32[]{:S(2)}) collective-permute-start(f32[256,128]{1,0:T(8,128)S(1)} %get-tuple-element.189.refs_0_), channel_id=1, source_target_pairs={{0,1},{2,3},{4,5},{6,7},{1,0},{3,2},{5,4},{7,6},{8,9},{10,11},{12,... | collective-permute-start | bytes 393224 | tf_op jit(solution)/shard_map/ppermute | solution.py:419
  151.3 5.4 %collective-permute-start.45 = (f32[256,128]{1,0:T(8,128)S(1)}, f32[256,128]{1,0:T(8,128)S(1)}, u32[]{:S(2)}, u32[]{:S(2)}) collective-permute-start(f32[256,128]{1,0:T(8,128)S(1)} %get-tuple-element.191.refs_2_), channel_id=1, source_target_pairs={{0,8},{16,24},{8,0},{24,16},{1,9},{17,25},{9,1},{25,17},{2,10},{18... | collective-permute-start | bytes 393224 | tf_op jit(solution)/shard_map/ppermute | solution.py:419
  157.6 3.0 %collective-permute-start.42 = (f32[144,128]{1,0:T(8,128)S(1)}, f32[144,128]{1,0:T(8,128)S(1)}, u32[]{:S(2)}, u32[]{:S(2)}) collective-permute-start(f32[144,128]{1,0:T(8,128)S(1)} %get-tuple-element.181), channel_id=1, source_target_pairs={{0,16},{8,24},{16,0},{24,8},{1,17},{9,25},{17,1},{25,9},{2,18},{10... | collective-permute-start | bytes 221192 | tf_op jit(solution)/shard_map/ppermute | solution.py:16
  160.6 4.2 %collective-permute-done.42 = f32[144,128]{1,0:T(8,128)S(1)} collective-permute-done((f32[144,128]{1,0:T(8,128)S(1)}, f32[144,128]{1,0:T(8,128)S(1)}, u32[]{:S(2)}, u32[]{:S(2)}) %collective-permute-start.42) | collective-permute-done | bytes 73760 | tf_op jit(solution)/shard_map/ppermute | solution.py:16
  164.9 6.7 %next_update.1 = (f32[1024,128]{1,0:T(8,128)S(1)}, f32[1024,128]{1,0:T(8,128)S(1)}, f32[1024,128]{1,0:T(8,128)S(1)}, f32[1024,128]{1,0:T(8,128)S(1)}, f32[1024,1...) custom-call(s32[2]{0:T(128)S(1)} %pad_add_fusion.1.parity, ...), custom_call_target="tpu_custom_call" | custom-call | flops 800000000 | bytes 11419656 | tf_op jit(solution)/shard_map/next_update/pallas_call | solution.py:399
  171.6 1.2 collective-permute-done.47
  172.8 3.9 %collective-permute-start.48 = (f32[72,128]{1,0:T(8,128)S(1)}, f32[72,128]{1,0:T(8,128)S(1)}, u32[]{:S(2)}, u32[]{:S(2)}) collective-permute-start(f32[72,128]{1,0:T(8,128)S(1)} %add.49), channel_id=1, source_target_pairs={{0,1},{1,0},{2,3},{3,2},{4,5},{5,4},{6,7},{7,6},{8,9},{9,8},{10,11... | collective-permute-start | bytes 110600 | tf_op jit(solution)/shard_map/ppermute | solution.py:16
  176.7 1.9 collective-permute-done.48
  178.6 1.1 collective-permute-start.49
  179.7 3.9 %inner_inverse.3 = f32[128,128]{1,0:T(8,128)S(1)} custom-call(f32[144,128]{1,0:T(8,128)S(1)} %add.48.grams), custom_call_target="tpu_custom_call" | custom-call | flops 400000000 | bytes 139264 | tf_op jit(solution)/shard_map/inner_inverse/pallas_call | solution.py:399
  183.7 1.3 collective-permute-start.50
  184.9 2.8 %collective-permute-done.50 = f32[72,128]{1,0:T(8,128)S(1)} collective-permute-done((f32[72,128]{1,0:T(8,128)S(1)}, f32[72,128]{1,0:T(8,128)S(1)}, u32[]{:S(2)}, u32[]{:S(2)}) %collective-permute-start.50) | collective-permute-done | bytes 36896 | tf_op jit(solution)/shard_map/ppermute | solution.py:16
  187.7 2.5 %collective-permute-start.51 = (f32[72,128]{1,0:T(8,128)S(1)}, f32[72,128]{1,0:T(8,128)S(1)}, u32[]{:S(2)}, u32[]{:S(2)}) collective-permute-start(f32[72,128]{1,0:T(8,128)S(1)} %add.52), channel_id=1, source_target_pairs={{0,4},{1,5},{2,6},{3,7},{4,0},{5,1},{6,2},{7,3},{8,12},{9,13},{10,... | collective-permute-start | bytes 110600 | tf_op jit(solution)/shard_map/ppermute | solution.py:16
  190.2 2.3 %collective-permute-done.51 = f32[72,128]{1,0:T(8,128)S(1)} collective-permute-done((f32[72,128]{1,0:T(8,128)S(1)}, f32[72,128]{1,0:T(8,128)S(1)}, u32[]{:S(2)}, u32[]{:S(2)}) %collective-permute-start.51) | collective-permute-done | bytes 36896 | tf_op jit(solution)/shard_map/ppermute | solution.py:16
  192.6 1.2 collective-permute-done.52.other
  193.8 6.8 %last_update.1 = (f32[1024,128]{1,0:T(8,128)}, f32[1024,128]{1,0:T(8,128)}) custom-call(s32[2]{0:T(128)S(1)} %pad_add_fusion.1.parity, f32[72,128]{1,0:T(8,128)S(1)} %add.53.half, f32[72,128]{1,0:T(8,128)S(1)} %collective-permute-done.52.other, f32[128,128]{1,0:T(8,128)S(1)} %inner_inverse.3, f32[128,128]{1,0:T(8,128)S(1)} %get-tuple-element.199.curvature, ...), custom_call_target="tpu_custom_call" | custom-call | flops 800000000 | bytes 4399112 | tf_op jit(solution)/shard_map/last_update/pallas_call | solution.py:399
  (112 shorter events, 24.7 us)
Async XLA Ops:
  0.6 37.8 %copy-start = (bf16[1,1,1024,1024]{3,2,1,0:T(8,128)(2,1)S(1)}, bf16[1,1,1024,1024]{3,2,1,0:T(8,128)(2,1)}, u32[]{:S(2)}) copy-start(bf16[1,1,1024,1024]{3,2,1,0:T(8,128)(2,1)} %param.9) | copy-start | bytes 6291460
  0.6 6.9 %collective-permute-start = (s32[32]{0:T(128)}, s32[32]{0:T(128)S(1)}, u32[]{:S(2)}, u32[]{:S(2)}) collective-permute-start(s32[32]{0:T(128)} %bitcast.37), channel_id=1, source_target_pairs={{0,1},{1,0},{2,3},{3,2},{4,5},{5,4},{6,7},{7,6},{8,9},{9,8},{10,11... | collective-permute-start | bytes 392 | tf_op jit(solution)/shard_map/ppermute | solution.py:16
  3.7 0.8 copy-start.2
  4.6 0.9 copy-start.4
  5.5 26.8 %copy-start.3 = (bf16[1,1,32,1024]{3,2,1,0:T(8,128)(2,1)S(1)}, bf16[1,1,32,1024]{3,2,1,0:T(8,128)(2,1)}, u32[]{:S(2)}) copy-start(bf16[1,1,32,1024]{3,2,1,0:T(8,128)(2,1)} %param.11) | copy-start | bytes 196612
  6.8 5.4 %collective-permute-start.3 = (bf16[256,128]{1,0:T(8,128)(2,1)S(1)}, bf16[256,128]{1,0:T(8,128)(2,1)S(1)}, u32[]{:S(2)}, u32[]{:S(2)}) collective-permute-start(bf16[256,128]{1,0:T(8,128)(2,1)S(1)} %get-tuple-element.121.refs_2_), channel_id=1, source_target_pairs={{0,8},{16,24},{8,0},{24,16},{1,9},{17,25},{9,1},{25,17},{2,10},{18... | collective-permute-start | bytes 196616 | tf_op jit(solution)/shard_map/ppermute | solution.py:419
  7.4 5.4 %collective-permute-start.2 = (bf16[320,128]{1,0:T(8,128)(2,1)S(1)}, bf16[320,128]{1,0:T(8,128)(2,1)S(1)}, u32[]{:S(2)}, u32[]{:S(2)}) collective-permute-start(bf16[320,128]{1,0:T(8,128)(2,1)S(1)} %get-tuple-element.119.refs_0_), channel_id=1, source_target_pairs={{0,1},{2,3},{4,5},{6,7},{1,0},{3,2},{5,4},{7,6},{8,9},{10,11},{12,... | collective-permute-start | bytes 245768 | tf_op jit(solution)/shard_map/ppermute | solution.py:419
  8.3 3.9 %collective-permute-start.1 = (s32[64]{0:T(128)S(1)}, s32[64]{0:T(128)S(1)}, u32[]{:S(2)}, u32[]{:S(2)}) collective-permute-start(s32[64]{0:T(128)S(1)} %pad_add_fusion.2), channel_id=1, source_target_pairs={{0,2},{1,3},{2,0},{3,1},{4,6},{5,7},{6,4},{7,5},{8,10},{9,11},{10,... | collective-permute-start | bytes 776 | tf_op jit(solution)/shard_map/ppermute | solution.py:16
  10.2 10.6 %collective-permute-start.6 = (bf16[256,128]{1,0:T(8,128)(2,1)}, bf16[256,128]{1,0:T(8,128)(2,1)}, u32[]{:S(2)}, u32[]{:S(2)}) collective-permute-start(bf16[256,128]{1,0:T(8,128)(2,1)} %get-tuple-element.122.refs_3_), channel_id=1, source_target_pairs={{8,16},{16,8},{9,17},{17,9},{10,18},{18,10},{11,19},{19,11},{12,20... | collective-permute-start | bytes 196616 | tf_op jit(solution)/shard_map/ppermute | solution.py:419
  11.5 9.3 %collective-permute-start.5 = (bf16[320,128]{1,0:T(8,128)(2,1)S(1)}, bf16[320,128]{1,0:T(8,128)(2,1)S(1)}, u32[]{:S(2)}, u32[]{:S(2)}) collective-permute-start(bf16[320,128]{1,0:T(8,128)(2,1)S(1)} %get-tuple-element.120.refs_1_), channel_id=1, source_target_pairs={{1,2},{3,4},{5,6},{2,1},{4,3},{6,5},{9,10},{11,12},{13,14},{10,9},... | collective-permute-start | bytes 245768 | tf_op jit(solution)/shard_map/ppermute | solution.py:419
  12.2 0.6 copy-start.7
  14.0 6.7 %collective-permute-start.4 = (s32[128]{0:T(128)}, s32[128]{0:T(128)S(1)}, u32[]{:S(2)}, u32[]{:S(2)}) collective-permute-start(s32[128]{0:T(128)} %pad_add_fusion.3), channel_id=1, source_target_pairs={{0,4},{1,5},{2,6},{3,7},{4,0},{5,1},{6,2},{7,3},{8,12},{9,13},{10,... | collective-permute-start | bytes 1544 | tf_op jit(solution)/shard_map/ppermute | solution.py:16
  18.2 0.7 copy-start.10
  18.9 0.7 copy-start.11
  21.5 1.0 copy-start.9
  23.2 5.2 %collective-permute-start.7 = (bf16[4,32,256]{2,1,0:T(8,128)(2,1)S(1)}, bf16[4,32,256]{2,1,0:T(8,128)(2,1)S(1)}, u32[]{:S(2)}, u32[]{:S(2)}) collective-permute-start(bf16[4,32,256]{2,1,0:T(8,128)(2,1)S(1)} %slice.25), channel_id=1, source_target_pairs={{0,4},{1,5},{2,6},{3,7},{4,0},{5,1},{6,2},{7,3},{8,12},{9,13},{10,... | collective-permute-start | bytes 196616 | tf_op jit(solution)/shard_map/ppermute | solution.py:16
  29.6 7.4 %collective-permute-start.8 = (bf16[2,32,256]{2,1,0:T(8,128)(2,1)}, bf16[2,32,256]{2,1,0:T(8,128)(2,1)}, u32[]{:S(2)}, u32[]{:S(2)}) collective-permute-start(bf16[2,32,256]{2,1,0:T(8,128)(2,1)} %slice.27), channel_id=1, source_target_pairs={{0,2},{1,3},{2,0},{3,1},{4,6},{5,7},{6,4},{7,5},{8,10},{9,11},{10,... | collective-permute-start | bytes 98312 | tf_op jit(solution)/shard_map/ppermute | solution.py:16
  32.3 0.8 copy-start.6
  33.2 0.8 copy-start.8
  35.4 6.5 %collective-permute-start.12 = (f32[32,128]{1,0:T(8,128)S(1)}, f32[32,128]{1,0:T(8,128)S(1)}, u32[]{:S(2)}, u32[]{:S(2)}) collective-permute-start(f32[32,128]{1,0:T(8,128)S(1)} %get-tuple-element.127.own), channel_id=1, source_target_pairs={{0,1},{1,0},{2,3},{3,2},{4,5},{5,4},{6,7},{7,6},{8,9},{9,8},{10,11... | collective-permute-start | bytes 49160 | tf_op jit(solution)/shard_map/ppermute | solution.py:16
  37.9 7.4 %collective-permute-start.9 = (bf16[1,32,256]{2,1,0:T(8,128)(2,1)S(1)}, bf16[1,32,256]{2,1,0:T(8,128)(2,1)S(1)}, u32[]{:S(2)}, u32[]{:S(2)}) collective-permute-start(bf16[1,32,256]{2,1,0:T(8,128)(2,1)S(1)} %slice.29), channel_id=1, source_target_pairs={{0,1},{1,0},{2,3},{3,2},{4,5},{5,4},{6,7},{7,6},{8,9},{9,8},{10,11... | collective-permute-start | bytes 49160 | tf_op jit(solution)/shard_map/ppermute | solution.py:16
  38.4 18.9 %copy-start.1 = (bf16[1,1,1024,1024]{3,2,1,0:T(8,128)(2,1)S(1)}, bf16[1,1,1024,1024]{3,2,1,0:T(8,128)(2,1)}, u32[]{:S(2)}) copy-start(bf16[1,1,1024,1024]{3,2,1,0:T(8,128)(2,1)} %param.8) | copy-start | bytes 6291460
  39.7 9.9 %collective-permute-start.14 = (f32[256,128]{1,0:T(8,128)S(1)}, f32[256,128]{1,0:T(8,128)S(1)}, u32[]{:S(2)}, u32[]{:S(2)}) collective-permute-start(f32[256,128]{1,0:T(8,128)S(1)} %get-tuple-element.128), channel_id=1, source_target_pairs={{0,1},{2,3},{4,5},{6,7},{1,0},{3,2},{5,4},{7,6},{8,9},{10,11},{12,... | collective-permute-start | bytes 393224 | tf_op jit(solution)/shard_map/ppermute | solution.py:419
  41.3 10.9 %collective-permute-start.16 = (f32[256,128]{1,0:T(8,128)S(1)}, f32[256,128]{1,0:T(8,128)S(1)}, u32[]{:S(2)}, u32[]{:S(2)}) collective-permute-start(f32[256,128]{1,0:T(8,128)S(1)} %get-tuple-element.131), channel_id=1, source_target_pairs={{1,2},{3,4},{5,6},{2,1},{4,3},{6,5},{9,10},{11,12},{13,14},{10,9},... | collective-permute-start | bytes 393224 | tf_op jit(solution)/shard_map/ppermute | solution.py:419
  42.0 7.6 %collective-permute-start.13 = (f32[64,128]{1,0:T(8,128)S(1)}, f32[64,128]{1,0:T(8,128)S(1)}, u32[]{:S(2)}, u32[]{:S(2)}) collective-permute-start(f32[64,128]{1,0:T(8,128)S(1)} %fold.6.own), channel_id=1, source_target_pairs={{0,2},{1,3},{2,0},{3,1},{4,6},{5,7},{6,4},{7,5},{8,10},{9,11},{10,... | collective-permute-start | bytes 98312 | tf_op jit(solution)/shard_map/ppermute | solution.py:16
  45.2 6.2 %collective-permute-start.11 = (bf16[32,256]{1,0:T(8,128)(2,1)S(1)}, bf16[32,256]{1,0:T(8,128)(2,1)S(1)}, u32[]{:S(2)}, u32[]{:S(2)}) collective-permute-start(bf16[32,256]{1,0:T(8,128)(2,1)S(1)} %fusion.chosen), channel_id=1, source_target_pairs={{1,2},{3,4},{5,6},{2,1},{4,3},{6,5},{9,10},{11,12},{13,14},{10,9},... | collective-permute-start | bytes 49160 | tf_op jit(solution)/shard_map/ppermute | solution.py:419
  45.9 5.6 %collective-permute-start.10 = (bf16[32,256]{1,0:T(8,128)(2,1)S(1)}, bf16[32,256]{1,0:T(8,128)(2,1)S(1)}, u32[]{:S(2)}, u32[]{:S(2)}) collective-permute-start(bf16[32,256]{1,0:T(8,128)(2,1)S(1)} %fusion.chosen), channel_id=1, source_target_pairs={{0,1},{2,3},{4,5},{6,7},{1,0},{3,2},{5,4},{7,6},{8,9},{10,11},{12,... | collective-permute-start | bytes 49160 | tf_op jit(solution)/shard_map/ppermute | solution.py:419
  49.6 5.2 %collective-permute-start.15 = (f32[128,128]{1,0:T(8,128)S(1)}, f32[128,128]{1,0:T(8,128)S(1)}, u32[]{:S(2)}, u32[]{:S(2)}) collective-permute-start(f32[128,128]{1,0:T(8,128)S(1)} %fold.7.own), channel_id=1, source_target_pairs={{0,4},{1,5},{2,6},{3,7},{4,0},{5,1},{6,2},{7,3},{8,12},{9,13},{10,... | collective-permute-start | bytes 196616 | tf_op jit(solution)/shard_map/ppermute | solution.py:16
  55.9 1.4 collective-permute-start.17
  56.0 1.3 collective-permute-start.18
  58.9 7.4 %collective-permute-start.19 = (f32[256,128]{1,0:T(8,128)S(1)}, f32[256,128]{1,0:T(8,128)S(1)}, u32[]{:S(2)}, u32[]{:S(2)}) collective-permute-start(f32[256,128]{1,0:T(8,128)S(1)} %get-tuple-element.140.refs_0_), channel_id=1, source_target_pairs={{0,1},{2,3},{4,5},{6,7},{1,0},{3,2},{5,4},{7,6},{8,9},{10,11},{12,... | collective-permute-start | bytes 393224 | tf_op jit(solution)/shard_map/ppermute | solution.py:419
  59.5 6.9 %collective-permute-start.20 = (f32[256,128]{1,0:T(8,128)S(1)}, f32[256,128]{1,0:T(8,128)S(1)}, u32[]{:S(2)}, u32[]{:S(2)}) collective-permute-start(f32[256,128]{1,0:T(8,128)S(1)} %get-tuple-element.141.refs_1_), channel_id=1, source_target_pairs={{1,2},{3,4},{5,6},{2,1},{4,3},{6,5},{9,10},{11,12},{13,14},{10,9},... | collective-permute-start | bytes 393224 | tf_op jit(solution)/shard_map/ppermute | solution.py:419
  60.2 6.5 %collective-permute-start.21 = (f32[256,128]{1,0:T(8,128)S(1)}, f32[256,128]{1,0:T(8,128)S(1)}, u32[]{:S(2)}, u32[]{:S(2)}) collective-permute-start(f32[256,128]{1,0:T(8,128)S(1)} %get-tuple-element.142.refs_2_), channel_id=1, source_target_pairs={{0,8},{16,24},{8,0},{24,16},{1,9},{17,25},{9,1},{25,17},{2,10},{18... | collective-permute-start | bytes 393224 | tf_op jit(solution)/shard_map/ppermute | solution.py:419
  65.7 1.0 collective-permute-start.22
  68.2 8.0 %collective-permute-start.23 = (f32[176,128]{1,0:T(8,128)S(1)}, f32[176,128]{1,0:T(8,128)S(1)}, u32[]{:S(2)}, u32[]{:S(2)}) collective-permute-start(f32[176,128]{1,0:T(8,128)S(1)} %get-tuple-element.146.own), channel_id=1, source_target_pairs={{0,1},{1,0},{2,3},{3,2},{4,5},{5,4},{6,7},{7,6},{8,9},{9,8},{10,11... | collective-permute-start | bytes 270344 | tf_op jit(solution)/shard_map/ppermute | solution.py:16
  74.9 5.0 %collective-permute-start.25 = (f32[256,128]{1,0:T(8,128)S(1)}, f32[256,128]{1,0:T(8,128)S(1)}, u32[]{:S(2)}, u32[]{:S(2)}) collective-permute-start(f32[256,128]{1,0:T(8,128)S(1)} %get-tuple-element.147), channel_id=1, source_target_pairs={{0,1},{2,3},{4,5},{6,7},{1,0},{3,2},{5,4},{7,6},{8,9},{10,11},{12,... | collective-permute-start | bytes 393224 | tf_op jit(solution)/shard_map/ppermute | solution.py:419
  76.2 4.8 %collective-permute-start.24 = (f32[208,128]{1,0:T(8,128)S(1)}, f32[208,128]{1,0:T(8,128)S(1)}, u32[]{:S(2)}, u32[]{:S(2)}) collective-permute-start(f32[208,128]{1,0:T(8,128)S(1)} %fold.8.own), channel_id=1, source_target_pairs={{0,2},{1,3},{2,0},{3,1},{4,6},{5,7},{6,4},{7,5},{8,10},{9,11},{10,... | collective-permute-start | bytes 319496 | tf_op jit(solution)/shard_map/ppermute | solution.py:16
  80.9 9.1 %collective-permute-start.26 = (f32[272,128]{1,0:T(8,128)S(1)}, f32[272,128]{1,0:T(8,128)S(1)}, u32[]{:S(2)}, u32[]{:S(2)}) collective-permute-start(f32[272,128]{1,0:T(8,128)S(1)} %fold.9.own), channel_id=1, source_target_pairs={{0,4},{1,5},{2,6},{3,7},{4,0},{5,1},{6,2},{7,3},{8,12},{9,13},{10,... | collective-permute-start | bytes 417800 | tf_op jit(solution)/shard_map/ppermute | solution.py:16
  83.2 0.7 collective-permute-start.27
  91.1 3.9 %collective-permute-start.28 = (f32[400,128]{1,0:T(8,128)S(1)}, f32[400,128]{1,0:T(8,128)S(1)}, u32[]{:S(2)}, u32[]{:S(2)}) collective-permute-start(f32[400,128]{1,0:T(8,128)S(1)} %get-tuple-element.154.refs_2_), channel_id=1, source_target_pairs={{0,8},{16,24},{8,0},{24,16},{1,9},{17,25},{9,1},{25,17},{2,10},{18... | collective-permute-start | bytes 614408 | tf_op jit(solution)/shard_map/ppermute | solution.py:419
  93.9 0.7 collective-permute-start.29
  96.6 18.0 %collective-permute-start.31 = (f32[256,128]{1,0:T(8,128)S(1)}, f32[256,128]{1,0:T(8,128)S(1)}, u32[]{:S(2)}, u32[]{:S(2)}) collective-permute-start(f32[256,128]{1,0:T(8,128)S(1)} %get-tuple-element.160.refs_0_), channel_id=1, source_target_pairs={{0,1},{2,3},{4,5},{6,7},{1,0},{3,2},{5,4},{7,6},{8,9},{10,11},{12,... | collective-permute-start | bytes 393224 | tf_op jit(solution)/shard_map/ppermute | solution.py:419
  98.3 16.3 %collective-permute-start.32 = (f32[256,128]{1,0:T(8,128)S(1)}, f32[256,128]{1,0:T(8,128)S(1)}, u32[]{:S(2)}, u32[]{:S(2)}) collective-permute-start(f32[256,128]{1,0:T(8,128)S(1)} %get-tuple-element.161.refs_1_), channel_id=1, source_target_pairs={{1,2},{3,4},{5,6},{2,1},{4,3},{6,5},{9,10},{11,12},{13,14},{10,9},... | collective-permute-start | bytes 393224 | tf_op jit(solution)/shard_map/ppermute | solution.py:419
  99.0 15.6 %collective-permute-start.33 = (f32[256,128]{1,0:T(8,128)S(1)}, f32[256,128]{1,0:T(8,128)S(1)}, u32[]{:S(2)}, u32[]{:S(2)}) collective-permute-start(f32[256,128]{1,0:T(8,128)S(1)} %get-tuple-element.162.refs_2_), channel_id=1, source_target_pairs={{0,8},{16,24},{8,0},{24,16},{1,9},{17,25},{9,1},{25,17},{2,10},{18... | collective-permute-start | bytes 393224 | tf_op jit(solution)/shard_map/ppermute | solution.py:419
  106.3 8.3 %collective-permute-start.34 = (f32[256,128]{1,0:T(8,128)S(1)}, f32[256,128]{1,0:T(8,128)S(1)}, u32[]{:S(2)}, u32[]{:S(2)}) collective-permute-start(f32[256,128]{1,0:T(8,128)S(1)} %get-tuple-element.163.refs_3_), channel_id=1, source_target_pairs={{8,16},{16,8},{9,17},{17,9},{10,18},{18,10},{11,19},{19,11},{12,20... | collective-permute-start | bytes 393224 | tf_op jit(solution)/shard_map/ppermute | solution.py:419
  107.1 7.4 %collective-permute-start.30 = (f32[144,128]{1,0:T(8,128)S(1)}, f32[144,128]{1,0:T(8,128)S(1)}, u32[]{:S(2)}, u32[]{:S(2)}) collective-permute-start(f32[144,128]{1,0:T(8,128)S(1)} %get-tuple-element.158), channel_id=1, source_target_pairs={{0,16},{8,24},{16,0},{24,8},{1,17},{9,25},{17,1},{25,9},{2,18},{10... | collective-permute-start | bytes 221192 | tf_op jit(solution)/shard_map/ppermute | solution.py:16
  121.3 8.8 %collective-permute-start.35 = (f32[176,128]{1,0:T(8,128)S(1)}, f32[176,128]{1,0:T(8,128)S(1)}, u32[]{:S(2)}, u32[]{:S(2)}) collective-permute-start(f32[176,128]{1,0:T(8,128)S(1)} %get-tuple-element.166.own), channel_id=1, source_target_pairs={{0,1},{1,0},{2,3},{3,2},{4,5},{5,4},{6,7},{7,6},{8,9},{9,8},{10,11... | collective-permute-start | bytes 270344 | tf_op jit(solution)/shard_map/ppermute | solution.py:16
  126.0 5.8 %collective-permute-start.37 = (f32[256,128]{1,0:T(8,128)S(1)}, f32[256,128]{1,0:T(8,128)S(1)}, u32[]{:S(2)}, u32[]{:S(2)}) collective-permute-start(f32[256,128]{1,0:T(8,128)S(1)} %get-tuple-element.170), channel_id=1, source_target_pairs={{0,1},{2,3},{4,5},{6,7},{1,0},{3,2},{5,4},{7,6},{8,9},{10,11},{12,... | collective-permute-start | bytes 393224 | tf_op jit(solution)/shard_map/ppermute | solution.py:419
  130.1 4.8 %collective-permute-start.36 = (f32[208,128]{1,0:T(8,128)S(1)}, f32[208,128]{1,0:T(8,128)S(1)}, u32[]{:S(2)}, u32[]{:S(2)}) collective-permute-start(f32[208,128]{1,0:T(8,128)S(1)} %fold.10.own), channel_id=1, source_target_pairs={{0,2},{1,3},{2,0},{3,1},{4,6},{5,7},{6,4},{7,5},{8,10},{9,11},{10,... | collective-permute-start | bytes 319496 | tf_op jit(solution)/shard_map/ppermute | solution.py:16
  134.9 9.1 %collective-permute-start.38 = (f32[272,128]{1,0:T(8,128)S(1)}, f32[272,128]{1,0:T(8,128)S(1)}, u32[]{:S(2)}, u32[]{:S(2)}) collective-permute-start(f32[272,128]{1,0:T(8,128)S(1)} %fold.11.own), channel_id=1, source_target_pairs={{0,4},{1,5},{2,6},{3,7},{4,0},{5,1},{6,2},{7,3},{8,12},{9,13},{10,... | collective-permute-start | bytes 417800 | tf_op jit(solution)/shard_map/ppermute | solution.py:16
  137.8 0.7 collective-permute-start.39
  145.1 1.5 collective-permute-start.40
  145.2 0.7 collective-permute-start.41
  148.2 16.6 %collective-permute-start.43 = (f32[256,128]{1,0:T(8,128)S(1)}, f32[256,128]{1,0:T(8,128)S(1)}, u32[]{:S(2)}, u32[]{:S(2)}) collective-permute-start(f32[256,128]{1,0:T(8,128)S(1)} %get-tuple-element.189.refs_0_), channel_id=1, source_target_pairs={{0,1},{2,3},{4,5},{6,7},{1,0},{3,2},{5,4},{7,6},{8,9},{10,11},{12,... | collective-permute-start | bytes 393224 | tf_op jit(solution)/shard_map/ppermute | solution.py:419
  150.7 14.2 %collective-permute-start.44 = (f32[256,128]{1,0:T(8,128)S(1)}, f32[256,128]{1,0:T(8,128)S(1)}, u32[]{:S(2)}, u32[]{:S(2)}) collective-permute-start(f32[256,128]{1,0:T(8,128)S(1)} %get-tuple-element.190.refs_1_), channel_id=1, source_target_pairs={{1,2},{3,4},{5,6},{2,1},{4,3},{6,5},{9,10},{11,12},{13,14},{10,9},... | collective-permute-start | bytes 393224 | tf_op jit(solution)/shard_map/ppermute | solution.py:419
  151.3 13.5 %collective-permute-start.45 = (f32[256,128]{1,0:T(8,128)S(1)}, f32[256,128]{1,0:T(8,128)S(1)}, u32[]{:S(2)}, u32[]{:S(2)}) collective-permute-start(f32[256,128]{1,0:T(8,128)S(1)} %get-tuple-element.191.refs_2_), channel_id=1, source_target_pairs={{0,8},{16,24},{8,0},{24,16},{1,9},{17,25},{9,1},{25,17},{2,10},{18... | collective-permute-start | bytes 393224 | tf_op jit(solution)/shard_map/ppermute | solution.py:419
  156.8 8.1 %collective-permute-start.46 = (f32[256,128]{1,0:T(8,128)S(1)}, f32[256,128]{1,0:T(8,128)S(1)}, u32[]{:S(2)}, u32[]{:S(2)}) collective-permute-start(f32[256,128]{1,0:T(8,128)S(1)} %get-tuple-element.192.refs_3_), channel_id=1, source_target_pairs={{8,16},{16,8},{9,17},{17,9},{10,18},{18,10},{11,19},{19,11},{12,20... | collective-permute-start | bytes 393224 | tf_op jit(solution)/shard_map/ppermute | solution.py:419
  157.6 7.2 %collective-permute-start.42 = (f32[144,128]{1,0:T(8,128)S(1)}, f32[144,128]{1,0:T(8,128)S(1)}, u32[]{:S(2)}, u32[]{:S(2)}) collective-permute-start(f32[144,128]{1,0:T(8,128)S(1)} %get-tuple-element.181), channel_id=1, source_target_pairs={{0,16},{8,24},{16,0},{24,8},{1,17},{9,25},{17,1},{25,9},{2,18},{10... | collective-permute-start | bytes 221192 | tf_op jit(solution)/shard_map/ppermute | solution.py:16
  171.5 1.3 collective-permute-start.47
  172.8 5.8 %collective-permute-start.48 = (f32[72,128]{1,0:T(8,128)S(1)}, f32[72,128]{1,0:T(8,128)S(1)}, u32[]{:S(2)}, u32[]{:S(2)}) collective-permute-start(f32[72,128]{1,0:T(8,128)S(1)} %add.49), channel_id=1, source_target_pairs={{0,1},{1,0},{2,3},{3,2},{4,5},{5,4},{6,7},{7,6},{8,9},{9,8},{10,11... | collective-permute-start | bytes 110600 | tf_op jit(solution)/shard_map/ppermute | solution.py:16
  178.6 5.0 %collective-permute-start.49 = (f32[72,128]{1,0:T(8,128)S(1)}, f32[72,128]{1,0:T(8,128)S(1)}, u32[]{:S(2)}, u32[]{:S(2)}) collective-permute-start(f32[72,128]{1,0:T(8,128)S(1)} %add.50), channel_id=1, source_target_pairs={{0,16},{8,24},{16,0},{24,8},{1,17},{9,25},{17,1},{25,9},{2,18},{10... | collective-permute-start | bytes 110600 | tf_op jit(solution)/shard_map/ppermute | solution.py:16
  183.7 4.0 %collective-permute-start.50 = (f32[72,128]{1,0:T(8,128)S(1)}, f32[72,128]{1,0:T(8,128)S(1)}, u32[]{:S(2)}, u32[]{:S(2)}) collective-permute-start(f32[72,128]{1,0:T(8,128)S(1)} %add.51), channel_id=1, source_target_pairs={{0,2},{1,3},{2,0},{3,1},{4,6},{5,7},{6,4},{7,5},{8,10},{9,11},{10,... | collective-permute-start | bytes 110600 | tf_op jit(solution)/shard_map/ppermute | solution.py:16
  187.7 4.9 %collective-permute-start.51 = (f32[72,128]{1,0:T(8,128)S(1)}, f32[72,128]{1,0:T(8,128)S(1)}, u32[]{:S(2)}, u32[]{:S(2)}) collective-permute-start(f32[72,128]{1,0:T(8,128)S(1)} %add.52), channel_id=1, source_target_pairs={{0,4},{1,5},{2,6},{3,7},{4,0},{5,1},{6,2},{7,3},{8,12},{9,13},{10,... | collective-permute-start | bytes 110600 | tf_op jit(solution)/shard_map/ppermute | solution.py:16
  192.6 1.2 collective-permute-start.52
  (2 other events, 1.3 us)

commit v3 on v0

--- a/solution.py
+++ b/solution.py
@@ -23,19 +23,26 @@
     return [1 << b for b in range(count.bit_length() - 1)]
 
 
-def total(kept, sent):
+def total(kept, sent, ride):
     half = kept + swap(sent, "group", 1)
     rest = [("group", bit) for bit in bits_of("group")[1:]]
     subs = [("sub", bit) for bit in bits_of("sub")]
-    for axis, bit in subs[:1] + rest + subs[1:]:
-        half = half + swap(half, axis, bit)
-    return half, swap(half, "group", 1)
-
-
-def gather_sub(x):
-    for bit in bits_of("sub"):
-        x = jnp.concatenate([x, swap(x, "sub", bit)], axis=0)
-    return x
+    for number, (axis, bit) in enumerate(subs[:1] + rest + subs[1:]):
+        arrived = swap(half, axis, bit)
+        if number == 1:
+            arrived, ride = lax.optimization_barrier((arrived, ride))
+        half = half + arrived
+    return half, swap(half, "group", 1), ride
+
+
+def gather_sub(x, *rides):
+    rides = list(rides)
+    for number, bit in enumerate(bits_of("sub")):
+        arrived = swap(x, "sub", bit)
+        if number < len(rides):
+            arrived, rides[number] = lax.optimization_barrier((arrived, rides[number]))
+        x = jnp.concatenate([x, arrived], axis=0)
+    return x, rides
 
 
 def eliminate(matrix, block, tile=8):
@@ -405,17 +412,38 @@
     )
     subs = lax.axis_size("sub")
     inverse_rows = coarse_inverse[0]
+    maps, (rhs_slots, (received[0], received[2]), (received[1], received[3], weight)) = gather_sub(
+        coarse_map[0, 0],
+        rhs_slots,
+        (received[0], received[2]),
+        (received[1], received[3], weight),
+    )
     (chosen,) = call(
         choice_kernel,
         "selected_inverse",
         product_flops // 4,
         [((subs, modes, subs * modes), jnp.bfloat16)],
         (lax.axis_index("sub") * inverse_rows.shape[0]).astype(jnp.int32)[None],
-        gather_sub(coarse_map[0, 0])[None],
+        maps[None],
         inverse_rows,
     )
+    r, pieces = call(
+        start_kernel,
+        "start",
+        product_flops // 8,
+        [block, share],
+        parity,
+        tables,
+        weight,
+        basis,
+        *rhs_slots,
+        *received,
+    )
     for bit in reversed(bits_of("sub")):
-        chosen = chosen[:bit] + swap(chosen[bit:], "sub", bit)
+        arrived = swap(chosen[bit:], "sub", bit)
+        if bit == bits_of("sub")[-1]:
+            arrived, r, pieces = lax.optimization_barrier((arrived, r, pieces))
+        chosen = chosen[:bit] + arrived
     chosen = chosen[0]
 
     def precondition(vector, carried):
@@ -468,18 +496,6 @@
             whole = [whole[0] + swap(whole[0], "group", bit)]
         return vector, image[:4], exchange(image[:4]), *whole
 
-    r, pieces = call(
-        start_kernel,
-        "start",
-        product_flops // 8,
-        [block, share],
-        parity,
-        tables,
-        weight,
-        basis,
-        *rhs_slots,
-        *received,
-    )
     z, image, received = operator(*precondition(r, pieces))
     w, carried = call(
         gram_start_kernel,
@@ -539,7 +555,7 @@
                 (carried,) = carried
         grams, curvature = lax.optimization_barrier((grams, curvature))
         (inner_inverse,) = call(inverse_kernel, "inner_inverse", solve_flops, [square], grams)
-    grams = total(*carried)
+    *grams, inner_inverse = total(*carried, inner_inverse)
     x, r = call(
         last_update_kernel,
         "last_update",

time: 198 us -> 196 us (0.990)
  waiting for transfers between devices: 64 us -> 60.5 us
  local copies, waits for them, and re-layouts: 3.28 us -> 6.37 us
  starting transfers between devices: 84.4 us -> 81.6 us
    ppermute x23, waiting for transfers between devices: 52.9 us -> 49.3 us  [swap(): lax.ppermute(x, axis, [(i, i ^ bit) for i in range(lax.axis_size(axis))])]
    unnamed x12 -> x20, local copies, waits for them, and re-layouts: 2.31 us -> 5.25 us
    ppermute x28, starting transfers between devices: 36.9 us -> 34.9 us  [exchange(): lax.ppermute(slot, axis, pairs(axis, first))]
  transfers between devices with their start and end apart: 51 -> 51, of which waited for: 24 -> 23; matrix products, arithmetic and copies ran while one was open for 1% -> 2% of each run, Pallas kernels for 7% -> 7%
where the time goes in v3:
time: 196 us; the launch traced here: 195 us
  starting transfers between devices  81.6 us (42%)
  waiting for transfers between devices  60.5 us (31%)
  Pallas kernels  42.9 us (22%)
  local copies, waits for them, and re-layouts  6.37 us (3%)
  other arithmetic  2.93 us (1%)
    ppermute x23, waiting for transfers between devices, swap(): lax.ppermute(x, axis, [(i, i ^ bit) for i in range(lax.axis_size(axis))])  49.3 us
    ppermute x23, starting transfers between devices, swap(): lax.ppermute(x, axis, [(i, i ^ bit) for i in range(lax.axis_size(axis))])  46.7 us
    pallas_call x24, Pallas kernels, call(): pl.pallas_call(kernel, out_shape=shapes, in_specs=[SMEM if a.ndim == 1 el...  42.9 us
    ppermute x28, starting transfers between devices, exchange(): lax.ppermute(slot, axis, pairs(axis, first))  34.9 us
    ppermute x28, waiting for transfers between devices, exchange(): lax.ppermute(slot, axis, pairs(axis, first))  11.2 us
    unnamed x20, local copies, waits for them, and re-layouts  5.25 us
  transfers between devices with their start and end apart: 51, of which 23 were waited for; matrix products, arithmetic and copies ran while one was open for 2% of the time, Pallas kernels for 7%

profile of v3, /device:TPU:0, one launch (start us, length us, event | category | flops | bytes accessed | tf_op | source)
XLA Modules:
  0.0 195.4 jit_solution(10729727591211655342)
XLA Ops:
  0.6 3.0 %collective-permute-start = (s32[32]{0:T(128)}, s32[32]{0:T(128)S(1)}, u32[]{:S(2)}, u32[]{:S(2)}) collective-permute-start(s32[32]{0:T(128)} %bitcast.40), channel_id=1, source_target_pairs={{0,1},{1,0},{2,3},{3,2},{4,5},{5,4},{6,7},{7,6},{8,9},{9,8},{10,11... | collective-permute-start | bytes 392 | tf_op jit(solution)/shard_map/ppermute | solution.py:16
  3.7 1.1 dynamic-slice_bitcast_fusion
  5.5 1.3 collective-permute-start.5
  6.7 3.7 %collective-permute-start.2 = (bf16[256,128]{1,0:T(8,128)(2,1)S(1)}, bf16[256,128]{1,0:T(8,128)(2,1)S(1)}, u32[]{:S(2)}, u32[]{:S(2)}) collective-permute-start(bf16[256,128]{1,0:T(8,128)(2,1)S(1)} %get-tuple-element.82.refs_0_), channel_id=1, source_target_pairs={{0,1},{2,3},{4,5},{6,7},{1,0},{3,2},{5,4},{7,6},{8,9},{10,11},{12,... | collective-permute-start | bytes 196616 | tf_op jit(solution)/shard_map/ppermute | solution.py:373
  10.5 2.3 %collective-permute-start.3 = (bf16[256,128]{1,0:T(8,128)(2,1)S(1)}, bf16[256,128]{1,0:T(8,128)(2,1)S(1)}, u32[]{:S(2)}, u32[]{:S(2)}) collective-permute-start(bf16[256,128]{1,0:T(8,128)(2,1)S(1)} %get-tuple-element.84.refs_2_), channel_id=1, source_target_pairs={{0,8},{16,24},{8,0},{24,16},{1,9},{17,25},{9,1},{25,17},{2,10},{18... | collective-permute-start | bytes 196616 | tf_op jit(solution)/shard_map/ppermute | solution.py:373
  13.5 1.6 collective-permute-start.1
  15.2 1.9 collective-permute-done.1
  18.3 1.3 pad_add_fusion.3
  19.6 2.6 %collective-permute-start.4 = (s32[128]{0:T(128)}, s32[128]{0:T(128)S(1)}, u32[]{:S(2)}, u32[]{:S(2)}) collective-permute-start(s32[128]{0:T(128)} %pad_add_fusion.3), channel_id=1, source_target_pairs={{0,4},{1,5},{2,6},{3,7},{4,0},{5,1},{6,2},{7,3},{8,12},{9,13},{10,... | collective-permute-start | bytes 1544 | tf_op jit(solution)/shard_map/ppermute | solution.py:16
  23.6 1.2 shared_row_tables.1
  25.6 0.9 copy-done.7
  27.2 1.9 collective-permute-start.7
  30.8 1.4 start.1
  32.2 0.9 collective-permute-done.7
  33.9 3.5 %collective-permute-done.10.received = f32[32,128]{1,0:T(8,128)S(1)} collective-permute-done((f32[32,128]{1,0:T(8,128)S(1)}, f32[32,128]{1,0:T(8,128)S(1)}, u32[]{:S(2)}, u32[]{:S(2)}) %collective-permute-start.10) | collective-permute-done | bytes 16416 | tf_op jit(solution)/shard_map/ppermute | solution.py:16
  37.3 1.7 collective-permute-start.11
  40.2 1.0 collective-permute-done.11.received
  41.3 1.0 collective-permute-start.12
  42.9 3.6 %collective-permute-done.12.received = f32[128,128]{1,0:T(8,128)S(1)} collective-permute-done((f32[128,128]{1,0:T(8,128)S(1)}, f32[128,128]{1,0:T(8,128)S(1)}, u32[]{:S(2)}, u32[]{:S(2)}) %collective-permute-start.12) | collective-permute-done | bytes 65568 | tf_op jit(solution)/shard_map/ppermute | solution.py:16
  46.4 1.0 coarse_part.3
  49.6 2.8 %collective-permute-done.13.refs_4_ = f32[256,128]{1,0:T(8,128)S(1)} collective-permute-done((f32[256,128]{1,0:T(8,128)S(1)}, f32[256,128]{1,0:T(8,128)S(1)}, u32[]{:S(2)}, u32[]{:S(2)}) %collective-permute-start.13) | collective-permute-done | bytes 131104 | tf_op jit(solution)/shard_map/ppermute | solution.py:373
  52.5 1.6 operator.3
  54.1 4.9 %collective-permute-start.17 = (f32[256,128]{1,0:T(8,128)S(1)}, f32[256,128]{1,0:T(8,128)S(1)}, u32[]{:S(2)}, u32[]{:S(2)}) collective-permute-start(f32[256,128]{1,0:T(8,128)S(1)} %get-tuple-element.100.refs_0_), channel_id=1, source_target_pairs={{0,1},{2,3},{4,5},{6,7},{1,0},{3,2},{5,4},{7,6},{8,9},{10,11},{12,... | collective-permute-start | bytes 393224 | tf_op jit(solution)/shard_map/ppermute | solution.py:373
  59.6 2.2 %collective-permute-start.19 = (f32[256,128]{1,0:T(8,128)S(1)}, f32[256,128]{1,0:T(8,128)S(1)}, u32[]{:S(2)}, u32[]{:S(2)}) collective-permute-start(f32[256,128]{1,0:T(8,128)S(1)} %get-tuple-element.102.refs_2_), channel_id=1, source_target_pairs={{0,8},{16,24},{8,0},{24,16},{1,9},{17,25},{9,1},{25,17},{2,10},{18... | collective-permute-start | bytes 393224 | tf_op jit(solution)/shard_map/ppermute | solution.py:373
  62.8 1.5 start_grams.1
  64.4 4.9 %collective-permute-start.21 = (f32[176,128]{1,0:T(8,128)S(1)}, f32[176,128]{1,0:T(8,128)S(1)}, u32[]{:S(2)}, u32[]{:S(2)}) collective-permute-start(f32[176,128]{1,0:T(8,128)S(1)} %get-tuple-element.105.own), channel_id=1, source_target_pairs={{0,1},{1,0},{2,3},{3,2},{4,5},{5,4},{6,7},{7,6},{8,9},{9,8},{10,11... | collective-permute-start | bytes 270344 | tf_op jit(solution)/shard_map/ppermute | solution.py:16
  69.3 2.5 %collective-permute-done.21.received = f32[176,128]{1,0:T(8,128)S(1)} collective-permute-done((f32[176,128]{1,0:T(8,128)S(1)}, f32[176,128]{1,0:T(8,128)S(1)}, u32[]{:S(2)}, u32[]{:S(2)}) %collective-permute-start.21) | collective-permute-done | bytes 90144 | tf_op jit(solution)/shard_map/ppermute | solution.py:16
  71.8 4.1 %collective-permute-start.22 = (f32[208,128]{1,0:T(8,128)S(1)}, f32[208,128]{1,0:T(8,128)S(1)}, u32[]{:S(2)}, u32[]{:S(2)}) collective-permute-start(f32[208,128]{1,0:T(8,128)S(1)} %fold.8.own), channel_id=1, source_target_pairs={{0,2},{1,3},{2,0},{3,1},{4,6},{5,7},{6,4},{7,5},{8,10},{9,11},{10,... | collective-permute-start | bytes 319496 | tf_op jit(solution)/shard_map/ppermute | solution.py:16
  75.9 3.8 %collective-permute-done.22.received = f32[208,128]{1,0:T(8,128)S(1)} collective-permute-done((f32[208,128]{1,0:T(8,128)S(1)}, f32[208,128]{1,0:T(8,128)S(1)}, u32[]{:S(2)}, u32[]{:S(2)}) %collective-permute-start.22) | collective-permute-done | bytes 106528 | tf_op jit(solution)/shard_map/ppermute | solution.py:16
  80.5 8.8 %collective-permute-done.23.received = f32[272,128]{1,0:T(8,128)S(1)} collective-permute-done((f32[272,128]{1,0:T(8,128)S(1)}, f32[272,128]{1,0:T(8,128)S(1)}, u32[]{:S(2)}, u32[]{:S(2)}) %collective-permute-start.23) | collective-permute-done | bytes 139296 | tf_op jit(solution)/shard_map/ppermute | solution.py:16
  89.4 1.0 coarse_part.4
  91.9 4.5 %collective-permute-done.24.refs_4_ = f32[256,128]{1,0:T(8,128)S(1)} collective-permute-done((f32[256,128]{1,0:T(8,128)S(1)}, f32[256,128]{1,0:T(8,128)S(1)}, u32[]{:S(2)}, u32[]{:S(2)}) %collective-permute-start.24) | collective-permute-done | bytes 131104 | tf_op jit(solution)/shard_map/ppermute | solution.py:373
  96.4 1.6 operator.4
  98.0 4.6 %collective-permute-start.29 = (f32[256,128]{1,0:T(8,128)S(1)}, f32[256,128]{1,0:T(8,128)S(1)}, u32[]{:S(2)}, u32[]{:S(2)}) collective-permute-start(f32[256,128]{1,0:T(8,128)S(1)} %get-tuple-element.112.refs_0_), channel_id=1, source_target_pairs={{0,1},{2,3},{4,5},{6,7},{1,0},{3,2},{5,4},{7,6},{8,9},{10,11},{12,... | collective-permute-start | bytes 393224 | tf_op jit(solution)/shard_map/ppermute | solution.py:373
  103.3 0.8 collective-permute-start.32
  104.1 3.4 %collective-permute-start.28 = (f32[144,128]{1,0:T(8,128)S(1)}, f32[144,128]{1,0:T(8,128)S(1)}, u32[]{:S(2)}, u32[]{:S(2)}) collective-permute-start(f32[144,128]{1,0:T(8,128)S(1)} %get-tuple-element.110), channel_id=1, source_target_pairs={{0,16},{8,24},{16,0},{24,8},{1,17},{9,25},{17,1},{25,9},{2,18},{10... | collective-permute-start | bytes 221192 | tf_op jit(solution)/shard_map/ppermute | solution.py:16
  107.6 4.3 %collective-permute-done.28 = f32[144,128]{1,0:T(8,128)S(1)} collective-permute-done((f32[144,128]{1,0:T(8,128)S(1)}, f32[144,128]{1,0:T(8,128)S(1)}, u32[]{:S(2)}, u32[]{:S(2)}) %collective-permute-start.28) | collective-permute-done | bytes 73760 | tf_op jit(solution)/shard_map/ppermute | solution.py:16
  111.9 6.7 %first_update.1 = (f32[1024,128]{1,0:T(8,128)S(1)}, f32[1024,128]{1,0:T(8,128)S(1)}, f32[1024,128]{1,0:T(8,128)S(1)}, f32[1024,128]{1,0:T(8,128)S(1)}, f32[1024,...) custom-call(s32[2]{0:T(128)S(1)} %pad_add_fusion.1.parity, ...), custom_call_target="tpu_custom_call" | custom-call | flops 800000000 | bytes 7110664 | tf_op jit(solution)/shard_map/first_update/pallas_call | solution.py:354
  118.6 3.2 %collective-permute-start.33 = (f32[176,128]{1,0:T(8,128)S(1)}, f32[176,128]{1,0:T(8,128)S(1)}, u32[]{:S(2)}, u32[]{:S(2)}) collective-permute-start(f32[176,128]{1,0:T(8,128)S(1)} %get-tuple-element.117.own), channel_id=1, source_target_pairs={{0,1},{1,0},{2,3},{3,2},{4,5},{5,4},{6,7},{7,6},{8,9},{9,8},{10,11... | collective-permute-start | bytes 270344 | tf_op jit(solution)/shard_map/ppermute | solution.py:16
  121.8 2.5 %collective-permute-done.33.received = f32[176,128]{1,0:T(8,128)S(1)} collective-permute-done((f32[176,128]{1,0:T(8,128)S(1)}, f32[176,128]{1,0:T(8,128)S(1)}, u32[]{:S(2)}, u32[]{:S(2)}) %collective-permute-start.33) | collective-permute-done | bytes 90144 | tf_op jit(solution)/shard_map/ppermute | solution.py:16
  124.3 1.7 collective-permute-start.34
  126.0 3.1 %collective-permute-done.34.received = f32[208,128]{1,0:T(8,128)S(1)} collective-permute-done((f32[208,128]{1,0:T(8,128)S(1)}, f32[208,128]{1,0:T(8,128)S(1)}, u32[]{:S(2)}, u32[]{:S(2)}) %collective-permute-start.34) | collective-permute-done | bytes 106528 | tf_op jit(solution)/shard_map/ppermute | solution.py:16
  129.1 4.1 %collective-permute-start.35 = (f32[272,128]{1,0:T(8,128)S(1)}, f32[272,128]{1,0:T(8,128)S(1)}, u32[]{:S(2)}, u32[]{:S(2)}) collective-permute-start(f32[272,128]{1,0:T(8,128)S(1)} %fold.11.own), channel_id=1, source_target_pairs={{0,4},{1,5},{2,6},{3,7},{4,0},{5,1},{6,2},{7,3},{8,12},{9,13},{10,... | collective-permute-start | bytes 417800 | tf_op jit(solution)/shard_map/ppermute | solution.py:16
  133.9 3.8 %collective-permute-done.35.received = f32[272,128]{1,0:T(8,128)S(1)} collective-permute-done((f32[272,128]{1,0:T(8,128)S(1)}, f32[272,128]{1,0:T(8,128)S(1)}, u32[]{:S(2)}, u32[]{:S(2)}) %collective-permute-start.35) | collective-permute-done | bytes 139296 | tf_op jit(solution)/shard_map/ppermute | solution.py:16
  137.6 1.0 coarse_part.5
  138.7 1.0 collective-permute-start.36
  141.1 3.5 %collective-permute-done.36.refs_4_ = f32[256,128]{1,0:T(8,128)S(1)} collective-permute-done((f32[256,128]{1,0:T(8,128)S(1)}, f32[256,128]{1,0:T(8,128)S(1)}, u32[]{:S(2)}, u32[]{:S(2)}) %collective-permute-start.36) | collective-permute-done | bytes 131104 | tf_op jit(solution)/shard_map/ppermute | solution.py:373
  144.6 1.6 operator.5
  146.2 4.6 %collective-permute-start.41 = (f32[256,128]{1,0:T(8,128)S(1)}, f32[256,128]{1,0:T(8,128)S(1)}, u32[]{:S(2)}, u32[]{:S(2)}) collective-permute-start(f32[256,128]{1,0:T(8,128)S(1)} %get-tuple-element.131.refs_0_), channel_id=1, source_target_pairs={{0,1},{2,3},{4,5},{6,7},{1,0},{3,2},{5,4},{7,6},{8,9},{10,11},{12,... | collective-permute-start | bytes 393224 | tf_op jit(solution)/shard_map/ppermute | solution.py:373
  151.6 0.9 collective-permute-start.44
  152.5 3.4 %collective-permute-start.40 = (f32[144,128]{1,0:T(8,128)S(1)}, f32[144,128]{1,0:T(8,128)S(1)}, u32[]{:S(2)}, u32[]{:S(2)}) collective-permute-start(f32[144,128]{1,0:T(8,128)S(1)} %get-tuple-element.122), channel_id=1, source_target_pairs={{0,16},{8,24},{16,0},{24,8},{1,17},{9,25},{17,1},{25,9},{2,18},{10... | collective-permute-start | bytes 221192 | tf_op jit(solution)/shard_map/ppermute | solution.py:16
  155.9 3.9 %inner_inverse.2 = f32[128,128]{1,0:T(8,128)S(1)} custom-call(f32[144,128]{1,0:T(8,128)S(1)} %add.67.grams), custom_call_target="tpu_custom_call" | custom-call | flops 400000000 | bytes 139264 | tf_op jit(solution)/shard_map/inner_inverse/pallas_call | solution.py:354
  160.1 6.7 %next_update.1 = (f32[1024,128]{1,0:T(8,128)S(1)}, f32[1024,128]{1,0:T(8,128)S(1)}, f32[1024,128]{1,0:T(8,128)S(1)}, f32[1024,128]{1,0:T(8,128)S(1)}, f32[1024,1...) custom-call(s32[2]{0:T(128)S(1)} %pad_add_fusion.1.parity, ...), custom_call_target="tpu_custom_call" | custom-call | flops 800000000 | bytes 11419656 | tf_op jit(solution)/shard_map/next_update/pallas_call | solution.py:354
  166.9 1.2 collective-permute-done.45
  168.1 3.2 %collective-permute-start.46 = (f32[72,128]{1,0:T(8,128)S(1)}, f32[72,128]{1,0:T(8,128)S(1)}, u32[]{:S(2)}, u32[]{:S(2)}) collective-permute-start(f32[72,128]{1,0:T(8,128)S(1)} %add.69), channel_id=1, source_target_pairs={{0,1},{1,0},{2,3},{3,2},{4,5},{5,4},{6,7},{7,6},{8,9},{9,8},{10,11... | collective-permute-start | bytes 110600 | tf_op jit(solution)/shard_map/ppermute | solution.py:16
  171.2 1.9 collective-permute-done.46
  173.2 0.9 collective-permute-start.47
  174.1 4.2 %inner_inverse.3 = f32[128,128]{1,0:T(8,128)S(1)} custom-call(f32[144,128]{1,0:T(8,128)S(1)} %add.68.grams), custom_call_target="tpu_custom_call" | custom-call | flops 400000000 | bytes 139264 | tf_op jit(solution)/shard_map/inner_inverse/pallas_call | solution.py:354
  178.3 1.4 collective-permute-start.48
  179.7 2.6 %collective-permute-done.48 = f32[72,128]{1,0:T(8,128)S(1)} collective-permute-done((f32[72,128]{1,0:T(8,128)S(1)}, f32[72,128]{1,0:T(8,128)S(1)}, u32[]{:S(2)}, u32[]{:S(2)}) %collective-permute-start.48) | collective-permute-done | bytes 36896 | tf_op jit(solution)/shard_map/ppermute | solution.py:16
  182.3 3.4 %collective-permute-start.49 = (f32[72,128]{1,0:T(8,128)S(1)}, f32[72,128]{1,0:T(8,128)S(1)}, u32[]{:S(2)}, u32[]{:S(2)}) collective-permute-start(f32[72,128]{1,0:T(8,128)S(1)} %add.72), channel_id=1, source_target_pairs={{0,4},{1,5},{2,6},{3,7},{4,0},{5,1},{6,2},{7,3},{8,12},{9,13},{10,... | collective-permute-start | bytes 110600 | tf_op jit(solution)/shard_map/ppermute | solution.py:16
  185.8 1.9 collective-permute-done.49
  187.7 1.2 collective-permute-done.50.other
  188.9 6.5 %last_update.1 = (f32[1024,128]{1,0:T(8,128)}, f32[1024,128]{1,0:T(8,128)}) custom-call(s32[2]{0:T(128)S(1)} %pad_add_fusion.1.parity, f32[72,128]{1,0:T(8,128)S(1)} %add.73.half, f32[72,128]{1,0:T(8,128)S(1)} %collective-permute-done.50.other, f32[128,128]{1,0:T(8,128)S(1)} %inner_inverse.3, f32[128,128]{1,0:T(8,128)S(1)} %get-tuple-element.141.curvature, ...), custom_call_target="tpu_custom_call" | custom-call | flops 800000000 | bytes 4399112 | tf_op jit(solution)/shard_map/last_update/pallas_call | solution.py:354
  (100 shorter events, 19.8 us)
Async XLA Ops:
  0.6 28.5 %copy-start.2 = (bf16[1,1,32,1024]{3,2,1,0:T(8,128)(2,1)S(1)}, bf16[1,1,32,1024]{3,2,1,0:T(8,128)(2,1)}, u32[]{:S(2)}) copy-start(bf16[1,1,32,1024]{3,2,1,0:T(8,128)(2,1)} %param.11) | copy-start | bytes 196612
  0.6 12.1 %collective-permute-start = (s32[32]{0:T(128)}, s32[32]{0:T(128)S(1)}, u32[]{:S(2)}, u32[]{:S(2)}) collective-permute-start(s32[32]{0:T(128)} %bitcast.40), channel_id=1, source_target_pairs={{0,1},{1,0},{2,3},{3,2},{4,5},{5,4},{6,7},{7,6},{8,9},{9,8},{10,11... | collective-permute-start | bytes 392 | tf_op jit(solution)/shard_map/ppermute | solution.py:16
  3.7 35.8 %copy-start = (bf16[1,1,1024,1024]{3,2,1,0:T(8,128)(2,1)S(1)}, bf16[1,1,1024,1024]{3,2,1,0:T(8,128)(2,1)}, u32[]{:S(2)}) copy-start(bf16[1,1,1024,1024]{3,2,1,0:T(8,128)(2,1)} %param.9) | copy-start | bytes 6291460
  4.8 20.0 %collective-permute-start.6 = (bf16[256,128]{1,0:T(8,128)(2,1)S(1)}, bf16[256,128]{1,0:T(8,128)(2,1)S(1)}, u32[]{:S(2)}, u32[]{:S(2)}) collective-permute-start(bf16[256,128]{1,0:T(8,128)(2,1)S(1)} %get-tuple-element.85.refs_3_), channel_id=1, source_target_pairs={{8,16},{16,8},{9,17},{17,9},{10,18},{18,10},{11,19},{19,11},{12,20... | collective-permute-start | bytes 196616 | tf_op jit(solution)/shard_map/ppermute | solution.py:373
  5.5 19.4 %collective-permute-start.5 = (bf16[256,128]{1,0:T(8,128)(2,1)S(1)}, bf16[256,128]{1,0:T(8,128)(2,1)}, u32[]{:S(2)}, u32[]{:S(2)}) collective-permute-start(bf16[256,128]{1,0:T(8,128)(2,1)S(1)} %get-tuple-element.83.refs_1_), channel_id=1, source_target_pairs={{1,2},{3,4},{5,6},{2,1},{4,3},{6,5},{9,10},{11,12},{13,14},{10,9},... | collective-permute-start | bytes 196616 | tf_op jit(solution)/shard_map/ppermute | solution.py:373
  6.7 10.3 %collective-permute-start.2 = (bf16[256,128]{1,0:T(8,128)(2,1)S(1)}, bf16[256,128]{1,0:T(8,128)(2,1)S(1)}, u32[]{:S(2)}, u32[]{:S(2)}) collective-permute-start(bf16[256,128]{1,0:T(8,128)(2,1)S(1)} %get-tuple-element.82.refs_0_), channel_id=1, source_target_pairs={{0,1},{2,3},{4,5},{6,7},{1,0},{3,2},{5,4},{7,6},{8,9},{10,11},{12,... | collective-permute-start | bytes 196616 | tf_op jit(solution)/shard_map/ppermute | solution.py:373
  10.5 7.2 %collective-permute-start.3 = (bf16[256,128]{1,0:T(8,128)(2,1)S(1)}, bf16[256,128]{1,0:T(8,128)(2,1)S(1)}, u32[]{:S(2)}, u32[]{:S(2)}) collective-permute-start(bf16[256,128]{1,0:T(8,128)(2,1)S(1)} %get-tuple-element.84.refs_2_), channel_id=1, source_target_pairs={{0,8},{16,24},{8,0},{24,16},{1,9},{17,25},{9,1},{25,17},{2,10},{18... | collective-permute-start | bytes 196616 | tf_op jit(solution)/shard_map/ppermute | solution.py:373
  13.5 3.5 %collective-permute-start.1 = (s32[64]{0:T(128)S(1)}, s32[64]{0:T(128)S(1)}, u32[]{:S(2)}, u32[]{:S(2)}) collective-permute-start(s32[64]{0:T(128)S(1)} %pad_add_fusion.2), channel_id=1, source_target_pairs={{0,2},{1,3},{2,0},{3,1},{4,6},{5,7},{6,4},{7,5},{8,10},{9,11},{10,... | collective-permute-start | bytes 776 | tf_op jit(solution)/shard_map/ppermute | solution.py:16
  17.0 0.6 copy-start.3
  17.7 0.6 copy-start.5
  19.6 5.2 %collective-permute-start.4 = (s32[128]{0:T(128)}, s32[128]{0:T(128)S(1)}, u32[]{:S(2)}, u32[]{:S(2)}) collective-permute-start(s32[128]{0:T(128)} %pad_add_fusion.3), channel_id=1, source_target_pairs={{0,4},{1,5},{2,6},{3,7},{4,0},{5,1},{6,2},{7,3},{8,12},{9,13},{10,... | collective-permute-start | bytes 1544 | tf_op jit(solution)/shard_map/ppermute | solution.py:16
  22.2 0.7 copy-start.8
  22.9 0.7 copy-start.9
  25.6 1.0 copy-start.7
  27.2 5.9 %collective-permute-start.7 = (bf16[4,32,256]{2,1,0:T(8,128)(2,1)S(1)}, bf16[4,32,256]{2,1,0:T(8,128)(2,1)S(1)}, u32[]{:S(2)}, u32[]{:S(2)}) collective-permute-start(bf16[4,32,256]{2,1,0:T(8,128)(2,1)S(1)} %slice.25), channel_id=1, source_target_pairs={{0,4},{1,5},{2,6},{3,7},{4,0},{5,1},{6,2},{7,3},{8,12},{9,13},{10,... | collective-permute-start | bytes 196616 | tf_op jit(solution)/shard_map/ppermute | solution.py:16
  29.2 0.8 copy-start.4
  30.0 0.8 copy-start.6
  33.2 5.8 %collective-permute-start.8 = (bf16[2,32,256]{2,1,0:T(8,128)(2,1)S(1)}, bf16[2,32,256]{2,1,0:T(8,128)(2,1)S(1)}, u32[]{:S(2)}, u32[]{:S(2)}) collective-permute-start(bf16[2,32,256]{2,1,0:T(8,128)(2,1)S(1)} %slice.27), channel_id=1, source_target_pairs={{0,2},{1,3},{2,0},{3,1},{4,6},{5,7},{6,4},{7,5},{8,10},{9,11},{10,... | collective-permute-start | bytes 98312 | tf_op jit(solution)/shard_map/ppermute | solution.py:16
  33.5 3.8 %collective-permute-start.10 = (f32[32,128]{1,0:T(8,128)S(1)}, f32[32,128]{1,0:T(8,128)S(1)}, u32[]{:S(2)}, u32[]{:S(2)}) collective-permute-start(f32[32,128]{1,0:T(8,128)S(1)} %get-tuple-element.94.own), channel_id=1, source_target_pairs={{0,1},{1,0},{2,3},{3,2},{4,5},{5,4},{6,7},{7,6},{8,9},{9,8},{10,11... | collective-permute-start | bytes 49160 | tf_op jit(solution)/shard_map/ppermute | solution.py:16
  37.3 3.9 %collective-permute-start.11 = (f32[64,128]{1,0:T(8,128)S(1)}, f32[64,128]{1,0:T(8,128)S(1)}, u32[]{:S(2)}, u32[]{:S(2)}) collective-permute-start(f32[64,128]{1,0:T(8,128)S(1)} %fold.6.own), channel_id=1, source_target_pairs={{0,2},{1,3},{2,0},{3,1},{4,6},{5,7},{6,4},{7,5},{8,10},{9,11},{10,... | collective-permute-start | bytes 98312 | tf_op jit(solution)/shard_map/ppermute | solution.py:16
  39.1 3.8 %collective-permute-start.9 = (bf16[1,32,256]{2,1,0:T(8,128)(2,1)S(1)}, bf16[1,32,256]{2,1,0:T(8,128)(2,1)S(1)}, u32[]{:S(2)}, u32[]{:S(2)}) collective-permute-start(bf16[1,32,256]{2,1,0:T(8,128)(2,1)S(1)} %slice.29), channel_id=1, source_target_pairs={{0,1},{1,0},{2,3},{3,2},{4,5},{5,4},{6,7},{7,6},{8,9},{9,8},{10,11... | collective-permute-start | bytes 49160 | tf_op jit(solution)/shard_map/ppermute | solution.py:16
  39.5 13.0 %copy-start.1 = (bf16[1,1,1024,1024]{3,2,1,0:T(8,128)(2,1)S(1)}, bf16[1,1,1024,1024]{3,2,1,0:T(8,128)(2,1)}, u32[]{:S(2)}) copy-start(bf16[1,1,1024,1024]{3,2,1,0:T(8,128)(2,1)} %param.8) | copy-start | bytes 6291460
  41.3 5.2 %collective-permute-start.12 = (f32[128,128]{1,0:T(8,128)S(1)}, f32[128,128]{1,0:T(8,128)S(1)}, u32[]{:S(2)}, u32[]{:S(2)}) collective-permute-start(f32[128,128]{1,0:T(8,128)S(1)} %fold.7.own), channel_id=1, source_target_pairs={{0,4},{1,5},{2,6},{3,7},{4,0},{5,1},{6,2},{7,3},{8,12},{9,13},{10,... | collective-permute-start | bytes 196616 | tf_op jit(solution)/shard_map/ppermute | solution.py:16
  47.4 5.0 %collective-permute-start.13 = (f32[256,128]{1,0:T(8,128)S(1)}, f32[256,128]{1,0:T(8,128)S(1)}, u32[]{:S(2)}, u32[]{:S(2)}) collective-permute-start(f32[256,128]{1,0:T(8,128)S(1)} %get-tuple-element.95.refs_0_), channel_id=1, source_target_pairs={{0,1},{2,3},{4,5},{6,7},{1,0},{3,2},{5,4},{7,6},{8,9},{10,11},{12,... | collective-permute-start | bytes 393224 | tf_op jit(solution)/shard_map/ppermute | solution.py:373
  48.2 4.2 %collective-permute-start.14 = (f32[256,128]{1,0:T(8,128)S(1)}, f32[256,128]{1,0:T(8,128)S(1)}, u32[]{:S(2)}, u32[]{:S(2)}) collective-permute-start(f32[256,128]{1,0:T(8,128)S(1)} %get-tuple-element.96.refs_1_), channel_id=1, source_target_pairs={{1,2},{3,4},{5,6},{2,1},{4,3},{6,5},{9,10},{11,12},{13,14},{10,9},... | collective-permute-start | bytes 393224 | tf_op jit(solution)/shard_map/ppermute | solution.py:373
  48.9 3.6 %collective-permute-start.15 = (f32[256,128]{1,0:T(8,128)S(1)}, f32[256,128]{1,0:T(8,128)S(1)}, u32[]{:S(2)}, u32[]{:S(2)}) collective-permute-start(f32[256,128]{1,0:T(8,128)S(1)} %get-tuple-element.97.refs_2_), channel_id=1, source_target_pairs={{0,8},{16,24},{8,0},{24,16},{1,9},{17,25},{9,1},{25,17},{2,10},{18... | collective-permute-start | bytes 393224 | tf_op jit(solution)/shard_map/ppermute | solution.py:373
  49.0 3.5 %collective-permute-start.16 = (f32[256,128]{1,0:T(8,128)S(1)}, f32[256,128]{1,0:T(8,128)S(1)}, u32[]{:S(2)}, u32[]{:S(2)}) collective-permute-start(f32[256,128]{1,0:T(8,128)S(1)} %get-tuple-element.98.refs_3_), channel_id=1, source_target_pairs={{8,16},{16,8},{9,17},{17,9},{10,18},{18,10},{11,19},{19,11},{12,20... | collective-permute-start | bytes 393224 | tf_op jit(solution)/shard_map/ppermute | solution.py:373
  54.1 8.4 %collective-permute-start.17 = (f32[256,128]{1,0:T(8,128)S(1)}, f32[256,128]{1,0:T(8,128)S(1)}, u32[]{:S(2)}, u32[]{:S(2)}) collective-permute-start(f32[256,128]{1,0:T(8,128)S(1)} %get-tuple-element.100.refs_0_), channel_id=1, source_target_pairs={{0,1},{2,3},{4,5},{6,7},{1,0},{3,2},{5,4},{7,6},{8,9},{10,11},{12,... | collective-permute-start | bytes 393224 | tf_op jit(solution)/shard_map/ppermute | solution.py:373
  58.9 3.6 %collective-permute-start.18 = (f32[256,128]{1,0:T(8,128)S(1)}, f32[256,128]{1,0:T(8,128)S(1)}, u32[]{:S(2)}, u32[]{:S(2)}) collective-permute-start(f32[256,128]{1,0:T(8,128)S(1)} %get-tuple-element.101.refs_1_), channel_id=1, source_target_pairs={{1,2},{3,4},{5,6},{2,1},{4,3},{6,5},{9,10},{11,12},{13,14},{10,9},... | collective-permute-start | bytes 393224 | tf_op jit(solution)/shard_map/ppermute | solution.py:373
  59.6 3.2 %collective-permute-start.19 = (f32[256,128]{1,0:T(8,128)S(1)}, f32[256,128]{1,0:T(8,128)S(1)}, u32[]{:S(2)}, u32[]{:S(2)}) collective-permute-start(f32[256,128]{1,0:T(8,128)S(1)} %get-tuple-element.102.refs_2_), channel_id=1, source_target_pairs={{0,8},{16,24},{8,0},{24,16},{1,9},{17,25},{9,1},{25,17},{2,10},{18... | collective-permute-start | bytes 393224 | tf_op jit(solution)/shard_map/ppermute | solution.py:373
  61.8 1.0 collective-permute-start.20
  64.4 7.5 %collective-permute-start.21 = (f32[176,128]{1,0:T(8,128)S(1)}, f32[176,128]{1,0:T(8,128)S(1)}, u32[]{:S(2)}, u32[]{:S(2)}) collective-permute-start(f32[176,128]{1,0:T(8,128)S(1)} %get-tuple-element.105.own), channel_id=1, source_target_pairs={{0,1},{1,0},{2,3},{3,2},{4,5},{5,4},{6,7},{7,6},{8,9},{9,8},{10,11... | collective-permute-start | bytes 270344 | tf_op jit(solution)/shard_map/ppermute | solution.py:16
  71.8 7.9 %collective-permute-start.22 = (f32[208,128]{1,0:T(8,128)S(1)}, f32[208,128]{1,0:T(8,128)S(1)}, u32[]{:S(2)}, u32[]{:S(2)}) collective-permute-start(f32[208,128]{1,0:T(8,128)S(1)} %fold.8.own), channel_id=1, source_target_pairs={{0,2},{1,3},{2,0},{3,1},{4,6},{5,7},{6,4},{7,5},{8,10},{9,11},{10,... | collective-permute-start | bytes 319496 | tf_op jit(solution)/shard_map/ppermute | solution.py:16
  79.7 9.6 %collective-permute-start.23 = (f32[272,128]{1,0:T(8,128)S(1)}, f32[272,128]{1,0:T(8,128)S(1)}, u32[]{:S(2)}, u32[]{:S(2)}) collective-permute-start(f32[272,128]{1,0:T(8,128)S(1)} %fold.9.own), channel_id=1, source_target_pairs={{0,4},{1,5},{2,6},{3,7},{4,0},{5,1},{6,2},{7,3},{8,12},{9,13},{10,... | collective-permute-start | bytes 417800 | tf_op jit(solution)/shard_map/ppermute | solution.py:16
  90.4 6.0 %collective-permute-start.26 = (f32[400,128]{1,0:T(8,128)S(1)}, f32[400,128]{1,0:T(8,128)S(1)}, u32[]{:S(2)}, u32[]{:S(2)}) collective-permute-start(f32[400,128]{1,0:T(8,128)S(1)} %get-tuple-element.108.refs_2_), channel_id=1, source_target_pairs={{0,8},{16,24},{8,0},{24,16},{1,9},{17,25},{9,1},{25,17},{2,10},{18... | collective-permute-start | bytes 614408 | tf_op jit(solution)/shard_map/ppermute | solution.py:373
  90.4 5.9 %collective-permute-start.24 = (f32[256,128]{1,0:T(8,128)S(1)}, f32[256,128]{1,0:T(8,128)S(1)}, u32[]{:S(2)}, u32[]{:S(2)}) collective-permute-start(f32[256,128]{1,0:T(8,128)S(1)} %get-tuple-element.106.refs_0_), channel_id=1, source_target_pairs={{0,1},{2,3},{4,5},{6,7},{1,0},{3,2},{5,4},{7,6},{8,9},{10,11},{12,... | collective-permute-start | bytes 393224 | tf_op jit(solution)/shard_map/ppermute | solution.py:373
  90.5 5.8 %collective-permute-start.25 = (f32[256,128]{1,0:T(8,128)S(1)}, f32[256,128]{1,0:T(8,128)S(1)}, u32[]{:S(2)}, u32[]{:S(2)}) collective-permute-start(f32[256,128]{1,0:T(8,128)S(1)} %get-tuple-element.107.refs_1_), channel_id=1, source_target_pairs={{1,2},{3,4},{5,6},{2,1},{4,3},{6,5},{9,10},{11,12},{13,14},{10,9},... | collective-permute-start | bytes 393224 | tf_op jit(solution)/shard_map/ppermute | solution.py:373
  91.2 5.2 %collective-permute-start.27 = (f32[256,128]{1,0:T(8,128)S(1)}, f32[256,128]{1,0:T(8,128)S(1)}, u32[]{:S(2)}, u32[]{:S(2)}) collective-permute-start(f32[256,128]{1,0:T(8,128)S(1)} %get-tuple-element.109.refs_3_), channel_id=1, source_target_pairs={{8,16},{16,8},{9,17},{17,9},{10,18},{18,10},{11,19},{19,11},{12,20... | collective-permute-start | bytes 393224 | tf_op jit(solution)/shard_map/ppermute | solution.py:373
  98.0 13.9 %collective-permute-start.29 = (f32[256,128]{1,0:T(8,128)S(1)}, f32[256,128]{1,0:T(8,128)S(1)}, u32[]{:S(2)}, u32[]{:S(2)}) collective-permute-start(f32[256,128]{1,0:T(8,128)S(1)} %get-tuple-element.112.refs_0_), channel_id=1, source_target_pairs={{0,1},{2,3},{4,5},{6,7},{1,0},{3,2},{5,4},{7,6},{8,9},{10,11},{12,... | collective-permute-start | bytes 393224 | tf_op jit(solution)/shard_map/ppermute | solution.py:373
  102.5 9.3 %collective-permute-start.30 = (f32[256,128]{1,0:T(8,128)S(1)}, f32[256,128]{1,0:T(8,128)S(1)}, u32[]{:S(2)}, u32[]{:S(2)}) collective-permute-start(f32[256,128]{1,0:T(8,128)S(1)} %get-tuple-element.113.refs_1_), channel_id=1, source_target_pairs={{1,2},{3,4},{5,6},{2,1},{4,3},{6,5},{9,10},{11,12},{13,14},{10,9},... | collective-permute-start | bytes 393224 | tf_op jit(solution)/shard_map/ppermute | solution.py:373
  103.2 8.6 %collective-permute-start.31 = (f32[256,128]{1,0:T(8,128)S(1)}, f32[256,128]{1,0:T(8,128)S(1)}, u32[]{:S(2)}, u32[]{:S(2)}) collective-permute-start(f32[256,128]{1,0:T(8,128)S(1)} %get-tuple-element.114.refs_2_), channel_id=1, source_target_pairs={{0,8},{16,24},{8,0},{24,16},{1,9},{17,25},{9,1},{25,17},{2,10},{18... | collective-permute-start | bytes 393224 | tf_op jit(solution)/shard_map/ppermute | solution.py:373
  103.3 8.6 %collective-permute-start.32 = (f32[256,128]{1,0:T(8,128)S(1)}, f32[256,128]{1,0:T(8,128)S(1)}, u32[]{:S(2)}, u32[]{:S(2)}) collective-permute-start(f32[256,128]{1,0:T(8,128)S(1)} %get-tuple-element.115.refs_3_), channel_id=1, source_target_pairs={{8,16},{16,8},{9,17},{17,9},{10,18},{18,10},{11,19},{19,11},{12,20... | collective-permute-start | bytes 393224 | tf_op jit(solution)/shard_map/ppermute | solution.py:373
  104.1 7.7 %collective-permute-start.28 = (f32[144,128]{1,0:T(8,128)S(1)}, f32[144,128]{1,0:T(8,128)S(1)}, u32[]{:S(2)}, u32[]{:S(2)}) collective-permute-start(f32[144,128]{1,0:T(8,128)S(1)} %get-tuple-element.110), channel_id=1, source_target_pairs={{0,16},{8,24},{16,0},{24,8},{1,17},{9,25},{17,1},{25,9},{2,18},{10... | collective-permute-start | bytes 221192 | tf_op jit(solution)/shard_map/ppermute | solution.py:16
  118.6 5.7 %collective-permute-start.33 = (f32[176,128]{1,0:T(8,128)S(1)}, f32[176,128]{1,0:T(8,128)S(1)}, u32[]{:S(2)}, u32[]{:S(2)}) collective-permute-start(f32[176,128]{1,0:T(8,128)S(1)} %get-tuple-element.117.own), channel_id=1, source_target_pairs={{0,1},{1,0},{2,3},{3,2},{4,5},{5,4},{6,7},{7,6},{8,9},{9,8},{10,11... | collective-permute-start | bytes 270344 | tf_op jit(solution)/shard_map/ppermute | solution.py:16
  124.3 4.8 %collective-permute-start.34 = (f32[208,128]{1,0:T(8,128)S(1)}, f32[208,128]{1,0:T(8,128)S(1)}, u32[]{:S(2)}, u32[]{:S(2)}) collective-permute-start(f32[208,128]{1,0:T(8,128)S(1)} %fold.10.own), channel_id=1, source_target_pairs={{0,2},{1,3},{2,0},{3,1},{4,6},{5,7},{6,4},{7,5},{8,10},{9,11},{10,... | collective-permute-start | bytes 319496 | tf_op jit(solution)/shard_map/ppermute | solution.py:16
  129.1 8.6 %collective-permute-start.35 = (f32[272,128]{1,0:T(8,128)S(1)}, f32[272,128]{1,0:T(8,128)S(1)}, u32[]{:S(2)}, u32[]{:S(2)}) collective-permute-start(f32[272,128]{1,0:T(8,128)S(1)} %fold.11.own), channel_id=1, source_target_pairs={{0,4},{1,5},{2,6},{3,7},{4,0},{5,1},{6,2},{7,3},{8,12},{9,13},{10,... | collective-permute-start | bytes 417800 | tf_op jit(solution)/shard_map/ppermute | solution.py:16
  138.6 6.0 %collective-permute-start.38 = (f32[400,128]{1,0:T(8,128)S(1)}, f32[400,128]{1,0:T(8,128)S(1)}, u32[]{:S(2)}, u32[]{:S(2)}) collective-permute-start(f32[400,128]{1,0:T(8,128)S(1)} %get-tuple-element.120.refs_2_), channel_id=1, source_target_pairs={{0,8},{16,24},{8,0},{24,16},{1,9},{17,25},{9,1},{25,17},{2,10},{18... | collective-permute-start | bytes 614408 | tf_op jit(solution)/shard_map/ppermute | solution.py:373
  138.7 5.9 %collective-permute-start.36 = (f32[256,128]{1,0:T(8,128)S(1)}, f32[256,128]{1,0:T(8,128)S(1)}, u32[]{:S(2)}, u32[]{:S(2)}) collective-permute-start(f32[256,128]{1,0:T(8,128)S(1)} %get-tuple-element.118.refs_0_), channel_id=1, source_target_pairs={{0,1},{2,3},{4,5},{6,7},{1,0},{3,2},{5,4},{7,6},{8,9},{10,11},{12,... | collective-permute-start | bytes 393224 | tf_op jit(solution)/shard_map/ppermute | solution.py:373
  139.8 4.9 %collective-permute-start.37 = (f32[256,128]{1,0:T(8,128)S(1)}, f32[256,128]{1,0:T(8,128)S(1)}, u32[]{:S(2)}, u32[]{:S(2)}) collective-permute-start(f32[256,128]{1,0:T(8,128)S(1)} %get-tuple-element.119.refs_1_), channel_id=1, source_target_pairs={{1,2},{3,4},{5,6},{2,1},{4,3},{6,5},{9,10},{11,12},{13,14},{10,9},... | collective-permute-start | bytes 393224 | tf_op jit(solution)/shard_map/ppermute | solution.py:373
  140.4 4.2 %collective-permute-start.39 = (f32[256,128]{1,0:T(8,128)S(1)}, f32[256,128]{1,0:T(8,128)S(1)}, u32[]{:S(2)}, u32[]{:S(2)}) collective-permute-start(f32[256,128]{1,0:T(8,128)S(1)} %get-tuple-element.121.refs_3_), channel_id=1, source_target_pairs={{8,16},{16,8},{9,17},{17,9},{10,18},{18,10},{11,19},{19,11},{12,20... | collective-permute-start | bytes 393224 | tf_op jit(solution)/shard_map/ppermute | solution.py:373
  146.2 13.9 %collective-permute-start.41 = (f32[256,128]{1,0:T(8,128)S(1)}, f32[256,128]{1,0:T(8,128)S(1)}, u32[]{:S(2)}, u32[]{:S(2)}) collective-permute-start(f32[256,128]{1,0:T(8,128)S(1)} %get-tuple-element.131.refs_0_), channel_id=1, source_target_pairs={{0,1},{2,3},{4,5},{6,7},{1,0},{3,2},{5,4},{7,6},{8,9},{10,11},{12,... | collective-permute-start | bytes 393224 | tf_op jit(solution)/shard_map/ppermute | solution.py:373
  150.8 9.3 %collective-permute-start.42 = (f32[256,128]{1,0:T(8,128)S(1)}, f32[256,128]{1,0:T(8,128)S(1)}, u32[]{:S(2)}, u32[]{:S(2)}) collective-permute-start(f32[256,128]{1,0:T(8,128)S(1)} %get-tuple-element.132.refs_1_), channel_id=1, source_target_pairs={{1,2},{3,4},{5,6},{2,1},{4,3},{6,5},{9,10},{11,12},{13,14},{10,9},... | collective-permute-start | bytes 393224 | tf_op jit(solution)/shard_map/ppermute | solution.py:373
  151.5 8.6 %collective-permute-start.43 = (f32[256,128]{1,0:T(8,128)S(1)}, f32[256,128]{1,0:T(8,128)S(1)}, u32[]{:S(2)}, u32[]{:S(2)}) collective-permute-start(f32[256,128]{1,0:T(8,128)S(1)} %get-tuple-element.133.refs_2_), channel_id=1, source_target_pairs={{0,8},{16,24},{8,0},{24,16},{1,9},{17,25},{9,1},{25,17},{2,10},{18... | collective-permute-start | bytes 393224 | tf_op jit(solution)/shard_map/ppermute | solution.py:373
  151.6 8.6 %collective-permute-start.44 = (f32[256,128]{1,0:T(8,128)S(1)}, f32[256,128]{1,0:T(8,128)S(1)}, u32[]{:S(2)}, u32[]{:S(2)}) collective-permute-start(f32[256,128]{1,0:T(8,128)S(1)} %get-tuple-element.134.refs_3_), channel_id=1, source_target_pairs={{8,16},{16,8},{9,17},{17,9},{10,18},{18,10},{11,19},{19,11},{12,20... | collective-permute-start | bytes 393224 | tf_op jit(solution)/shard_map/ppermute | solution.py:373
  152.5 7.6 %collective-permute-start.40 = (f32[144,128]{1,0:T(8,128)S(1)}, f32[144,128]{1,0:T(8,128)S(1)}, u32[]{:S(2)}, u32[]{:S(2)}) collective-permute-start(f32[144,128]{1,0:T(8,128)S(1)} %get-tuple-element.122), channel_id=1, source_target_pairs={{0,16},{8,24},{16,0},{24,8},{1,17},{9,25},{17,1},{25,9},{2,18},{10... | collective-permute-start | bytes 221192 | tf_op jit(solution)/shard_map/ppermute | solution.py:16
  166.8 1.3 collective-permute-start.45
  168.1 5.1 %collective-permute-start.46 = (f32[72,128]{1,0:T(8,128)S(1)}, f32[72,128]{1,0:T(8,128)S(1)}, u32[]{:S(2)}, u32[]{:S(2)}) collective-permute-start(f32[72,128]{1,0:T(8,128)S(1)} %add.69), channel_id=1, source_target_pairs={{0,1},{1,0},{2,3},{3,2},{4,5},{5,4},{6,7},{7,6},{8,9},{9,8},{10,11... | collective-permute-start | bytes 110600 | tf_op jit(solution)/shard_map/ppermute | solution.py:16
  173.2 5.1 %collective-permute-start.47 = (f32[72,128]{1,0:T(8,128)S(1)}, f32[72,128]{1,0:T(8,128)S(1)}, u32[]{:S(2)}, u32[]{:S(2)}) collective-permute-start(f32[72,128]{1,0:T(8,128)S(1)} %add.70), channel_id=1, source_target_pairs={{0,16},{8,24},{16,0},{24,8},{1,17},{9,25},{17,1},{25,9},{2,18},{10... | collective-permute-start | bytes 110600 | tf_op jit(solution)/shard_map/ppermute | solution.py:16
  178.3 4.0 %collective-permute-start.48 = (f32[72,128]{1,0:T(8,128)S(1)}, f32[72,128]{1,0:T(8,128)S(1)}, u32[]{:S(2)}, u32[]{:S(2)}) collective-permute-start(f32[72,128]{1,0:T(8,128)S(1)} %add.71), channel_id=1, source_target_pairs={{0,2},{1,3},{2,0},{3,1},{4,6},{5,7},{6,4},{7,5},{8,10},{9,11},{10,... | collective-permute-start | bytes 110600 | tf_op jit(solution)/shard_map/ppermute | solution.py:16
  182.3 5.4 %collective-permute-start.49 = (f32[72,128]{1,0:T(8,128)S(1)}, f32[72,128]{1,0:T(8,128)S(1)}, u32[]{:S(2)}, u32[]{:S(2)}) collective-permute-start(f32[72,128]{1,0:T(8,128)S(1)} %add.72), channel_id=1, source_target_pairs={{0,4},{1,5},{2,6},{3,7},{4,0},{5,1},{6,2},{7,3},{8,12},{9,13},{10,... | collective-permute-start | bytes 110600 | tf_op jit(solution)/shard_map/ppermute | solution.py:16
  187.7 1.2 collective-permute-start.50

commit v4 on v3

--- a/solution.py
+++ b/solution.py
@@ -446,21 +446,24 @@
         chosen = chosen[:bit] + arrived
     chosen = chosen[0]
 
-    def precondition(vector, carried):
+    def precondition(vector, carried, ride=None):
         grams = carried.shape[0] - modes
         (local,) = call(
             local_kernel, "local_inverse", product_flops, [block], weight, local_inverse, vector
         )
         bits = bits_of("sub")
-        for bit in bits[:-1]:
+        for number, bit in enumerate(bits[:-1]):
             rows_out = 2 * carried.shape[0] - grams
+            arrived = swap(carried, "sub", bit)
+            if ride is not None and number == len(bits[:-1]) - 1:
+                arrived, ride = lax.optimization_barrier((arrived, ride))
             (carried,) = call(
                 functools.partial(fold_kernel, grams),
                 "fold",
                 columns * rows_out,
                 [((rows_out, columns), jnp.float32)],
                 carried,
-                swap(carried, "sub", bit),
+                arrived,
             )
         slots = call(
             functools.partial(finish_kernel, grams),
@@ -475,7 +478,7 @@
             carried,
             swap(carried, "sub", bits[-1]),
         )
-        return slots, exchange(slots)
+        return slots, exchange(slots), ride
 
     def operator(slots, received):
         grams = slots[2].shape[0] - zone
@@ -496,7 +499,7 @@
             whole = [whole[0] + swap(whole[0], "group", bit)]
         return vector, image[:4], exchange(image[:4]), *whole
 
-    z, image, received = operator(*precondition(r, pieces))
+    z, image, received = operator(*precondition(r, pieces)[:2])
     w, carried = call(
         gram_start_kernel,
         "start_grams",
@@ -511,9 +514,11 @@
         *image,
         *received,
     )
+    ride = None
     for iteration in range(ITERS - 1):
         final = iteration + 2 == ITERS
-        m, image, received, grams = operator(*precondition(w, carried))
+        slots, received, inner_inverse = precondition(w, carried, ride)
+        m, image, received, grams = operator(slots, received)
         common = (parity, tables, weight, basis, grams)
         if iteration == 0:
             p, s, q = z, w, m
@@ -554,8 +559,8 @@
             if not final:
                 (carried,) = carried
         grams, curvature = lax.optimization_barrier((grams, curvature))
-        (inner_inverse,) = call(inverse_kernel, "inner_inverse", solve_flops, [square], grams)
-    *grams, inner_inverse = total(*carried, inner_inverse)
+        (ride,) = call(inverse_kernel, "inner_inverse", solve_flops, [square], grams)
+    *grams, inner_inverse = total(*carried, ride)
     x, r = call(
         last_update_kernel,
         "last_update",

time: 196 us -> 197 us (level)
  transfers between devices with their start and end apart: 51 -> 51, of which waited for: 23 -> 22; matrix products, arithmetic and copies ran while one was open for 2% -> 2% of each run, Pallas kernels for 7% -> 6%
where the time goes in v4:
time: 197 us; the launch traced here: 196 us
  starting transfers between devices  81.6 us (41%)
  waiting for transfers between devices  61.5 us (31%)
  Pallas kernels  42.9 us (22%)
  local copies, waits for them, and re-layouts  6.37 us (3%)
  other arithmetic  2.93 us (1%)
    ppermute x23, waiting for transfers between devices, swap(): lax.ppermute(x, axis, [(i, i ^ bit) for i in range(lax.axis_size(axis))])  51.1 us
    ppermute x23, starting transfers between devices, swap(): lax.ppermute(x, axis, [(i, i ^ bit) for i in range(lax.axis_size(axis))])  45.7 us
    pallas_call x24, Pallas kernels, call(): pl.pallas_call(kernel, out_shape=shapes, in_specs=[SMEM if a.ndim == 1 el...  42.9 us
    ppermute x28, starting transfers between devices, exchange(): lax.ppermute(slot, axis, pairs(axis, first))  35.9 us
    ppermute x28, waiting for transfers between devices, exchange(): lax.ppermute(slot, axis, pairs(axis, first))  10.4 us
    unnamed x20, local copies, waits for them, and re-layouts  5.25 us
  transfers between devices with their start and end apart: 51, of which 22 were waited for; matrix products, arithmetic and copies ran while one was open for 2% of the time, Pallas kernels for 6%

profile of v4, /device:TPU:0, one launch (start us, length us, event | category | flops | bytes accessed | tf_op | source)
XLA Modules:
  0.0 196.4 jit_solution(9013046423057086661)
XLA Ops:
  0.6 3.0 %collective-permute-start = (s32[32]{0:T(128)}, s32[32]{0:T(128)S(1)}, u32[]{:S(2)}, u32[]{:S(2)}) collective-permute-start(s32[32]{0:T(128)} %bitcast.40), channel_id=1, source_target_pairs={{0,1},{1,0},{2,3},{3,2},{4,5},{5,4},{6,7},{7,6},{8,9},{9,8},{10,11... | collective-permute-start | bytes 392 | tf_op jit(solution)/shard_map/ppermute | solution.py:16
  3.7 1.1 dynamic-slice_bitcast_fusion
  5.5 1.3 collective-permute-start.5
  6.7 3.7 %collective-permute-start.2 = (bf16[256,128]{1,0:T(8,128)(2,1)S(1)}, bf16[256,128]{1,0:T(8,128)(2,1)S(1)}, u32[]{:S(2)}, u32[]{:S(2)}) collective-permute-start(bf16[256,128]{1,0:T(8,128)(2,1)S(1)} %get-tuple-element.84.refs_0_), channel_id=1, source_target_pairs={{0,1},{2,3},{4,5},{6,7},{1,0},{3,2},{5,4},{7,6},{8,9},{10,11},{12,... | collective-permute-start | bytes 196616 | tf_op jit(solution)/shard_map/ppermute | solution.py:373
  10.5 2.3 %collective-permute-start.3 = (bf16[256,128]{1,0:T(8,128)(2,1)S(1)}, bf16[256,128]{1,0:T(8,128)(2,1)S(1)}, u32[]{:S(2)}, u32[]{:S(2)}) collective-permute-start(bf16[256,128]{1,0:T(8,128)(2,1)S(1)} %get-tuple-element.86.refs_2_), channel_id=1, source_target_pairs={{0,8},{16,24},{8,0},{24,16},{1,9},{17,25},{9,1},{25,17},{2,10},{18... | collective-permute-start | bytes 196616 | tf_op jit(solution)/shard_map/ppermute | solution.py:373
  13.5 1.6 collective-permute-start.1
  15.2 1.9 collective-permute-done.1
  18.3 1.3 pad_add_fusion.3
  19.6 2.6 %collective-permute-start.4 = (s32[128]{0:T(128)}, s32[128]{0:T(128)S(1)}, u32[]{:S(2)}, u32[]{:S(2)}) collective-permute-start(s32[128]{0:T(128)} %pad_add_fusion.3), channel_id=1, source_target_pairs={{0,4},{1,5},{2,6},{3,7},{4,0},{5,1},{6,2},{7,3},{8,12},{9,13},{10,... | collective-permute-start | bytes 1544 | tf_op jit(solution)/shard_map/ppermute | solution.py:16
  23.6 1.2 shared_row_tables.1
  25.6 0.9 copy-done.7
  27.2 1.9 collective-permute-start.7
  30.8 1.4 start.1
  32.2 0.9 collective-permute-done.7
  33.9 3.5 %collective-permute-done.10.received = f32[32,128]{1,0:T(8,128)S(1)} collective-permute-done((f32[32,128]{1,0:T(8,128)S(1)}, f32[32,128]{1,0:T(8,128)S(1)}, u32[]{:S(2)}, u32[]{:S(2)}) %collective-permute-start.10) | collective-permute-done | bytes 16416 | tf_op jit(solution)/shard_map/ppermute | solution.py:16
  37.3 1.7 collective-permute-start.11
  40.2 1.0 collective-permute-done.11.received
  41.3 1.0 collective-permute-start.12
  42.9 3.6 %collective-permute-done.12.received = f32[128,128]{1,0:T(8,128)S(1)} collective-permute-done((f32[128,128]{1,0:T(8,128)S(1)}, f32[128,128]{1,0:T(8,128)S(1)}, u32[]{:S(2)}, u32[]{:S(2)}) %collective-permute-start.12) | collective-permute-done | bytes 65568 | tf_op jit(solution)/shard_map/ppermute | solution.py:16
  46.4 1.0 coarse_part.3
  49.6 2.8 %collective-permute-done.13.refs_4_ = f32[256,128]{1,0:T(8,128)S(1)} collective-permute-done((f32[256,128]{1,0:T(8,128)S(1)}, f32[256,128]{1,0:T(8,128)S(1)}, u32[]{:S(2)}, u32[]{:S(2)}) %collective-permute-start.13) | collective-permute-done | bytes 131104 | tf_op jit(solution)/shard_map/ppermute | solution.py:373
  52.5 1.6 operator.3
  54.1 4.9 %collective-permute-start.17 = (f32[256,128]{1,0:T(8,128)S(1)}, f32[256,128]{1,0:T(8,128)S(1)}, u32[]{:S(2)}, u32[]{:S(2)}) collective-permute-start(f32[256,128]{1,0:T(8,128)S(1)} %get-tuple-element.102.refs_0_), channel_id=1, source_target_pairs={{0,1},{2,3},{4,5},{6,7},{1,0},{3,2},{5,4},{7,6},{8,9},{10,11},{12,... | collective-permute-start | bytes 393224 | tf_op jit(solution)/shard_map/ppermute | solution.py:373
  59.6 2.2 %collective-permute-start.19 = (f32[256,128]{1,0:T(8,128)S(1)}, f32[256,128]{1,0:T(8,128)S(1)}, u32[]{:S(2)}, u32[]{:S(2)}) collective-permute-start(f32[256,128]{1,0:T(8,128)S(1)} %get-tuple-element.104.refs_2_), channel_id=1, source_target_pairs={{0,8},{16,24},{8,0},{24,16},{1,9},{17,25},{9,1},{25,17},{2,10},{18... | collective-permute-start | bytes 393224 | tf_op jit(solution)/shard_map/ppermute | solution.py:373
  62.8 1.5 start_grams.1
  64.4 4.9 %collective-permute-start.21 = (f32[176,128]{1,0:T(8,128)S(1)}, f32[176,128]{1,0:T(8,128)S(1)}, u32[]{:S(2)}, u32[]{:S(2)}) collective-permute-start(f32[176,128]{1,0:T(8,128)S(1)} %get-tuple-element.107.own), channel_id=1, source_target_pairs={{0,1},{1,0},{2,3},{3,2},{4,5},{5,4},{6,7},{7,6},{8,9},{9,8},{10,11... | collective-permute-start | bytes 270344 | tf_op jit(solution)/shard_map/ppermute | solution.py:16
  69.3 2.5 %collective-permute-done.21.received = f32[176,128]{1,0:T(8,128)S(1)} collective-permute-done((f32[176,128]{1,0:T(8,128)S(1)}, f32[176,128]{1,0:T(8,128)S(1)}, u32[]{:S(2)}, u32[]{:S(2)}) %collective-permute-start.21) | collective-permute-done | bytes 90144 | tf_op jit(solution)/shard_map/ppermute | solution.py:16
  71.8 4.1 %collective-permute-start.22 = (f32[208,128]{1,0:T(8,128)S(1)}, f32[208,128]{1,0:T(8,128)S(1)}, u32[]{:S(2)}, u32[]{:S(2)}) collective-permute-start(f32[208,128]{1,0:T(8,128)S(1)} %fold.8.own), channel_id=1, source_target_pairs={{0,2},{1,3},{2,0},{3,1},{4,6},{5,7},{6,4},{7,5},{8,10},{9,11},{10,... | collective-permute-start | bytes 319496 | tf_op jit(solution)/shard_map/ppermute | solution.py:16
  75.9 3.8 %collective-permute-done.22.received = f32[208,128]{1,0:T(8,128)S(1)} collective-permute-done((f32[208,128]{1,0:T(8,128)S(1)}, f32[208,128]{1,0:T(8,128)S(1)}, u32[]{:S(2)}, u32[]{:S(2)}) %collective-permute-start.22) | collective-permute-done | bytes 106528 | tf_op jit(solution)/shard_map/ppermute | solution.py:16
  80.5 8.8 %collective-permute-done.23.received = f32[272,128]{1,0:T(8,128)S(1)} collective-permute-done((f32[272,128]{1,0:T(8,128)S(1)}, f32[272,128]{1,0:T(8,128)S(1)}, u32[]{:S(2)}, u32[]{:S(2)}) %collective-permute-start.23) | collective-permute-done | bytes 139296 | tf_op jit(solution)/shard_map/ppermute | solution.py:16
  89.4 1.0 coarse_part.4
  91.9 4.5 %collective-permute-done.24.refs_4_ = f32[256,128]{1,0:T(8,128)S(1)} collective-permute-done((f32[256,128]{1,0:T(8,128)S(1)}, f32[256,128]{1,0:T(8,128)S(1)}, u32[]{:S(2)}, u32[]{:S(2)}) %collective-permute-start.24) | collective-permute-done | bytes 131104 | tf_op jit(solution)/shard_map/ppermute | solution.py:373
  96.4 1.6 operator.4
  98.0 4.6 %collective-permute-start.29 = (f32[256,128]{1,0:T(8,128)S(1)}, f32[256,128]{1,0:T(8,128)S(1)}, u32[]{:S(2)}, u32[]{:S(2)}) collective-permute-start(f32[256,128]{1,0:T(8,128)S(1)} %get-tuple-element.114.refs_0_), channel_id=1, source_target_pairs={{0,1},{2,3},{4,5},{6,7},{1,0},{3,2},{5,4},{7,6},{8,9},{10,11},{12,... | collective-permute-start | bytes 393224 | tf_op jit(solution)/shard_map/ppermute | solution.py:373
  103.3 0.8 collective-permute-start.32
  104.1 3.4 %collective-permute-start.28 = (f32[144,128]{1,0:T(8,128)S(1)}, f32[144,128]{1,0:T(8,128)S(1)}, u32[]{:S(2)}, u32[]{:S(2)}) collective-permute-start(f32[144,128]{1,0:T(8,128)S(1)} %get-tuple-element.112), channel_id=1, source_target_pairs={{0,16},{8,24},{16,0},{24,8},{1,17},{9,25},{17,1},{25,9},{2,18},{10... | collective-permute-start | bytes 221192 | tf_op jit(solution)/shard_map/ppermute | solution.py:16
  107.6 4.3 %collective-permute-done.28 = f32[144,128]{1,0:T(8,128)S(1)} collective-permute-done((f32[144,128]{1,0:T(8,128)S(1)}, f32[144,128]{1,0:T(8,128)S(1)}, u32[]{:S(2)}, u32[]{:S(2)}) %collective-permute-start.28) | collective-permute-done | bytes 73760 | tf_op jit(solution)/shard_map/ppermute | solution.py:16
  111.9 6.7 %first_update.1 = (f32[1024,128]{1,0:T(8,128)S(1)}, f32[1024,128]{1,0:T(8,128)S(1)}, f32[1024,128]{1,0:T(8,128)S(1)}, f32[1024,128]{1,0:T(8,128)S(1)}, f32[1024,...) custom-call(s32[2]{0:T(128)S(1)} %pad_add_fusion.1.parity, ...), custom_call_target="tpu_custom_call" | custom-call | flops 800000000 | bytes 7110664 | tf_op jit(solution)/shard_map/first_update/pallas_call | solution.py:354
  118.6 3.2 %collective-permute-start.33 = (f32[176,128]{1,0:T(8,128)S(1)}, f32[176,128]{1,0:T(8,128)S(1)}, u32[]{:S(2)}, u32[]{:S(2)}) collective-permute-start(f32[176,128]{1,0:T(8,128)S(1)} %get-tuple-element.119.own), channel_id=1, source_target_pairs={{0,1},{1,0},{2,3},{3,2},{4,5},{5,4},{6,7},{7,6},{8,9},{9,8},{10,11... | collective-permute-start | bytes 270344 | tf_op jit(solution)/shard_map/ppermute | solution.py:16
  121.8 2.5 %collective-permute-done.33.received = f32[176,128]{1,0:T(8,128)S(1)} collective-permute-done((f32[176,128]{1,0:T(8,128)S(1)}, f32[176,128]{1,0:T(8,128)S(1)}, u32[]{:S(2)}, u32[]{:S(2)}) %collective-permute-start.33) | collective-permute-done | bytes 90144 | tf_op jit(solution)/shard_map/ppermute | solution.py:16
  124.3 1.7 collective-permute-start.34
  126.0 3.9 %inner_inverse.2 = f32[128,128]{1,0:T(8,128)S(1)} custom-call(f32[144,128]{1,0:T(8,128)S(1)} %add.67.grams), custom_call_target="tpu_custom_call" | custom-call | flops 400000000 | bytes 139264 | tf_op jit(solution)/shard_map/inner_inverse/pallas_call | solution.py:354
  129.9 2.6 %collective-permute-start.35 = (f32[272,128]{1,0:T(8,128)S(1)}, f32[272,128]{1,0:T(8,128)S(1)}, u32[]{:S(2)}, u32[]{:S(2)}) collective-permute-start(f32[272,128]{1,0:T(8,128)S(1)} %fold.11.own), channel_id=1, source_target_pairs={{0,4},{1,5},{2,6},{3,7},{4,0},{5,1},{6,2},{7,3},{8,12},{9,13},{10,... | collective-permute-start | bytes 417800 | tf_op jit(solution)/shard_map/ppermute | solution.py:16
  133.3 4.2 %collective-permute-done.35.received = f32[272,128]{1,0:T(8,128)S(1)} collective-permute-done((f32[272,128]{1,0:T(8,128)S(1)}, f32[272,128]{1,0:T(8,128)S(1)}, u32[]{:S(2)}, u32[]{:S(2)}) %collective-permute-start.35) | collective-permute-done | bytes 139296 | tf_op jit(solution)/shard_map/ppermute | solution.py:16
  137.5 1.0 coarse_part.5
  138.6 2.0 %collective-permute-start.36 = (f32[256,128]{1,0:T(8,128)S(1)}, f32[256,128]{1,0:T(8,128)S(1)}, u32[]{:S(2)}, u32[]{:S(2)}) collective-permute-start(f32[256,128]{1,0:T(8,128)S(1)} %get-tuple-element.123.refs_0_), channel_id=1, source_target_pairs={{0,1},{2,3},{4,5},{6,7},{1,0},{3,2},{5,4},{7,6},{8,9},{10,11},{12,... | collective-permute-start | bytes 393224 | tf_op jit(solution)/shard_map/ppermute | solution.py:373
  142.0 2.7 %collective-permute-done.36.refs_4_ = f32[256,128]{1,0:T(8,128)S(1)} collective-permute-done((f32[256,128]{1,0:T(8,128)S(1)}, f32[256,128]{1,0:T(8,128)S(1)}, u32[]{:S(2)}, u32[]{:S(2)}) %collective-permute-start.36) | collective-permute-done | bytes 131104 | tf_op jit(solution)/shard_map/ppermute | solution.py:373
  144.7 1.6 operator.5
  146.3 4.6 %collective-permute-start.41 = (f32[256,128]{1,0:T(8,128)S(1)}, f32[256,128]{1,0:T(8,128)S(1)}, u32[]{:S(2)}, u32[]{:S(2)}) collective-permute-start(f32[256,128]{1,0:T(8,128)S(1)} %get-tuple-element.135.refs_0_), channel_id=1, source_target_pairs={{0,1},{2,3},{4,5},{6,7},{1,0},{3,2},{5,4},{7,6},{8,9},{10,11},{12,... | collective-permute-start | bytes 393224 | tf_op jit(solution)/shard_map/ppermute | solution.py:373
  151.7 0.9 collective-permute-start.44
  152.6 3.4 %collective-permute-start.40 = (f32[144,128]{1,0:T(8,128)S(1)}, f32[144,128]{1,0:T(8,128)S(1)}, u32[]{:S(2)}, u32[]{:S(2)}) collective-permute-start(f32[144,128]{1,0:T(8,128)S(1)} %get-tuple-element.127), channel_id=1, source_target_pairs={{0,16},{8,24},{16,0},{24,8},{1,17},{9,25},{17,1},{25,9},{2,18},{10... | collective-permute-start | bytes 221192 | tf_op jit(solution)/shard_map/ppermute | solution.py:16
  156.0 4.2 %collective-permute-done.40 = f32[144,128]{1,0:T(8,128)S(1)} collective-permute-done((f32[144,128]{1,0:T(8,128)S(1)}, f32[144,128]{1,0:T(8,128)S(1)}, u32[]{:S(2)}, u32[]{:S(2)}) %collective-permute-start.40) | collective-permute-done | bytes 73760 | tf_op jit(solution)/shard_map/ppermute | solution.py:16
  160.3 6.7 %next_update.1 = (f32[1024,128]{1,0:T(8,128)S(1)}, f32[1024,128]{1,0:T(8,128)S(1)}, f32[1024,128]{1,0:T(8,128)S(1)}, f32[1024,128]{1,0:T(8,128)S(1)}, f32[1024,1...) custom-call(s32[2]{0:T(128)S(1)} %pad_add_fusion.1.parity, ...), custom_call_target="tpu_custom_call" | custom-call | flops 800000000 | bytes 11419656 | tf_op jit(solution)/shard_map/next_update/pallas_call | solution.py:354
  167.0 1.2 collective-permute-done.45
  168.2 3.4 %collective-permute-start.46 = (f32[72,128]{1,0:T(8,128)S(1)}, f32[72,128]{1,0:T(8,128)S(1)}, u32[]{:S(2)}, u32[]{:S(2)}) collective-permute-start(f32[72,128]{1,0:T(8,128)S(1)} %add.69), channel_id=1, source_target_pairs={{0,1},{1,0},{2,3},{3,2},{4,5},{5,4},{6,7},{7,6},{8,9},{9,8},{10,11... | collective-permute-start | bytes 110600 | tf_op jit(solution)/shard_map/ppermute | solution.py:16
  171.6 1.9 collective-permute-done.46
  173.6 1.1 collective-permute-start.47
  174.7 3.9 %inner_inverse.3 = f32[128,128]{1,0:T(8,128)S(1)} custom-call(f32[144,128]{1,0:T(8,128)S(1)} %add.68.grams), custom_call_target="tpu_custom_call" | custom-call | flops 400000000 | bytes 139264 | tf_op jit(solution)/shard_map/inner_inverse/pallas_call | solution.py:354
  178.6 1.3 collective-permute-start.48
  180.0 2.7 %collective-permute-done.48 = f32[72,128]{1,0:T(8,128)S(1)} collective-permute-done((f32[72,128]{1,0:T(8,128)S(1)}, f32[72,128]{1,0:T(8,128)S(1)}, u32[]{:S(2)}, u32[]{:S(2)}) %collective-permute-start.48) | collective-permute-done | bytes 36896 | tf_op jit(solution)/shard_map/ppermute | solution.py:16
  182.7 3.4 %collective-permute-start.49 = (f32[72,128]{1,0:T(8,128)S(1)}, f32[72,128]{1,0:T(8,128)S(1)}, u32[]{:S(2)}, u32[]{:S(2)}) collective-permute-start(f32[72,128]{1,0:T(8,128)S(1)} %add.72), channel_id=1, source_target_pairs={{0,4},{1,5},{2,6},{3,7},{4,0},{5,1},{6,2},{7,3},{8,12},{9,13},{10,... | collective-permute-start | bytes 110600 | tf_op jit(solution)/shard_map/ppermute | solution.py:16
  186.1 2.3 %collective-permute-done.49 = f32[72,128]{1,0:T(8,128)S(1)} collective-permute-done((f32[72,128]{1,0:T(8,128)S(1)}, f32[72,128]{1,0:T(8,128)S(1)}, u32[]{:S(2)}, u32[]{:S(2)}) %collective-permute-start.49) | collective-permute-done | bytes 36896 | tf_op jit(solution)/shard_map/ppermute | solution.py:16
  188.4 1.2 collective-permute-done.50.other
  189.6 6.8 %last_update.1 = (f32[1024,128]{1,0:T(8,128)}, f32[1024,128]{1,0:T(8,128)}) custom-call(s32[2]{0:T(128)S(1)} %pad_add_fusion.1.parity, f32[72,128]{1,0:T(8,128)S(1)} %add.73.half, f32[72,128]{1,0:T(8,128)S(1)} %collective-permute-done.50.other, f32[128,128]{1,0:T(8,128)S(1)} %inner_inverse.3, f32[128,128]{1,0:T(8,128)S(1)} %get-tuple-element.145.curvature, ...), custom_call_target="tpu_custom_call" | custom-call | flops 800000000 | bytes 4399112 | tf_op jit(solution)/shard_map/last_update/pallas_call | solution.py:354
  (100 shorter events, 19.5 us)
Async XLA Ops:
  0.6 28.5 %copy-start.2 = (bf16[1,1,32,1024]{3,2,1,0:T(8,128)(2,1)S(1)}, bf16[1,1,32,1024]{3,2,1,0:T(8,128)(2,1)}, u32[]{:S(2)}) copy-start(bf16[1,1,32,1024]{3,2,1,0:T(8,128)(2,1)} %param.11) | copy-start | bytes 196612
  0.6 12.1 %collective-permute-start = (s32[32]{0:T(128)}, s32[32]{0:T(128)S(1)}, u32[]{:S(2)}, u32[]{:S(2)}) collective-permute-start(s32[32]{0:T(128)} %bitcast.40), channel_id=1, source_target_pairs={{0,1},{1,0},{2,3},{3,2},{4,5},{5,4},{6,7},{7,6},{8,9},{9,8},{10,11... | collective-permute-start | bytes 392 | tf_op jit(solution)/shard_map/ppermute | solution.py:16
  3.7 35.8 %copy-start = (bf16[1,1,1024,1024]{3,2,1,0:T(8,128)(2,1)S(1)}, bf16[1,1,1024,1024]{3,2,1,0:T(8,128)(2,1)}, u32[]{:S(2)}) copy-start(bf16[1,1,1024,1024]{3,2,1,0:T(8,128)(2,1)} %param.9) | copy-start | bytes 6291460
  4.8 20.0 %collective-permute-start.6 = (bf16[256,128]{1,0:T(8,128)(2,1)S(1)}, bf16[256,128]{1,0:T(8,128)(2,1)S(1)}, u32[]{:S(2)}, u32[]{:S(2)}) collective-permute-start(bf16[256,128]{1,0:T(8,128)(2,1)S(1)} %get-tuple-element.87.refs_3_), channel_id=1, source_target_pairs={{8,16},{16,8},{9,17},{17,9},{10,18},{18,10},{11,19},{19,11},{12,20... | collective-permute-start | bytes 196616 | tf_op jit(solution)/shard_map/ppermute | solution.py:373
  5.5 19.4 %collective-permute-start.5 = (bf16[256,128]{1,0:T(8,128)(2,1)S(1)}, bf16[256,128]{1,0:T(8,128)(2,1)}, u32[]{:S(2)}, u32[]{:S(2)}) collective-permute-start(bf16[256,128]{1,0:T(8,128)(2,1)S(1)} %get-tuple-element.85.refs_1_), channel_id=1, source_target_pairs={{1,2},{3,4},{5,6},{2,1},{4,3},{6,5},{9,10},{11,12},{13,14},{10,9},... | collective-permute-start | bytes 196616 | tf_op jit(solution)/shard_map/ppermute | solution.py:373
  6.7 10.3 %collective-permute-start.2 = (bf16[256,128]{1,0:T(8,128)(2,1)S(1)}, bf16[256,128]{1,0:T(8,128)(2,1)S(1)}, u32[]{:S(2)}, u32[]{:S(2)}) collective-permute-start(bf16[256,128]{1,0:T(8,128)(2,1)S(1)} %get-tuple-element.84.refs_0_), channel_id=1, source_target_pairs={{0,1},{2,3},{4,5},{6,7},{1,0},{3,2},{5,4},{7,6},{8,9},{10,11},{12,... | collective-permute-start | bytes 196616 | tf_op jit(solution)/shard_map/ppermute | solution.py:373
  10.5 7.2 %collective-permute-start.3 = (bf16[256,128]{1,0:T(8,128)(2,1)S(1)}, bf16[256,128]{1,0:T(8,128)(2,1)S(1)}, u32[]{:S(2)}, u32[]{:S(2)}) collective-permute-start(bf16[256,128]{1,0:T(8,128)(2,1)S(1)} %get-tuple-element.86.refs_2_), channel_id=1, source_target_pairs={{0,8},{16,24},{8,0},{24,16},{1,9},{17,25},{9,1},{25,17},{2,10},{18... | collective-permute-start | bytes 196616 | tf_op jit(solution)/shard_map/ppermute | solution.py:373
  13.5 3.5 %collective-permute-start.1 = (s32[64]{0:T(128)S(1)}, s32[64]{0:T(128)S(1)}, u32[]{:S(2)}, u32[]{:S(2)}) collective-permute-start(s32[64]{0:T(128)S(1)} %pad_add_fusion.2), channel_id=1, source_target_pairs={{0,2},{1,3},{2,0},{3,1},{4,6},{5,7},{6,4},{7,5},{8,10},{9,11},{10,... | collective-permute-start | bytes 776 | tf_op jit(solution)/shard_map/ppermute | solution.py:16
  17.0 0.6 copy-start.3
  17.7 0.6 copy-start.5
  19.6 5.2 %collective-permute-start.4 = (s32[128]{0:T(128)}, s32[128]{0:T(128)S(1)}, u32[]{:S(2)}, u32[]{:S(2)}) collective-permute-start(s32[128]{0:T(128)} %pad_add_fusion.3), channel_id=1, source_target_pairs={{0,4},{1,5},{2,6},{3,7},{4,0},{5,1},{6,2},{7,3},{8,12},{9,13},{10,... | collective-permute-start | bytes 1544 | tf_op jit(solution)/shard_map/ppermute | solution.py:16
  22.2 0.7 copy-start.8
  22.9 0.7 copy-start.9
  25.6 1.0 copy-start.7
  27.2 5.9 %collective-permute-start.7 = (bf16[4,32,256]{2,1,0:T(8,128)(2,1)S(1)}, bf16[4,32,256]{2,1,0:T(8,128)(2,1)S(1)}, u32[]{:S(2)}, u32[]{:S(2)}) collective-permute-start(bf16[4,32,256]{2,1,0:T(8,128)(2,1)S(1)} %slice.25), channel_id=1, source_target_pairs={{0,4},{1,5},{2,6},{3,7},{4,0},{5,1},{6,2},{7,3},{8,12},{9,13},{10,... | collective-permute-start | bytes 196616 | tf_op jit(solution)/shard_map/ppermute | solution.py:16
  29.2 0.8 copy-start.4
  30.0 0.8 copy-start.6
  33.2 5.8 %collective-permute-start.8 = (bf16[2,32,256]{2,1,0:T(8,128)(2,1)S(1)}, bf16[2,32,256]{2,1,0:T(8,128)(2,1)S(1)}, u32[]{:S(2)}, u32[]{:S(2)}) collective-permute-start(bf16[2,32,256]{2,1,0:T(8,128)(2,1)S(1)} %slice.27), channel_id=1, source_target_pairs={{0,2},{1,3},{2,0},{3,1},{4,6},{5,7},{6,4},{7,5},{8,10},{9,11},{10,... | collective-permute-start | bytes 98312 | tf_op jit(solution)/shard_map/ppermute | solution.py:16
  33.5 3.8 %collective-permute-start.10 = (f32[32,128]{1,0:T(8,128)S(1)}, f32[32,128]{1,0:T(8,128)S(1)}, u32[]{:S(2)}, u32[]{:S(2)}) collective-permute-start(f32[32,128]{1,0:T(8,128)S(1)} %get-tuple-element.96.own), channel_id=1, source_target_pairs={{0,1},{1,0},{2,3},{3,2},{4,5},{5,4},{6,7},{7,6},{8,9},{9,8},{10,11... | collective-permute-start | bytes 49160 | tf_op jit(solution)/shard_map/ppermute | solution.py:16
  37.3 3.9 %collective-permute-start.11 = (f32[64,128]{1,0:T(8,128)S(1)}, f32[64,128]{1,0:T(8,128)S(1)}, u32[]{:S(2)}, u32[]{:S(2)}) collective-permute-start(f32[64,128]{1,0:T(8,128)S(1)} %fold.6.own), channel_id=1, source_target_pairs={{0,2},{1,3},{2,0},{3,1},{4,6},{5,7},{6,4},{7,5},{8,10},{9,11},{10,... | collective-permute-start | bytes 98312 | tf_op jit(solution)/shard_map/ppermute | solution.py:16
  39.1 3.8 %collective-permute-start.9 = (bf16[1,32,256]{2,1,0:T(8,128)(2,1)S(1)}, bf16[1,32,256]{2,1,0:T(8,128)(2,1)S(1)}, u32[]{:S(2)}, u32[]{:S(2)}) collective-permute-start(bf16[1,32,256]{2,1,0:T(8,128)(2,1)S(1)} %slice.29), channel_id=1, source_target_pairs={{0,1},{1,0},{2,3},{3,2},{4,5},{5,4},{6,7},{7,6},{8,9},{9,8},{10,11... | collective-permute-start | bytes 49160 | tf_op jit(solution)/shard_map/ppermute | solution.py:16
  39.5 13.0 %copy-start.1 = (bf16[1,1,1024,1024]{3,2,1,0:T(8,128)(2,1)S(1)}, bf16[1,1,1024,1024]{3,2,1,0:T(8,128)(2,1)}, u32[]{:S(2)}) copy-start(bf16[1,1,1024,1024]{3,2,1,0:T(8,128)(2,1)} %param.8) | copy-start | bytes 6291460
  41.3 5.2 %collective-permute-start.12 = (f32[128,128]{1,0:T(8,128)S(1)}, f32[128,128]{1,0:T(8,128)S(1)}, u32[]{:S(2)}, u32[]{:S(2)}) collective-permute-start(f32[128,128]{1,0:T(8,128)S(1)} %fold.7.own), channel_id=1, source_target_pairs={{0,4},{1,5},{2,6},{3,7},{4,0},{5,1},{6,2},{7,3},{8,12},{9,13},{10,... | collective-permute-start | bytes 196616 | tf_op jit(solution)/shard_map/ppermute | solution.py:16
  47.4 5.0 %collective-permute-start.13 = (f32[256,128]{1,0:T(8,128)S(1)}, f32[256,128]{1,0:T(8,128)S(1)}, u32[]{:S(2)}, u32[]{:S(2)}) collective-permute-start(f32[256,128]{1,0:T(8,128)S(1)} %get-tuple-element.97.refs_0_), channel_id=1, source_target_pairs={{0,1},{2,3},{4,5},{6,7},{1,0},{3,2},{5,4},{7,6},{8,9},{10,11},{12,... | collective-permute-start | bytes 393224 | tf_op jit(solution)/shard_map/ppermute | solution.py:373
  48.2 4.2 %collective-permute-start.14 = (f32[256,128]{1,0:T(8,128)S(1)}, f32[256,128]{1,0:T(8,128)S(1)}, u32[]{:S(2)}, u32[]{:S(2)}) collective-permute-start(f32[256,128]{1,0:T(8,128)S(1)} %get-tuple-element.98.refs_1_), channel_id=1, source_target_pairs={{1,2},{3,4},{5,6},{2,1},{4,3},{6,5},{9,10},{11,12},{13,14},{10,9},... | collective-permute-start | bytes 393224 | tf_op jit(solution)/shard_map/ppermute | solution.py:373
  48.9 3.6 %collective-permute-start.15 = (f32[256,128]{1,0:T(8,128)S(1)}, f32[256,128]{1,0:T(8,128)S(1)}, u32[]{:S(2)}, u32[]{:S(2)}) collective-permute-start(f32[256,128]{1,0:T(8,128)S(1)} %get-tuple-element.99.refs_2_), channel_id=1, source_target_pairs={{0,8},{16,24},{8,0},{24,16},{1,9},{17,25},{9,1},{25,17},{2,10},{18... | collective-permute-start | bytes 393224 | tf_op jit(solution)/shard_map/ppermute | solution.py:373
  49.0 3.5 %collective-permute-start.16 = (f32[256,128]{1,0:T(8,128)S(1)}, f32[256,128]{1,0:T(8,128)S(1)}, u32[]{:S(2)}, u32[]{:S(2)}) collective-permute-start(f32[256,128]{1,0:T(8,128)S(1)} %get-tuple-element.100.refs_3_), channel_id=1, source_target_pairs={{8,16},{16,8},{9,17},{17,9},{10,18},{18,10},{11,19},{19,11},{12,20... | collective-permute-start | bytes 393224 | tf_op jit(solution)/shard_map/ppermute | solution.py:373
  54.1 8.4 %collective-permute-start.17 = (f32[256,128]{1,0:T(8,128)S(1)}, f32[256,128]{1,0:T(8,128)S(1)}, u32[]{:S(2)}, u32[]{:S(2)}) collective-permute-start(f32[256,128]{1,0:T(8,128)S(1)} %get-tuple-element.102.refs_0_), channel_id=1, source_target_pairs={{0,1},{2,3},{4,5},{6,7},{1,0},{3,2},{5,4},{7,6},{8,9},{10,11},{12,... | collective-permute-start | bytes 393224 | tf_op jit(solution)/shard_map/ppermute | solution.py:373
  58.9 3.6 %collective-permute-start.18 = (f32[256,128]{1,0:T(8,128)S(1)}, f32[256,128]{1,0:T(8,128)S(1)}, u32[]{:S(2)}, u32[]{:S(2)}) collective-permute-start(f32[256,128]{1,0:T(8,128)S(1)} %get-tuple-element.103.refs_1_), channel_id=1, source_target_pairs={{1,2},{3,4},{5,6},{2,1},{4,3},{6,5},{9,10},{11,12},{13,14},{10,9},... | collective-permute-start | bytes 393224 | tf_op jit(solution)/shard_map/ppermute | solution.py:373
  59.6 3.2 %collective-permute-start.19 = (f32[256,128]{1,0:T(8,128)S(1)}, f32[256,128]{1,0:T(8,128)S(1)}, u32[]{:S(2)}, u32[]{:S(2)}) collective-permute-start(f32[256,128]{1,0:T(8,128)S(1)} %get-tuple-element.104.refs_2_), channel_id=1, source_target_pairs={{0,8},{16,24},{8,0},{24,16},{1,9},{17,25},{9,1},{25,17},{2,10},{18... | collective-permute-start | bytes 393224 | tf_op jit(solution)/shard_map/ppermute | solution.py:373
  61.8 1.0 collective-permute-start.20
  64.4 7.5 %collective-permute-start.21 = (f32[176,128]{1,0:T(8,128)S(1)}, f32[176,128]{1,0:T(8,128)S(1)}, u32[]{:S(2)}, u32[]{:S(2)}) collective-permute-start(f32[176,128]{1,0:T(8,128)S(1)} %get-tuple-element.107.own), channel_id=1, source_target_pairs={{0,1},{1,0},{2,3},{3,2},{4,5},{5,4},{6,7},{7,6},{8,9},{9,8},{10,11... | collective-permute-start | bytes 270344 | tf_op jit(solution)/shard_map/ppermute | solution.py:16
  71.8 7.9 %collective-permute-start.22 = (f32[208,128]{1,0:T(8,128)S(1)}, f32[208,128]{1,0:T(8,128)S(1)}, u32[]{:S(2)}, u32[]{:S(2)}) collective-permute-start(f32[208,128]{1,0:T(8,128)S(1)} %fold.8.own), channel_id=1, source_target_pairs={{0,2},{1,3},{2,0},{3,1},{4,6},{5,7},{6,4},{7,5},{8,10},{9,11},{10,... | collective-permute-start | bytes 319496 | tf_op jit(solution)/shard_map/ppermute | solution.py:16
  79.7 9.6 %collective-permute-start.23 = (f32[272,128]{1,0:T(8,128)S(1)}, f32[272,128]{1,0:T(8,128)S(1)}, u32[]{:S(2)}, u32[]{:S(2)}) collective-permute-start(f32[272,128]{1,0:T(8,128)S(1)} %fold.9.own), channel_id=1, source_target_pairs={{0,4},{1,5},{2,6},{3,7},{4,0},{5,1},{6,2},{7,3},{8,12},{9,13},{10,... | collective-permute-start | bytes 417800 | tf_op jit(solution)/shard_map/ppermute | solution.py:16
  90.4 6.0 %collective-permute-start.26 = (f32[400,128]{1,0:T(8,128)S(1)}, f32[400,128]{1,0:T(8,128)S(1)}, u32[]{:S(2)}, u32[]{:S(2)}) collective-permute-start(f32[400,128]{1,0:T(8,128)S(1)} %get-tuple-element.110.refs_2_), channel_id=1, source_target_pairs={{0,8},{16,24},{8,0},{24,16},{1,9},{17,25},{9,1},{25,17},{2,10},{18... | collective-permute-start | bytes 614408 | tf_op jit(solution)/shard_map/ppermute | solution.py:373
  90.4 5.9 %collective-permute-start.24 = (f32[256,128]{1,0:T(8,128)S(1)}, f32[256,128]{1,0:T(8,128)S(1)}, u32[]{:S(2)}, u32[]{:S(2)}) collective-permute-start(f32[256,128]{1,0:T(8,128)S(1)} %get-tuple-element.108.refs_0_), channel_id=1, source_target_pairs={{0,1},{2,3},{4,5},{6,7},{1,0},{3,2},{5,4},{7,6},{8,9},{10,11},{12,... | collective-permute-start | bytes 393224 | tf_op jit(solution)/shard_map/ppermute | solution.py:373
  90.5 5.8 %collective-permute-start.25 = (f32[256,128]{1,0:T(8,128)S(1)}, f32[256,128]{1,0:T(8,128)S(1)}, u32[]{:S(2)}, u32[]{:S(2)}) collective-permute-start(f32[256,128]{1,0:T(8,128)S(1)} %get-tuple-element.109.refs_1_), channel_id=1, source_target_pairs={{1,2},{3,4},{5,6},{2,1},{4,3},{6,5},{9,10},{11,12},{13,14},{10,9},... | collective-permute-start | bytes 393224 | tf_op jit(solution)/shard_map/ppermute | solution.py:373
  91.2 5.2 %collective-permute-start.27 = (f32[256,128]{1,0:T(8,128)S(1)}, f32[256,128]{1,0:T(8,128)S(1)}, u32[]{:S(2)}, u32[]{:S(2)}) collective-permute-start(f32[256,128]{1,0:T(8,128)S(1)} %get-tuple-element.111.refs_3_), channel_id=1, source_target_pairs={{8,16},{16,8},{9,17},{17,9},{10,18},{18,10},{11,19},{19,11},{12,20... | collective-permute-start | bytes 393224 | tf_op jit(solution)/shard_map/ppermute | solution.py:373
  98.0 13.9 %collective-permute-start.29 = (f32[256,128]{1,0:T(8,128)S(1)}, f32[256,128]{1,0:T(8,128)S(1)}, u32[]{:S(2)}, u32[]{:S(2)}) collective-permute-start(f32[256,128]{1,0:T(8,128)S(1)} %get-tuple-element.114.refs_0_), channel_id=1, source_target_pairs={{0,1},{2,3},{4,5},{6,7},{1,0},{3,2},{5,4},{7,6},{8,9},{10,11},{12,... | collective-permute-start | bytes 393224 | tf_op jit(solution)/shard_map/ppermute | solution.py:373
  102.5 9.3 %collective-permute-start.30 = (f32[256,128]{1,0:T(8,128)S(1)}, f32[256,128]{1,0:T(8,128)S(1)}, u32[]{:S(2)}, u32[]{:S(2)}) collective-permute-start(f32[256,128]{1,0:T(8,128)S(1)} %get-tuple-element.115.refs_1_), channel_id=1, source_target_pairs={{1,2},{3,4},{5,6},{2,1},{4,3},{6,5},{9,10},{11,12},{13,14},{10,9},... | collective-permute-start | bytes 393224 | tf_op jit(solution)/shard_map/ppermute | solution.py:373
  103.2 8.6 %collective-permute-start.31 = (f32[256,128]{1,0:T(8,128)S(1)}, f32[256,128]{1,0:T(8,128)S(1)}, u32[]{:S(2)}, u32[]{:S(2)}) collective-permute-start(f32[256,128]{1,0:T(8,128)S(1)} %get-tuple-element.116.refs_2_), channel_id=1, source_target_pairs={{0,8},{16,24},{8,0},{24,16},{1,9},{17,25},{9,1},{25,17},{2,10},{18... | collective-permute-start | bytes 393224 | tf_op jit(solution)/shard_map/ppermute | solution.py:373
  103.3 8.6 %collective-permute-start.32 = (f32[256,128]{1,0:T(8,128)S(1)}, f32[256,128]{1,0:T(8,128)S(1)}, u32[]{:S(2)}, u32[]{:S(2)}) collective-permute-start(f32[256,128]{1,0:T(8,128)S(1)} %get-tuple-element.117.refs_3_), channel_id=1, source_target_pairs={{8,16},{16,8},{9,17},{17,9},{10,18},{18,10},{11,19},{19,11},{12,20... | collective-permute-start | bytes 393224 | tf_op jit(solution)/shard_map/ppermute | solution.py:373
  104.1 7.7 %collective-permute-start.28 = (f32[144,128]{1,0:T(8,128)S(1)}, f32[144,128]{1,0:T(8,128)S(1)}, u32[]{:S(2)}, u32[]{:S(2)}) collective-permute-start(f32[144,128]{1,0:T(8,128)S(1)} %get-tuple-element.112), channel_id=1, source_target_pairs={{0,16},{8,24},{16,0},{24,8},{1,17},{9,25},{17,1},{25,9},{2,18},{10... | collective-permute-start | bytes 221192 | tf_op jit(solution)/shard_map/ppermute | solution.py:16
  118.6 5.7 %collective-permute-start.33 = (f32[176,128]{1,0:T(8,128)S(1)}, f32[176,128]{1,0:T(8,128)S(1)}, u32[]{:S(2)}, u32[]{:S(2)}) collective-permute-start(f32[176,128]{1,0:T(8,128)S(1)} %get-tuple-element.119.own), channel_id=1, source_target_pairs={{0,1},{1,0},{2,3},{3,2},{4,5},{5,4},{6,7},{7,6},{8,9},{9,8},{10,11... | collective-permute-start | bytes 270344 | tf_op jit(solution)/shard_map/ppermute | solution.py:16
  124.3 5.6 %collective-permute-start.34 = (f32[208,128]{1,0:T(8,128)S(1)}, f32[208,128]{1,0:T(8,128)S(1)}, u32[]{:S(2)}, u32[]{:S(2)}) collective-permute-start(f32[208,128]{1,0:T(8,128)S(1)} %fold.10.own), channel_id=1, source_target_pairs={{0,2},{1,3},{2,0},{3,1},{4,6},{5,7},{6,4},{7,5},{8,10},{9,11},{10,... | collective-permute-start | bytes 319496 | tf_op jit(solution)/shard_map/ppermute | solution.py:16
  129.9 7.6 %collective-permute-start.35 = (f32[272,128]{1,0:T(8,128)S(1)}, f32[272,128]{1,0:T(8,128)S(1)}, u32[]{:S(2)}, u32[]{:S(2)}) collective-permute-start(f32[272,128]{1,0:T(8,128)S(1)} %fold.11.own), channel_id=1, source_target_pairs={{0,4},{1,5},{2,6},{3,7},{4,0},{5,1},{6,2},{7,3},{8,12},{9,13},{10,... | collective-permute-start | bytes 417800 | tf_op jit(solution)/shard_map/ppermute | solution.py:16
  138.5 6.2 %collective-permute-start.38 = (f32[400,128]{1,0:T(8,128)S(1)}, f32[400,128]{1,0:T(8,128)S(1)}, u32[]{:S(2)}, u32[]{:S(2)}) collective-permute-start(f32[400,128]{1,0:T(8,128)S(1)} %get-tuple-element.125.refs_2_), channel_id=1, source_target_pairs={{0,8},{16,24},{8,0},{24,16},{1,9},{17,25},{9,1},{25,17},{2,10},{18... | collective-permute-start | bytes 614408 | tf_op jit(solution)/shard_map/ppermute | solution.py:373
  138.6 6.1 %collective-permute-start.36 = (f32[256,128]{1,0:T(8,128)S(1)}, f32[256,128]{1,0:T(8,128)S(1)}, u32[]{:S(2)}, u32[]{:S(2)}) collective-permute-start(f32[256,128]{1,0:T(8,128)S(1)} %get-tuple-element.123.refs_0_), channel_id=1, source_target_pairs={{0,1},{2,3},{4,5},{6,7},{1,0},{3,2},{5,4},{7,6},{8,9},{10,11},{12,... | collective-permute-start | bytes 393224 | tf_op jit(solution)/shard_map/ppermute | solution.py:373
  140.6 4.1 %collective-permute-start.37 = (f32[256,128]{1,0:T(8,128)S(1)}, f32[256,128]{1,0:T(8,128)S(1)}, u32[]{:S(2)}, u32[]{:S(2)}) collective-permute-start(f32[256,128]{1,0:T(8,128)S(1)} %get-tuple-element.124.refs_1_), channel_id=1, source_target_pairs={{1,2},{3,4},{5,6},{2,1},{4,3},{6,5},{9,10},{11,12},{13,14},{10,9},... | collective-permute-start | bytes 393224 | tf_op jit(solution)/shard_map/ppermute | solution.py:373
  141.3 3.4 %collective-permute-start.39 = (f32[256,128]{1,0:T(8,128)S(1)}, f32[256,128]{1,0:T(8,128)S(1)}, u32[]{:S(2)}, u32[]{:S(2)}) collective-permute-start(f32[256,128]{1,0:T(8,128)S(1)} %get-tuple-element.126.refs_3_), channel_id=1, source_target_pairs={{8,16},{16,8},{9,17},{17,9},{10,18},{18,10},{11,19},{19,11},{12,20... | collective-permute-start | bytes 393224 | tf_op jit(solution)/shard_map/ppermute | solution.py:373
  146.3 13.9 %collective-permute-start.41 = (f32[256,128]{1,0:T(8,128)S(1)}, f32[256,128]{1,0:T(8,128)S(1)}, u32[]{:S(2)}, u32[]{:S(2)}) collective-permute-start(f32[256,128]{1,0:T(8,128)S(1)} %get-tuple-element.135.refs_0_), channel_id=1, source_target_pairs={{0,1},{2,3},{4,5},{6,7},{1,0},{3,2},{5,4},{7,6},{8,9},{10,11},{12,... | collective-permute-start | bytes 393224 | tf_op jit(solution)/shard_map/ppermute | solution.py:373
  150.9 9.3 %collective-permute-start.42 = (f32[256,128]{1,0:T(8,128)S(1)}, f32[256,128]{1,0:T(8,128)S(1)}, u32[]{:S(2)}, u32[]{:S(2)}) collective-permute-start(f32[256,128]{1,0:T(8,128)S(1)} %get-tuple-element.136.refs_1_), channel_id=1, source_target_pairs={{1,2},{3,4},{5,6},{2,1},{4,3},{6,5},{9,10},{11,12},{13,14},{10,9},... | collective-permute-start | bytes 393224 | tf_op jit(solution)/shard_map/ppermute | solution.py:373
  151.6 8.6 %collective-permute-start.43 = (f32[256,128]{1,0:T(8,128)S(1)}, f32[256,128]{1,0:T(8,128)S(1)}, u32[]{:S(2)}, u32[]{:S(2)}) collective-permute-start(f32[256,128]{1,0:T(8,128)S(1)} %get-tuple-element.137.refs_2_), channel_id=1, source_target_pairs={{0,8},{16,24},{8,0},{24,16},{1,9},{17,25},{9,1},{25,17},{2,10},{18... | collective-permute-start | bytes 393224 | tf_op jit(solution)/shard_map/ppermute | solution.py:373
  151.7 8.6 %collective-permute-start.44 = (f32[256,128]{1,0:T(8,128)S(1)}, f32[256,128]{1,0:T(8,128)S(1)}, u32[]{:S(2)}, u32[]{:S(2)}) collective-permute-start(f32[256,128]{1,0:T(8,128)S(1)} %get-tuple-element.138.refs_3_), channel_id=1, source_target_pairs={{8,16},{16,8},{9,17},{17,9},{10,18},{18,10},{11,19},{19,11},{12,20... | collective-permute-start | bytes 393224 | tf_op jit(solution)/shard_map/ppermute | solution.py:373
  152.6 7.6 %collective-permute-start.40 = (f32[144,128]{1,0:T(8,128)S(1)}, f32[144,128]{1,0:T(8,128)S(1)}, u32[]{:S(2)}, u32[]{:S(2)}) collective-permute-start(f32[144,128]{1,0:T(8,128)S(1)} %get-tuple-element.127), channel_id=1, source_target_pairs={{0,16},{8,24},{16,0},{24,8},{1,17},{9,25},{17,1},{25,9},{2,18},{10... | collective-permute-start | bytes 221192 | tf_op jit(solution)/shard_map/ppermute | solution.py:16
  166.9 1.3 collective-permute-start.45
  168.2 5.3 %collective-permute-start.46 = (f32[72,128]{1,0:T(8,128)S(1)}, f32[72,128]{1,0:T(8,128)S(1)}, u32[]{:S(2)}, u32[]{:S(2)}) collective-permute-start(f32[72,128]{1,0:T(8,128)S(1)} %add.69), channel_id=1, source_target_pairs={{0,1},{1,0},{2,3},{3,2},{4,5},{5,4},{6,7},{7,6},{8,9},{9,8},{10,11... | collective-permute-start | bytes 110600 | tf_op jit(solution)/shard_map/ppermute | solution.py:16
  173.6 5.0 %collective-permute-start.47 = (f32[72,128]{1,0:T(8,128)S(1)}, f32[72,128]{1,0:T(8,128)S(1)}, u32[]{:S(2)}, u32[]{:S(2)}) collective-permute-start(f32[72,128]{1,0:T(8,128)S(1)} %add.70), channel_id=1, source_target_pairs={{0,16},{8,24},{16,0},{24,8},{1,17},{9,25},{17,1},{25,9},{2,18},{10... | collective-permute-start | bytes 110600 | tf_op jit(solution)/shard_map/ppermute | solution.py:16
  178.6 4.0 %collective-permute-start.48 = (f32[72,128]{1,0:T(8,128)S(1)}, f32[72,128]{1,0:T(8,128)S(1)}, u32[]{:S(2)}, u32[]{:S(2)}) collective-permute-start(f32[72,128]{1,0:T(8,128)S(1)} %add.71), channel_id=1, source_target_pairs={{0,2},{1,3},{2,0},{3,1},{4,6},{5,7},{6,4},{7,5},{8,10},{9,11},{10,... | collective-permute-start | bytes 110600 | tf_op jit(solution)/shard_map/ppermute | solution.py:16
  182.7 5.8 %collective-permute-start.49 = (f32[72,128]{1,0:T(8,128)S(1)}, f32[72,128]{1,0:T(8,128)S(1)}, u32[]{:S(2)}, u32[]{:S(2)}) collective-permute-start(f32[72,128]{1,0:T(8,128)S(1)} %add.72), channel_id=1, source_target_pairs={{0,4},{1,5},{2,6},{3,7},{4,0},{5,1},{6,2},{7,3},{8,12},{9,13},{10,... | collective-permute-start | bytes 110600 | tf_op jit(solution)/shard_map/ppermute | solution.py:16
  188.4 1.2 collective-permute-start.50

commit v5 on v3

--- a/solution.py
+++ b/solution.py
@@ -25,13 +25,15 @@
 
 def total(kept, sent, ride):
     half = kept + swap(sent, "group", 1)
-    rest = [("group", bit) for bit in bits_of("group")[1:]]
-    subs = [("sub", bit) for bit in bits_of("sub")]
-    for number, (axis, bit) in enumerate(subs[:1] + rest + subs[1:]):
-        arrived = swap(half, axis, bit)
-        if number == 1:
+    subs = bits_of("sub")
+    rounds = [[("sub", bit)] for bit in subs[:-2]]
+    rounds += [[("group", bit)] for bit in bits_of("group")[1:]]
+    rounds += [[("sub", bit) for bit in (*subs[-2:], sum(subs[-2:]))]]
+    for number, partners in enumerate(rounds):
+        arrived = [swap(half, axis, bit) for axis, bit in partners]
+        if number + 1 == len(rounds):
             arrived, ride = lax.optimization_barrier((arrived, ride))
-        half = half + arrived
+        half = half + sum(arrived[1:], arrived[0])
     return half, swap(half, "group", 1), ride
 
 

time: 196 us -> 194 us (0.990)
    ppermute x23 -> x24, waiting for transfers between devices: 49.3 us -> 47.9 us  [swap(): lax.ppermute(x, axis, [(i, i ^ bit) for i in range(lax.axis_size(axis))])]
    ppermute x23 -> x24, starting transfers between devices: 46.7 us -> 46.3 us  [swap(): lax.ppermute(x, axis, [(i, i ^ bit) for i in range(lax.axis_size(axis))])]
  transfers between devices with their start and end apart: 51 -> 52, of which waited for: 23 -> 22; matrix products, arithmetic and copies ran while one was open for 2% -> 2% of each run, Pallas kernels for 7% -> 7%
where the time goes in v5:
time: 194 us
  starting transfers between devices  81.2 us (42%)
  waiting for transfers between devices  59.1 us (30%)
  Pallas kernels  42.9 us (22%)
  local copies, waits for them, and re-layouts  6.37 us (3%)
  other arithmetic  2.88 us (1%)
    ppermute x24, waiting for transfers between devices, swap(): lax.ppermute(x, axis, [(i, i ^ bit) for i in range(lax.axis_size(axis))])  47.9 us
    ppermute x24, starting transfers between devices, swap(): lax.ppermute(x, axis, [(i, i ^ bit) for i in range(lax.axis_size(axis))])  46.3 us
    pallas_call x24, Pallas kernels, call(): pl.pallas_call(kernel, out_shape=shapes, in_specs=[SMEM if a.ndim == 1 el...  42.9 us
    ppermute x28, starting transfers between devices, exchange(): lax.ppermute(slot, axis, pairs(axis, first))  34.9 us
    ppermute x28, waiting for transfers between devices, exchange(): lax.ppermute(slot, axis, pairs(axis, first))  11.2 us
    unnamed x20, local copies, waits for them, and re-layouts  5.25 us
  transfers between devices with their start and end apart: 52, of which 22 were waited for; matrix products, arithmetic and copies ran while one was open for 2% of the time, Pallas kernels for 7%

profile of v5, /device:TPU:0, one launch (start us, length us, event | category | flops | bytes accessed | tf_op | source)
XLA Modules:
  0.0 193.5 jit_solution(5330980420962206797)
XLA Ops:
  0.6 3.0 %collective-permute-start = (s32[32]{0:T(128)}, s32[32]{0:T(128)S(1)}, u32[]{:S(2)}, u32[]{:S(2)}) collective-permute-start(s32[32]{0:T(128)} %bitcast.40), channel_id=1, source_target_pairs={{0,1},{1,0},{2,3},{3,2},{4,5},{5,4},{6,7},{7,6},{8,9},{9,8},{10,11... | collective-permute-start | bytes 392 | tf_op jit(solution)/shard_map/ppermute | solution.py:16
  3.7 1.1 dynamic-slice_bitcast_fusion
  5.5 1.3 collective-permute-start.5
  6.8 3.7 %collective-permute-start.2 = (bf16[256,128]{1,0:T(8,128)(2,1)S(1)}, bf16[256,128]{1,0:T(8,128)(2,1)S(1)}, u32[]{:S(2)}, u32[]{:S(2)}) collective-permute-start(bf16[256,128]{1,0:T(8,128)(2,1)S(1)} %get-tuple-element.84.refs_0_), channel_id=1, source_target_pairs={{0,1},{2,3},{4,5},{6,7},{1,0},{3,2},{5,4},{7,6},{8,9},{10,11},{12,... | collective-permute-start | bytes 196616 | tf_op jit(solution)/shard_map/ppermute | solution.py:375
  10.5 2.3 %collective-permute-start.3 = (bf16[256,128]{1,0:T(8,128)(2,1)S(1)}, bf16[256,128]{1,0:T(8,128)(2,1)S(1)}, u32[]{:S(2)}, u32[]{:S(2)}) collective-permute-start(bf16[256,128]{1,0:T(8,128)(2,1)S(1)} %get-tuple-element.86.refs_2_), channel_id=1, source_target_pairs={{0,8},{16,24},{8,0},{24,16},{1,9},{17,25},{9,1},{25,17},{2,10},{18... | collective-permute-start | bytes 196616 | tf_op jit(solution)/shard_map/ppermute | solution.py:375
  13.5 1.6 collective-permute-start.1
  15.2 1.9 collective-permute-done.1
  18.3 1.3 pad_add_fusion.3
  19.6 2.6 %collective-permute-start.4 = (s32[128]{0:T(128)}, s32[128]{0:T(128)S(1)}, u32[]{:S(2)}, u32[]{:S(2)}) collective-permute-start(s32[128]{0:T(128)} %pad_add_fusion.3), channel_id=1, source_target_pairs={{0,4},{1,5},{2,6},{3,7},{4,0},{5,1},{6,2},{7,3},{8,12},{9,13},{10,... | collective-permute-start | bytes 1544 | tf_op jit(solution)/shard_map/ppermute | solution.py:16
  23.5 1.2 shared_row_tables.1
  25.5 0.9 copy-done.7
  27.2 1.9 collective-permute-start.7
  29.1 0.8 copy-done.4
  30.8 1.4 start.1
  32.2 0.9 collective-permute-done.7
  33.8 3.5 %collective-permute-done.10.received = f32[32,128]{1,0:T(8,128)S(1)} collective-permute-done((f32[32,128]{1,0:T(8,128)S(1)}, f32[32,128]{1,0:T(8,128)S(1)}, u32[]{:S(2)}, u32[]{:S(2)}) %collective-permute-start.10) | collective-permute-done | bytes 16416 | tf_op jit(solution)/shard_map/ppermute | solution.py:16
  37.3 1.7 collective-permute-start.11
  40.2 1.0 collective-permute-done.11.received
  41.2 1.0 collective-permute-start.12
  42.8 3.6 %collective-permute-done.12.received = f32[128,128]{1,0:T(8,128)S(1)} collective-permute-done((f32[128,128]{1,0:T(8,128)S(1)}, f32[128,128]{1,0:T(8,128)S(1)}, u32[]{:S(2)}, u32[]{:S(2)}) %collective-permute-start.12) | collective-permute-done | bytes 65568 | tf_op jit(solution)/shard_map/ppermute | solution.py:16
  46.4 1.0 coarse_part.3
  49.6 2.8 %collective-permute-done.13.refs_4_ = f32[256,128]{1,0:T(8,128)S(1)} collective-permute-done((f32[256,128]{1,0:T(8,128)S(1)}, f32[256,128]{1,0:T(8,128)S(1)}, u32[]{:S(2)}, u32[]{:S(2)}) %collective-permute-start.13) | collective-permute-done | bytes 131104 | tf_op jit(solution)/shard_map/ppermute | solution.py:375
  52.4 1.6 operator.3
  54.0 4.9 %collective-permute-start.17 = (f32[256,128]{1,0:T(8,128)S(1)}, f32[256,128]{1,0:T(8,128)S(1)}, u32[]{:S(2)}, u32[]{:S(2)}) collective-permute-start(f32[256,128]{1,0:T(8,128)S(1)} %get-tuple-element.102.refs_0_), channel_id=1, source_target_pairs={{0,1},{2,3},{4,5},{6,7},{1,0},{3,2},{5,4},{7,6},{8,9},{10,11},{12,... | collective-permute-start | bytes 393224 | tf_op jit(solution)/shard_map/ppermute | solution.py:375
  59.5 2.3 %collective-permute-start.19 = (f32[256,128]{1,0:T(8,128)S(1)}, f32[256,128]{1,0:T(8,128)S(1)}, u32[]{:S(2)}, u32[]{:S(2)}) collective-permute-start(f32[256,128]{1,0:T(8,128)S(1)} %get-tuple-element.104.refs_2_), channel_id=1, source_target_pairs={{0,8},{16,24},{8,0},{24,16},{1,9},{17,25},{9,1},{25,17},{2,10},{18... | collective-permute-start | bytes 393224 | tf_op jit(solution)/shard_map/ppermute | solution.py:375
  62.8 1.5 start_grams.1
  64.3 4.9 %collective-permute-start.21 = (f32[176,128]{1,0:T(8,128)S(1)}, f32[176,128]{1,0:T(8,128)S(1)}, u32[]{:S(2)}, u32[]{:S(2)}) collective-permute-start(f32[176,128]{1,0:T(8,128)S(1)} %get-tuple-element.107.own), channel_id=1, source_target_pairs={{0,1},{1,0},{2,3},{3,2},{4,5},{5,4},{6,7},{7,6},{8,9},{9,8},{10,11... | collective-permute-start | bytes 270344 | tf_op jit(solution)/shard_map/ppermute | solution.py:16
  69.3 2.5 %collective-permute-done.21.received = f32[176,128]{1,0:T(8,128)S(1)} collective-permute-done((f32[176,128]{1,0:T(8,128)S(1)}, f32[176,128]{1,0:T(8,128)S(1)}, u32[]{:S(2)}, u32[]{:S(2)}) %collective-permute-start.21) | collective-permute-done | bytes 90144 | tf_op jit(solution)/shard_map/ppermute | solution.py:16
  71.8 4.1 %collective-permute-start.22 = (f32[208,128]{1,0:T(8,128)S(1)}, f32[208,128]{1,0:T(8,128)S(1)}, u32[]{:S(2)}, u32[]{:S(2)}) collective-permute-start(f32[208,128]{1,0:T(8,128)S(1)} %fold.8.own), channel_id=1, source_target_pairs={{0,2},{1,3},{2,0},{3,1},{4,6},{5,7},{6,4},{7,5},{8,10},{9,11},{10,... | collective-permute-start | bytes 319496 | tf_op jit(solution)/shard_map/ppermute | solution.py:16
  75.9 3.8 %collective-permute-done.22.received = f32[208,128]{1,0:T(8,128)S(1)} collective-permute-done((f32[208,128]{1,0:T(8,128)S(1)}, f32[208,128]{1,0:T(8,128)S(1)}, u32[]{:S(2)}, u32[]{:S(2)}) %collective-permute-start.22) | collective-permute-done | bytes 106528 | tf_op jit(solution)/shard_map/ppermute | solution.py:16
  80.5 8.8 %collective-permute-done.23.received = f32[272,128]{1,0:T(8,128)S(1)} collective-permute-done((f32[272,128]{1,0:T(8,128)S(1)}, f32[272,128]{1,0:T(8,128)S(1)}, u32[]{:S(2)}, u32[]{:S(2)}) %collective-permute-start.23) | collective-permute-done | bytes 139296 | tf_op jit(solution)/shard_map/ppermute | solution.py:16
  89.3 1.0 coarse_part.4
  91.8 4.5 %collective-permute-done.24.refs_4_ = f32[256,128]{1,0:T(8,128)S(1)} collective-permute-done((f32[256,128]{1,0:T(8,128)S(1)}, f32[256,128]{1,0:T(8,128)S(1)}, u32[]{:S(2)}, u32[]{:S(2)}) %collective-permute-start.24) | collective-permute-done | bytes 131104 | tf_op jit(solution)/shard_map/ppermute | solution.py:375
  96.3 1.6 operator.4
  97.9 4.6 %collective-permute-start.29 = (f32[256,128]{1,0:T(8,128)S(1)}, f32[256,128]{1,0:T(8,128)S(1)}, u32[]{:S(2)}, u32[]{:S(2)}) collective-permute-start(f32[256,128]{1,0:T(8,128)S(1)} %get-tuple-element.114.refs_0_), channel_id=1, source_target_pairs={{0,1},{2,3},{4,5},{6,7},{1,0},{3,2},{5,4},{7,6},{8,9},{10,11},{12,... | collective-permute-start | bytes 393224 | tf_op jit(solution)/shard_map/ppermute | solution.py:375
  103.2 0.8 collective-permute-start.32
  104.1 3.4 %collective-permute-start.28 = (f32[144,128]{1,0:T(8,128)S(1)}, f32[144,128]{1,0:T(8,128)S(1)}, u32[]{:S(2)}, u32[]{:S(2)}) collective-permute-start(f32[144,128]{1,0:T(8,128)S(1)} %get-tuple-element.112), channel_id=1, source_target_pairs={{0,16},{8,24},{16,0},{24,8},{1,17},{9,25},{17,1},{25,9},{2,18},{10... | collective-permute-start | bytes 221192 | tf_op jit(solution)/shard_map/ppermute | solution.py:16
  107.5 4.3 %collective-permute-done.28 = f32[144,128]{1,0:T(8,128)S(1)} collective-permute-done((f32[144,128]{1,0:T(8,128)S(1)}, f32[144,128]{1,0:T(8,128)S(1)}, u32[]{:S(2)}, u32[]{:S(2)}) %collective-permute-start.28) | collective-permute-done | bytes 73760 | tf_op jit(solution)/shard_map/ppermute | solution.py:16
  111.8 6.7 %first_update.1 = (f32[1024,128]{1,0:T(8,128)S(1)}, f32[1024,128]{1,0:T(8,128)S(1)}, f32[1024,128]{1,0:T(8,128)S(1)}, f32[1024,128]{1,0:T(8,128)S(1)}, f32[1024,...) custom-call(s32[2]{0:T(128)S(1)} %pad_add_fusion.1.parity, ...), custom_call_target="tpu_custom_call" | custom-call | flops 800000000 | bytes 7110664 | tf_op jit(solution)/shard_map/first_update/pallas_call | solution.py:356
  118.5 3.2 %collective-permute-start.33 = (f32[176,128]{1,0:T(8,128)S(1)}, f32[176,128]{1,0:T(8,128)S(1)}, u32[]{:S(2)}, u32[]{:S(2)}) collective-permute-start(f32[176,128]{1,0:T(8,128)S(1)} %get-tuple-element.119.own), channel_id=1, source_target_pairs={{0,1},{1,0},{2,3},{3,2},{4,5},{5,4},{6,7},{7,6},{8,9},{9,8},{10,11... | collective-permute-start | bytes 270344 | tf_op jit(solution)/shard_map/ppermute | solution.py:16
  121.7 2.5 %collective-permute-done.33.received = f32[176,128]{1,0:T(8,128)S(1)} collective-permute-done((f32[176,128]{1,0:T(8,128)S(1)}, f32[176,128]{1,0:T(8,128)S(1)}, u32[]{:S(2)}, u32[]{:S(2)}) %collective-permute-start.33) | collective-permute-done | bytes 90144 | tf_op jit(solution)/shard_map/ppermute | solution.py:16
  124.2 1.7 collective-permute-start.34
  125.9 3.1 %collective-permute-done.34.received = f32[208,128]{1,0:T(8,128)S(1)} collective-permute-done((f32[208,128]{1,0:T(8,128)S(1)}, f32[208,128]{1,0:T(8,128)S(1)}, u32[]{:S(2)}, u32[]{:S(2)}) %collective-permute-start.34) | collective-permute-done | bytes 106528 | tf_op jit(solution)/shard_map/ppermute | solution.py:16
  129.0 4.1 %collective-permute-start.35 = (f32[272,128]{1,0:T(8,128)S(1)}, f32[272,128]{1,0:T(8,128)S(1)}, u32[]{:S(2)}, u32[]{:S(2)}) collective-permute-start(f32[272,128]{1,0:T(8,128)S(1)} %fold.11.own), channel_id=1, source_target_pairs={{0,4},{1,5},{2,6},{3,7},{4,0},{5,1},{6,2},{7,3},{8,12},{9,13},{10,... | collective-permute-start | bytes 417800 | tf_op jit(solution)/shard_map/ppermute | solution.py:16
  133.8 3.8 %collective-permute-done.35.received = f32[272,128]{1,0:T(8,128)S(1)} collective-permute-done((f32[272,128]{1,0:T(8,128)S(1)}, f32[272,128]{1,0:T(8,128)S(1)}, u32[]{:S(2)}, u32[]{:S(2)}) %collective-permute-start.35) | collective-permute-done | bytes 139296 | tf_op jit(solution)/shard_map/ppermute | solution.py:16
  137.6 1.0 coarse_part.5
  138.7 1.0 collective-permute-start.36
  141.0 3.5 %collective-permute-done.36.refs_4_ = f32[256,128]{1,0:T(8,128)S(1)} collective-permute-done((f32[256,128]{1,0:T(8,128)S(1)}, f32[256,128]{1,0:T(8,128)S(1)}, u32[]{:S(2)}, u32[]{:S(2)}) %collective-permute-start.36) | collective-permute-done | bytes 131104 | tf_op jit(solution)/shard_map/ppermute | solution.py:375
  144.6 1.6 operator.5
  146.2 4.6 %collective-permute-start.41 = (f32[256,128]{1,0:T(8,128)S(1)}, f32[256,128]{1,0:T(8,128)S(1)}, u32[]{:S(2)}, u32[]{:S(2)}) collective-permute-start(f32[256,128]{1,0:T(8,128)S(1)} %get-tuple-element.133.refs_0_), channel_id=1, source_target_pairs={{0,1},{2,3},{4,5},{6,7},{1,0},{3,2},{5,4},{7,6},{8,9},{10,11},{12,... | collective-permute-start | bytes 393224 | tf_op jit(solution)/shard_map/ppermute | solution.py:375
  151.5 0.9 collective-permute-start.44
  152.4 3.4 %collective-permute-start.40 = (f32[144,128]{1,0:T(8,128)S(1)}, f32[144,128]{1,0:T(8,128)S(1)}, u32[]{:S(2)}, u32[]{:S(2)}) collective-permute-start(f32[144,128]{1,0:T(8,128)S(1)} %get-tuple-element.124), channel_id=1, source_target_pairs={{0,16},{8,24},{16,0},{24,8},{1,17},{9,25},{17,1},{25,9},{2,18},{10... | collective-permute-start | bytes 221192 | tf_op jit(solution)/shard_map/ppermute | solution.py:16
  155.8 3.9 %inner_inverse.2 = f32[128,128]{1,0:T(8,128)S(1)} custom-call(f32[144,128]{1,0:T(8,128)S(1)} %add.70.grams), custom_call_target="tpu_custom_call" | custom-call | flops 400000000 | bytes 139264 | tf_op jit(solution)/shard_map/inner_inverse/pallas_call | solution.py:356
  160.1 6.7 %next_update.1 = (f32[1024,128]{1,0:T(8,128)S(1)}, f32[1024,128]{1,0:T(8,128)S(1)}, f32[1024,128]{1,0:T(8,128)S(1)}, f32[1024,128]{1,0:T(8,128)S(1)}, f32[1024,1...) custom-call(s32[2]{0:T(128)S(1)} %pad_add_fusion.1.parity, ...), custom_call_target="tpu_custom_call" | custom-call | flops 800000000 | bytes 11419656 | tf_op jit(solution)/shard_map/next_update/pallas_call | solution.py:356
  166.8 1.2 collective-permute-done.45
  168.0 3.2 %collective-permute-start.46 = (f32[72,128]{1,0:T(8,128)S(1)}, f32[72,128]{1,0:T(8,128)S(1)}, u32[]{:S(2)}, u32[]{:S(2)}) collective-permute-start(f32[72,128]{1,0:T(8,128)S(1)} %add.72), channel_id=1, source_target_pairs={{0,1},{1,0},{2,3},{3,2},{4,5},{5,4},{6,7},{7,6},{8,9},{9,8},{10,11... | collective-permute-start | bytes 110600 | tf_op jit(solution)/shard_map/ppermute | solution.py:16
  171.2 1.9 collective-permute-done.46
  173.1 0.9 collective-permute-start.47
  174.0 3.1 %collective-permute-done.47 = f32[72,128]{1,0:T(8,128)S(1)} collective-permute-done((f32[72,128]{1,0:T(8,128)S(1)}, f32[72,128]{1,0:T(8,128)S(1)}, u32[]{:S(2)}, u32[]{:S(2)}) %collective-permute-start.47) | collective-permute-done | bytes 36896 | tf_op jit(solution)/shard_map/ppermute | solution.py:16
  177.1 2.8 %collective-permute-start.50 = (f32[72,128]{1,0:T(8,128)S(1)}, f32[72,128]{1,0:T(8,128)S(1)}, u32[]{:S(2)}, u32[]{:S(2)}) collective-permute-start(f32[72,128]{1,0:T(8,128)S(1)} %add.74), channel_id=1, source_target_pairs={{0,6},{1,7},{2,4},{3,5},{4,2},{5,3},{6,0},{7,1},{8,14},{9,15},{10,... | collective-permute-start | bytes 110600 | tf_op jit(solution)/shard_map/ppermute | solution.py:16
  180.4 1.1 collective-permute-start.48
  181.5 4.2 %inner_inverse.3 = f32[128,128]{1,0:T(8,128)S(1)} custom-call(f32[144,128]{1,0:T(8,128)S(1)} %add.71.grams), custom_call_target="tpu_custom_call" | custom-call | flops 400000000 | bytes 139264 | tf_op jit(solution)/shard_map/inner_inverse/pallas_call | solution.py:356
  185.8 1.2 collective-permute-done.51.other
  187.0 6.5 %last_update.1 = (f32[1024,128]{1,0:T(8,128)}, f32[1024,128]{1,0:T(8,128)}) custom-call(s32[2]{0:T(128)S(1)} %pad_add_fusion.1.parity, f32[72,128]{1,0:T(8,128)S(1)} %add_add_fusion.half, f32[72,128]{1,0:T(8,128)S(1)} %collective-permute-done.51.other, f32[128,128]{1,0:T(8,128)S(1)} %inner_inverse.3, f32[128,128]{1,0:T(8,128)S(1)} %get-tuple-element.145.curvature, ...), custom_call_target="tpu_custom_call" | custom-call | flops 800000000 | bytes 4399112 | tf_op jit(solution)/shard_map/last_update/pallas_call | solution.py:356
  (101 shorter events, 19.5 us)
Async XLA Ops:
  0.6 28.5 %copy-start.2 = (bf16[1,1,32,1024]{3,2,1,0:T(8,128)(2,1)S(1)}, bf16[1,1,32,1024]{3,2,1,0:T(8,128)(2,1)}, u32[]{:S(2)}) copy-start(bf16[1,1,32,1024]{3,2,1,0:T(8,128)(2,1)} %param.11) | copy-start | bytes 196612
  0.6 12.1 %collective-permute-start = (s32[32]{0:T(128)}, s32[32]{0:T(128)S(1)}, u32[]{:S(2)}, u32[]{:S(2)}) collective-permute-start(s32[32]{0:T(128)} %bitcast.40), channel_id=1, source_target_pairs={{0,1},{1,0},{2,3},{3,2},{4,5},{5,4},{6,7},{7,6},{8,9},{9,8},{10,11... | collective-permute-start | bytes 392 | tf_op jit(solution)/shard_map/ppermute | solution.py:16
  3.7 35.8 %copy-start = (bf16[1,1,1024,1024]{3,2,1,0:T(8,128)(2,1)S(1)}, bf16[1,1,1024,1024]{3,2,1,0:T(8,128)(2,1)}, u32[]{:S(2)}) copy-start(bf16[1,1,1024,1024]{3,2,1,0:T(8,128)(2,1)} %param.9) | copy-start | bytes 6291460
  4.8 20.0 %collective-permute-start.6 = (bf16[256,128]{1,0:T(8,128)(2,1)S(1)}, bf16[256,128]{1,0:T(8,128)(2,1)S(1)}, u32[]{:S(2)}, u32[]{:S(2)}) collective-permute-start(bf16[256,128]{1,0:T(8,128)(2,1)S(1)} %get-tuple-element.87.refs_3_), channel_id=1, source_target_pairs={{8,16},{16,8},{9,17},{17,9},{10,18},{18,10},{11,19},{19,11},{12,20... | collective-permute-start | bytes 196616 | tf_op jit(solution)/shard_map/ppermute | solution.py:375
  5.5 19.3 %collective-permute-start.5 = (bf16[256,128]{1,0:T(8,128)(2,1)S(1)}, bf16[256,128]{1,0:T(8,128)(2,1)}, u32[]{:S(2)}, u32[]{:S(2)}) collective-permute-start(bf16[256,128]{1,0:T(8,128)(2,1)S(1)} %get-tuple-element.85.refs_1_), channel_id=1, source_target_pairs={{1,2},{3,4},{5,6},{2,1},{4,3},{6,5},{9,10},{11,12},{13,14},{10,9},... | collective-permute-start | bytes 196616 | tf_op jit(solution)/shard_map/ppermute | solution.py:375
  6.8 10.3 %collective-permute-start.2 = (bf16[256,128]{1,0:T(8,128)(2,1)S(1)}, bf16[256,128]{1,0:T(8,128)(2,1)S(1)}, u32[]{:S(2)}, u32[]{:S(2)}) collective-permute-start(bf16[256,128]{1,0:T(8,128)(2,1)S(1)} %get-tuple-element.84.refs_0_), channel_id=1, source_target_pairs={{0,1},{2,3},{4,5},{6,7},{1,0},{3,2},{5,4},{7,6},{8,9},{10,11},{12,... | collective-permute-start | bytes 196616 | tf_op jit(solution)/shard_map/ppermute | solution.py:375
  10.5 7.2 %collective-permute-start.3 = (bf16[256,128]{1,0:T(8,128)(2,1)S(1)}, bf16[256,128]{1,0:T(8,128)(2,1)S(1)}, u32[]{:S(2)}, u32[]{:S(2)}) collective-permute-start(bf16[256,128]{1,0:T(8,128)(2,1)S(1)} %get-tuple-element.86.refs_2_), channel_id=1, source_target_pairs={{0,8},{16,24},{8,0},{24,16},{1,9},{17,25},{9,1},{25,17},{2,10},{18... | collective-permute-start | bytes 196616 | tf_op jit(solution)/shard_map/ppermute | solution.py:375
  13.5 3.5 %collective-permute-start.1 = (s32[64]{0:T(128)S(1)}, s32[64]{0:T(128)S(1)}, u32[]{:S(2)}, u32[]{:S(2)}) collective-permute-start(s32[64]{0:T(128)S(1)} %pad_add_fusion.2), channel_id=1, source_target_pairs={{0,2},{1,3},{2,0},{3,1},{4,6},{5,7},{6,4},{7,5},{8,10},{9,11},{10,... | collective-permute-start | bytes 776 | tf_op jit(solution)/shard_map/ppermute | solution.py:16
  17.0 0.6 copy-start.3
  17.7 0.6 copy-start.5
  19.6 5.2 %collective-permute-start.4 = (s32[128]{0:T(128)}, s32[128]{0:T(128)S(1)}, u32[]{:S(2)}, u32[]{:S(2)}) collective-permute-start(s32[128]{0:T(128)} %pad_add_fusion.3), channel_id=1, source_target_pairs={{0,4},{1,5},{2,6},{3,7},{4,0},{5,1},{6,2},{7,3},{8,12},{9,13},{10,... | collective-permute-start | bytes 1544 | tf_op jit(solution)/shard_map/ppermute | solution.py:16
  22.2 0.7 copy-start.8
  22.9 0.7 copy-start.9
  25.5 1.0 copy-start.7
  27.2 5.9 %collective-permute-start.7 = (bf16[4,32,256]{2,1,0:T(8,128)(2,1)S(1)}, bf16[4,32,256]{2,1,0:T(8,128)(2,1)S(1)}, u32[]{:S(2)}, u32[]{:S(2)}) collective-permute-start(bf16[4,32,256]{2,1,0:T(8,128)(2,1)S(1)} %slice.25), channel_id=1, source_target_pairs={{0,4},{1,5},{2,6},{3,7},{4,0},{5,1},{6,2},{7,3},{8,12},{9,13},{10,... | collective-permute-start | bytes 196616 | tf_op jit(solution)/shard_map/ppermute | solution.py:16
  29.1 0.8 copy-start.4
  29.9 0.8 copy-start.6
  33.2 5.8 %collective-permute-start.8 = (bf16[2,32,256]{2,1,0:T(8,128)(2,1)S(1)}, bf16[2,32,256]{2,1,0:T(8,128)(2,1)S(1)}, u32[]{:S(2)}, u32[]{:S(2)}) collective-permute-start(bf16[2,32,256]{2,1,0:T(8,128)(2,1)S(1)} %slice.27), channel_id=1, source_target_pairs={{0,2},{1,3},{2,0},{3,1},{4,6},{5,7},{6,4},{7,5},{8,10},{9,11},{10,... | collective-permute-start | bytes 98312 | tf_op jit(solution)/shard_map/ppermute | solution.py:16
  33.5 3.8 %collective-permute-start.10 = (f32[32,128]{1,0:T(8,128)S(1)}, f32[32,128]{1,0:T(8,128)S(1)}, u32[]{:S(2)}, u32[]{:S(2)}) collective-permute-start(f32[32,128]{1,0:T(8,128)S(1)} %get-tuple-element.96.own), channel_id=1, source_target_pairs={{0,1},{1,0},{2,3},{3,2},{4,5},{5,4},{6,7},{7,6},{8,9},{9,8},{10,11... | collective-permute-start | bytes 49160 | tf_op jit(solution)/shard_map/ppermute | solution.py:16
  37.3 3.9 %collective-permute-start.11 = (f32[64,128]{1,0:T(8,128)S(1)}, f32[64,128]{1,0:T(8,128)S(1)}, u32[]{:S(2)}, u32[]{:S(2)}) collective-permute-start(f32[64,128]{1,0:T(8,128)S(1)} %fold.6.own), channel_id=1, source_target_pairs={{0,2},{1,3},{2,0},{3,1},{4,6},{5,7},{6,4},{7,5},{8,10},{9,11},{10,... | collective-permute-start | bytes 98312 | tf_op jit(solution)/shard_map/ppermute | solution.py:16
  39.0 3.8 %collective-permute-start.9 = (bf16[1,32,256]{2,1,0:T(8,128)(2,1)S(1)}, bf16[1,32,256]{2,1,0:T(8,128)(2,1)S(1)}, u32[]{:S(2)}, u32[]{:S(2)}) collective-permute-start(bf16[1,32,256]{2,1,0:T(8,128)(2,1)S(1)} %slice.29), channel_id=1, source_target_pairs={{0,1},{1,0},{2,3},{3,2},{4,5},{5,4},{6,7},{7,6},{8,9},{9,8},{10,11... | collective-permute-start | bytes 49160 | tf_op jit(solution)/shard_map/ppermute | solution.py:16
  39.4 13.0 %copy-start.1 = (bf16[1,1,1024,1024]{3,2,1,0:T(8,128)(2,1)S(1)}, bf16[1,1,1024,1024]{3,2,1,0:T(8,128)(2,1)}, u32[]{:S(2)}) copy-start(bf16[1,1,1024,1024]{3,2,1,0:T(8,128)(2,1)} %param.8) | copy-start | bytes 6291460
  41.2 5.2 %collective-permute-start.12 = (f32[128,128]{1,0:T(8,128)S(1)}, f32[128,128]{1,0:T(8,128)S(1)}, u32[]{:S(2)}, u32[]{:S(2)}) collective-permute-start(f32[128,128]{1,0:T(8,128)S(1)} %fold.7.own), channel_id=1, source_target_pairs={{0,4},{1,5},{2,6},{3,7},{4,0},{5,1},{6,2},{7,3},{8,12},{9,13},{10,... | collective-permute-start | bytes 196616 | tf_op jit(solution)/shard_map/ppermute | solution.py:16
  47.4 5.0 %collective-permute-start.13 = (f32[256,128]{1,0:T(8,128)S(1)}, f32[256,128]{1,0:T(8,128)S(1)}, u32[]{:S(2)}, u32[]{:S(2)}) collective-permute-start(f32[256,128]{1,0:T(8,128)S(1)} %get-tuple-element.97.refs_0_), channel_id=1, source_target_pairs={{0,1},{2,3},{4,5},{6,7},{1,0},{3,2},{5,4},{7,6},{8,9},{10,11},{12,... | collective-permute-start | bytes 393224 | tf_op jit(solution)/shard_map/ppermute | solution.py:375
  48.2 4.2 %collective-permute-start.14 = (f32[256,128]{1,0:T(8,128)S(1)}, f32[256,128]{1,0:T(8,128)S(1)}, u32[]{:S(2)}, u32[]{:S(2)}) collective-permute-start(f32[256,128]{1,0:T(8,128)S(1)} %get-tuple-element.98.refs_1_), channel_id=1, source_target_pairs={{1,2},{3,4},{5,6},{2,1},{4,3},{6,5},{9,10},{11,12},{13,14},{10,9},... | collective-permute-start | bytes 393224 | tf_op jit(solution)/shard_map/ppermute | solution.py:375
  48.8 3.6 %collective-permute-start.15 = (f32[256,128]{1,0:T(8,128)S(1)}, f32[256,128]{1,0:T(8,128)S(1)}, u32[]{:S(2)}, u32[]{:S(2)}) collective-permute-start(f32[256,128]{1,0:T(8,128)S(1)} %get-tuple-element.99.refs_2_), channel_id=1, source_target_pairs={{0,8},{16,24},{8,0},{24,16},{1,9},{17,25},{9,1},{25,17},{2,10},{18... | collective-permute-start | bytes 393224 | tf_op jit(solution)/shard_map/ppermute | solution.py:375
  48.9 3.5 %collective-permute-start.16 = (f32[256,128]{1,0:T(8,128)S(1)}, f32[256,128]{1,0:T(8,128)S(1)}, u32[]{:S(2)}, u32[]{:S(2)}) collective-permute-start(f32[256,128]{1,0:T(8,128)S(1)} %get-tuple-element.100.refs_3_), channel_id=1, source_target_pairs={{8,16},{16,8},{9,17},{17,9},{10,18},{18,10},{11,19},{19,11},{12,20... | collective-permute-start | bytes 393224 | tf_op jit(solution)/shard_map/ppermute | solution.py:375
  54.0 8.5 %collective-permute-start.17 = (f32[256,128]{1,0:T(8,128)S(1)}, f32[256,128]{1,0:T(8,128)S(1)}, u32[]{:S(2)}, u32[]{:S(2)}) collective-permute-start(f32[256,128]{1,0:T(8,128)S(1)} %get-tuple-element.102.refs_0_), channel_id=1, source_target_pairs={{0,1},{2,3},{4,5},{6,7},{1,0},{3,2},{5,4},{7,6},{8,9},{10,11},{12,... | collective-permute-start | bytes 393224 | tf_op jit(solution)/shard_map/ppermute | solution.py:375
  58.9 3.6 %collective-permute-start.18 = (f32[256,128]{1,0:T(8,128)S(1)}, f32[256,128]{1,0:T(8,128)S(1)}, u32[]{:S(2)}, u32[]{:S(2)}) collective-permute-start(f32[256,128]{1,0:T(8,128)S(1)} %get-tuple-element.103.refs_1_), channel_id=1, source_target_pairs={{1,2},{3,4},{5,6},{2,1},{4,3},{6,5},{9,10},{11,12},{13,14},{10,9},... | collective-permute-start | bytes 393224 | tf_op jit(solution)/shard_map/ppermute | solution.py:375
  59.5 3.2 %collective-permute-start.19 = (f32[256,128]{1,0:T(8,128)S(1)}, f32[256,128]{1,0:T(8,128)S(1)}, u32[]{:S(2)}, u32[]{:S(2)}) collective-permute-start(f32[256,128]{1,0:T(8,128)S(1)} %get-tuple-element.104.refs_2_), channel_id=1, source_target_pairs={{0,8},{16,24},{8,0},{24,16},{1,9},{17,25},{9,1},{25,17},{2,10},{18... | collective-permute-start | bytes 393224 | tf_op jit(solution)/shard_map/ppermute | solution.py:375
  61.8 1.0 collective-permute-start.20
  64.3 7.4 %collective-permute-start.21 = (f32[176,128]{1,0:T(8,128)S(1)}, f32[176,128]{1,0:T(8,128)S(1)}, u32[]{:S(2)}, u32[]{:S(2)}) collective-permute-start(f32[176,128]{1,0:T(8,128)S(1)} %get-tuple-element.107.own), channel_id=1, source_target_pairs={{0,1},{1,0},{2,3},{3,2},{4,5},{5,4},{6,7},{7,6},{8,9},{9,8},{10,11... | collective-permute-start | bytes 270344 | tf_op jit(solution)/shard_map/ppermute | solution.py:16
  71.8 7.9 %collective-permute-start.22 = (f32[208,128]{1,0:T(8,128)S(1)}, f32[208,128]{1,0:T(8,128)S(1)}, u32[]{:S(2)}, u32[]{:S(2)}) collective-permute-start(f32[208,128]{1,0:T(8,128)S(1)} %fold.8.own), channel_id=1, source_target_pairs={{0,2},{1,3},{2,0},{3,1},{4,6},{5,7},{6,4},{7,5},{8,10},{9,11},{10,... | collective-permute-start | bytes 319496 | tf_op jit(solution)/shard_map/ppermute | solution.py:16
  79.7 9.6 %collective-permute-start.23 = (f32[272,128]{1,0:T(8,128)S(1)}, f32[272,128]{1,0:T(8,128)S(1)}, u32[]{:S(2)}, u32[]{:S(2)}) collective-permute-start(f32[272,128]{1,0:T(8,128)S(1)} %fold.9.own), channel_id=1, source_target_pairs={{0,4},{1,5},{2,6},{3,7},{4,0},{5,1},{6,2},{7,3},{8,12},{9,13},{10,... | collective-permute-start | bytes 417800 | tf_op jit(solution)/shard_map/ppermute | solution.py:16
  90.3 6.0 %collective-permute-start.26 = (f32[400,128]{1,0:T(8,128)S(1)}, f32[400,128]{1,0:T(8,128)S(1)}, u32[]{:S(2)}, u32[]{:S(2)}) collective-permute-start(f32[400,128]{1,0:T(8,128)S(1)} %get-tuple-element.110.refs_2_), channel_id=1, source_target_pairs={{0,8},{16,24},{8,0},{24,16},{1,9},{17,25},{9,1},{25,17},{2,10},{18... | collective-permute-start | bytes 614408 | tf_op jit(solution)/shard_map/ppermute | solution.py:375
  90.4 5.9 %collective-permute-start.24 = (f32[256,128]{1,0:T(8,128)S(1)}, f32[256,128]{1,0:T(8,128)S(1)}, u32[]{:S(2)}, u32[]{:S(2)}) collective-permute-start(f32[256,128]{1,0:T(8,128)S(1)} %get-tuple-element.108.refs_0_), channel_id=1, source_target_pairs={{0,1},{2,3},{4,5},{6,7},{1,0},{3,2},{5,4},{7,6},{8,9},{10,11},{12,... | collective-permute-start | bytes 393224 | tf_op jit(solution)/shard_map/ppermute | solution.py:375
  90.5 5.8 %collective-permute-start.25 = (f32[256,128]{1,0:T(8,128)S(1)}, f32[256,128]{1,0:T(8,128)S(1)}, u32[]{:S(2)}, u32[]{:S(2)}) collective-permute-start(f32[256,128]{1,0:T(8,128)S(1)} %get-tuple-element.109.refs_1_), channel_id=1, source_target_pairs={{1,2},{3,4},{5,6},{2,1},{4,3},{6,5},{9,10},{11,12},{13,14},{10,9},... | collective-permute-start | bytes 393224 | tf_op jit(solution)/shard_map/ppermute | solution.py:375
  91.2 5.2 %collective-permute-start.27 = (f32[256,128]{1,0:T(8,128)S(1)}, f32[256,128]{1,0:T(8,128)S(1)}, u32[]{:S(2)}, u32[]{:S(2)}) collective-permute-start(f32[256,128]{1,0:T(8,128)S(1)} %get-tuple-element.111.refs_3_), channel_id=1, source_target_pairs={{8,16},{16,8},{9,17},{17,9},{10,18},{18,10},{11,19},{19,11},{12,20... | collective-permute-start | bytes 393224 | tf_op jit(solution)/shard_map/ppermute | solution.py:375
  97.9 13.9 %collective-permute-start.29 = (f32[256,128]{1,0:T(8,128)S(1)}, f32[256,128]{1,0:T(8,128)S(1)}, u32[]{:S(2)}, u32[]{:S(2)}) collective-permute-start(f32[256,128]{1,0:T(8,128)S(1)} %get-tuple-element.114.refs_0_), channel_id=1, source_target_pairs={{0,1},{2,3},{4,5},{6,7},{1,0},{3,2},{5,4},{7,6},{8,9},{10,11},{12,... | collective-permute-start | bytes 393224 | tf_op jit(solution)/shard_map/ppermute | solution.py:375
  102.5 9.3 %collective-permute-start.30 = (f32[256,128]{1,0:T(8,128)S(1)}, f32[256,128]{1,0:T(8,128)S(1)}, u32[]{:S(2)}, u32[]{:S(2)}) collective-permute-start(f32[256,128]{1,0:T(8,128)S(1)} %get-tuple-element.115.refs_1_), channel_id=1, source_target_pairs={{1,2},{3,4},{5,6},{2,1},{4,3},{6,5},{9,10},{11,12},{13,14},{10,9},... | collective-permute-start | bytes 393224 | tf_op jit(solution)/shard_map/ppermute | solution.py:375
  103.2 8.6 %collective-permute-start.31 = (f32[256,128]{1,0:T(8,128)S(1)}, f32[256,128]{1,0:T(8,128)S(1)}, u32[]{:S(2)}, u32[]{:S(2)}) collective-permute-start(f32[256,128]{1,0:T(8,128)S(1)} %get-tuple-element.116.refs_2_), channel_id=1, source_target_pairs={{0,8},{16,24},{8,0},{24,16},{1,9},{17,25},{9,1},{25,17},{2,10},{18... | collective-permute-start | bytes 393224 | tf_op jit(solution)/shard_map/ppermute | solution.py:375
  103.2 8.6 %collective-permute-start.32 = (f32[256,128]{1,0:T(8,128)S(1)}, f32[256,128]{1,0:T(8,128)S(1)}, u32[]{:S(2)}, u32[]{:S(2)}) collective-permute-start(f32[256,128]{1,0:T(8,128)S(1)} %get-tuple-element.117.refs_3_), channel_id=1, source_target_pairs={{8,16},{16,8},{9,17},{17,9},{10,18},{18,10},{11,19},{19,11},{12,20... | collective-permute-start | bytes 393224 | tf_op jit(solution)/shard_map/ppermute | solution.py:375
  104.1 7.7 %collective-permute-start.28 = (f32[144,128]{1,0:T(8,128)S(1)}, f32[144,128]{1,0:T(8,128)S(1)}, u32[]{:S(2)}, u32[]{:S(2)}) collective-permute-start(f32[144,128]{1,0:T(8,128)S(1)} %get-tuple-element.112), channel_id=1, source_target_pairs={{0,16},{8,24},{16,0},{24,8},{1,17},{9,25},{17,1},{25,9},{2,18},{10... | collective-permute-start | bytes 221192 | tf_op jit(solution)/shard_map/ppermute | solution.py:16
  118.5 5.7 %collective-permute-start.33 = (f32[176,128]{1,0:T(8,128)S(1)}, f32[176,128]{1,0:T(8,128)S(1)}, u32[]{:S(2)}, u32[]{:S(2)}) collective-permute-start(f32[176,128]{1,0:T(8,128)S(1)} %get-tuple-element.119.own), channel_id=1, source_target_pairs={{0,1},{1,0},{2,3},{3,2},{4,5},{5,4},{6,7},{7,6},{8,9},{9,8},{10,11... | collective-permute-start | bytes 270344 | tf_op jit(solution)/shard_map/ppermute | solution.py:16
  124.2 4.8 %collective-permute-start.34 = (f32[208,128]{1,0:T(8,128)S(1)}, f32[208,128]{1,0:T(8,128)S(1)}, u32[]{:S(2)}, u32[]{:S(2)}) collective-permute-start(f32[208,128]{1,0:T(8,128)S(1)} %fold.10.own), channel_id=1, source_target_pairs={{0,2},{1,3},{2,0},{3,1},{4,6},{5,7},{6,4},{7,5},{8,10},{9,11},{10,... | collective-permute-start | bytes 319496 | tf_op jit(solution)/shard_map/ppermute | solution.py:16
  129.0 8.6 %collective-permute-start.35 = (f32[272,128]{1,0:T(8,128)S(1)}, f32[272,128]{1,0:T(8,128)S(1)}, u32[]{:S(2)}, u32[]{:S(2)}) collective-permute-start(f32[272,128]{1,0:T(8,128)S(1)} %fold.11.own), channel_id=1, source_target_pairs={{0,4},{1,5},{2,6},{3,7},{4,0},{5,1},{6,2},{7,3},{8,12},{9,13},{10,... | collective-permute-start | bytes 417800 | tf_op jit(solution)/shard_map/ppermute | solution.py:16
  138.6 6.0 %collective-permute-start.38 = (f32[400,128]{1,0:T(8,128)S(1)}, f32[400,128]{1,0:T(8,128)S(1)}, u32[]{:S(2)}, u32[]{:S(2)}) collective-permute-start(f32[400,128]{1,0:T(8,128)S(1)} %get-tuple-element.122.refs_2_), channel_id=1, source_target_pairs={{0,8},{16,24},{8,0},{24,16},{1,9},{17,25},{9,1},{25,17},{2,10},{18... | collective-permute-start | bytes 614408 | tf_op jit(solution)/shard_map/ppermute | solution.py:375
  138.7 5.9 %collective-permute-start.36 = (f32[256,128]{1,0:T(8,128)S(1)}, f32[256,128]{1,0:T(8,128)S(1)}, u32[]{:S(2)}, u32[]{:S(2)}) collective-permute-start(f32[256,128]{1,0:T(8,128)S(1)} %get-tuple-element.120.refs_0_), channel_id=1, source_target_pairs={{0,1},{2,3},{4,5},{6,7},{1,0},{3,2},{5,4},{7,6},{8,9},{10,11},{12,... | collective-permute-start | bytes 393224 | tf_op jit(solution)/shard_map/ppermute | solution.py:375
  139.7 4.9 %collective-permute-start.37 = (f32[256,128]{1,0:T(8,128)S(1)}, f32[256,128]{1,0:T(8,128)S(1)}, u32[]{:S(2)}, u32[]{:S(2)}) collective-permute-start(f32[256,128]{1,0:T(8,128)S(1)} %get-tuple-element.121.refs_1_), channel_id=1, source_target_pairs={{1,2},{3,4},{5,6},{2,1},{4,3},{6,5},{9,10},{11,12},{13,14},{10,9},... | collective-permute-start | bytes 393224 | tf_op jit(solution)/shard_map/ppermute | solution.py:375
  140.4 4.2 %collective-permute-start.39 = (f32[256,128]{1,0:T(8,128)S(1)}, f32[256,128]{1,0:T(8,128)S(1)}, u32[]{:S(2)}, u32[]{:S(2)}) collective-permute-start(f32[256,128]{1,0:T(8,128)S(1)} %get-tuple-element.123.refs_3_), channel_id=1, source_target_pairs={{8,16},{16,8},{9,17},{17,9},{10,18},{18,10},{11,19},{19,11},{12,20... | collective-permute-start | bytes 393224 | tf_op jit(solution)/shard_map/ppermute | solution.py:375
  146.2 13.9 %collective-permute-start.41 = (f32[256,128]{1,0:T(8,128)S(1)}, f32[256,128]{1,0:T(8,128)S(1)}, u32[]{:S(2)}, u32[]{:S(2)}) collective-permute-start(f32[256,128]{1,0:T(8,128)S(1)} %get-tuple-element.133.refs_0_), channel_id=1, source_target_pairs={{0,1},{2,3},{4,5},{6,7},{1,0},{3,2},{5,4},{7,6},{8,9},{10,11},{12,... | collective-permute-start | bytes 393224 | tf_op jit(solution)/shard_map/ppermute | solution.py:375
  150.8 9.3 %collective-permute-start.42 = (f32[256,128]{1,0:T(8,128)S(1)}, f32[256,128]{1,0:T(8,128)S(1)}, u32[]{:S(2)}, u32[]{:S(2)}) collective-permute-start(f32[256,128]{1,0:T(8,128)S(1)} %get-tuple-element.134.refs_1_), channel_id=1, source_target_pairs={{1,2},{3,4},{5,6},{2,1},{4,3},{6,5},{9,10},{11,12},{13,14},{10,9},... | collective-permute-start | bytes 393224 | tf_op jit(solution)/shard_map/ppermute | solution.py:375
  151.4 8.6 %collective-permute-start.43 = (f32[256,128]{1,0:T(8,128)S(1)}, f32[256,128]{1,0:T(8,128)S(1)}, u32[]{:S(2)}, u32[]{:S(2)}) collective-permute-start(f32[256,128]{1,0:T(8,128)S(1)} %get-tuple-element.135.refs_2_), channel_id=1, source_target_pairs={{0,8},{16,24},{8,0},{24,16},{1,9},{17,25},{9,1},{25,17},{2,10},{18... | collective-permute-start | bytes 393224 | tf_op jit(solution)/shard_map/ppermute | solution.py:375
  151.5 8.6 %collective-permute-start.44 = (f32[256,128]{1,0:T(8,128)S(1)}, f32[256,128]{1,0:T(8,128)S(1)}, u32[]{:S(2)}, u32[]{:S(2)}) collective-permute-start(f32[256,128]{1,0:T(8,128)S(1)} %get-tuple-element.136.refs_3_), channel_id=1, source_target_pairs={{8,16},{16,8},{9,17},{17,9},{10,18},{18,10},{11,19},{19,11},{12,20... | collective-permute-start | bytes 393224 | tf_op jit(solution)/shard_map/ppermute | solution.py:375
  152.4 7.6 %collective-permute-start.40 = (f32[144,128]{1,0:T(8,128)S(1)}, f32[144,128]{1,0:T(8,128)S(1)}, u32[]{:S(2)}, u32[]{:S(2)}) collective-permute-start(f32[144,128]{1,0:T(8,128)S(1)} %get-tuple-element.124), channel_id=1, source_target_pairs={{0,16},{8,24},{16,0},{24,8},{1,17},{9,25},{17,1},{25,9},{2,18},{10... | collective-permute-start | bytes 221192 | tf_op jit(solution)/shard_map/ppermute | solution.py:16
  166.8 1.3 collective-permute-start.45
  168.0 5.1 %collective-permute-start.46 = (f32[72,128]{1,0:T(8,128)S(1)}, f32[72,128]{1,0:T(8,128)S(1)}, u32[]{:S(2)}, u32[]{:S(2)}) collective-permute-start(f32[72,128]{1,0:T(8,128)S(1)} %add.72), channel_id=1, source_target_pairs={{0,1},{1,0},{2,3},{3,2},{4,5},{5,4},{6,7},{7,6},{8,9},{9,8},{10,11... | collective-permute-start | bytes 110600 | tf_op jit(solution)/shard_map/ppermute | solution.py:16
  173.1 4.0 %collective-permute-start.47 = (f32[72,128]{1,0:T(8,128)S(1)}, f32[72,128]{1,0:T(8,128)S(1)}, u32[]{:S(2)}, u32[]{:S(2)}) collective-permute-start(f32[72,128]{1,0:T(8,128)S(1)} %add.73), channel_id=1, source_target_pairs={{0,16},{8,24},{16,0},{24,8},{1,17},{9,25},{17,1},{25,9},{2,18},{10... | collective-permute-start | bytes 110600 | tf_op jit(solution)/shard_map/ppermute | solution.py:16
  177.1 8.6 %collective-permute-start.50 = (f32[72,128]{1,0:T(8,128)S(1)}, f32[72,128]{1,0:T(8,128)S(1)}, u32[]{:S(2)}, u32[]{:S(2)}) collective-permute-start(f32[72,128]{1,0:T(8,128)S(1)} %add.74), channel_id=1, source_target_pairs={{0,6},{1,7},{2,4},{3,5},{4,2},{5,3},{6,0},{7,1},{8,14},{9,15},{10,... | collective-permute-start | bytes 110600 | tf_op jit(solution)/shard_map/ppermute | solution.py:16
  179.9 5.8 %collective-permute-start.49 = (f32[72,128]{1,0:T(8,128)S(1)}, f32[72,128]{1,0:T(8,128)S(1)}, u32[]{:S(2)}, u32[]{:S(2)}) collective-permute-start(f32[72,128]{1,0:T(8,128)S(1)} %add.74), channel_id=1, source_target_pairs={{0,4},{1,5},{2,6},{3,7},{4,0},{5,1},{6,2},{7,3},{8,12},{9,13},{10,... | collective-permute-start | bytes 110600 | tf_op jit(solution)/shard_map/ppermute | solution.py:16
  180.4 5.4 %collective-permute-start.48 = (f32[72,128]{1,0:T(8,128)S(1)}, f32[72,128]{1,0:T(8,128)S(1)}, u32[]{:S(2)}, u32[]{:S(2)}) collective-permute-start(f32[72,128]{1,0:T(8,128)S(1)} %add.74), channel_id=1, source_target_pairs={{0,2},{1,3},{2,0},{3,1},{4,6},{5,7},{6,4},{7,5},{8,10},{9,11},{10,... | collective-permute-start | bytes 110600 | tf_op jit(solution)/shard_map/ppermute | solution.py:16
  185.8 1.3 collective-permute-start.51
